TPU v7x, 256 devices: a whole 4x4x8 slice. The times are simulated.
256 devices in a mesh: dp: 8 (over y, core), expert: 8 (over x, z_hi), mp: 4 (over z_lo).
Axes of the slice: x: 4, y: 4, z: 8 (z_hi: 2, z_lo: 4; z = z_hi * 4 + z_lo), core: 2. Of those that a mesh axis runs over, the one named last changes fastest.
Arguments:
- tokens: bfloat16 [1024, 4096], P('dp', ('expert', 'mp')), may hold values from -6 to 6
- cotangent: bfloat16 [1024, 4096], P('dp', ('expert', 'mp')), may hold values from -6 to 6
- gates: float32 [1024, 2], P('dp'), may hold values from 0.2 to 1
- expert_ids: int32 [1024, 2], P('dp'), may hold values from 0 to 7, all different within a row; in each aligned block of 128 rows (0 to 127, 128 to 255, ...) at most 48 rows name the same one
- dense_ffn: bfloat16 [3, 4096, 8192], P(None, 'expert', ('dp', 'mp')), may hold values from -0.09375 to 0.09375
- redrawn: int32 [8, 8192], P(None, ('dp', 'mp')), may hold values from 0 to 1, as said below
- redraw: bfloat16 [8, 3, 4096, 4096], P('expert', None, None, ('dp', 'mp')), may hold values from -0.09375 to 0.09375
Outputs:
- mixed: bfloat16 [1024, 4096], P('dp', ('expert', 'mp'))
- token_grad: bfloat16 [1024, 4096], P('dp', ('expert', 'mp'))
- new_weights: bfloat16 [8, 3, 4096, 8192], P('expert', None, None, ('dp', 'mp'))
Inputs may be any that keep to these rules, and one draw needn't show every extreme that they name: `expert_ids`: the two experts of a token differ; in every aligned block of 128 tokens each expert is named by at most 48 tokens, and in some block one expert by exactly 48. `redrawn`: in every expert, exactly half of every aligned block of 256 hidden units is 1.
All inputs are finite; a program needn't handle non-finite values.
Results may differ from a plain program's by a relative error of at most 0.023.
Values may be sent and summed in bfloat16 or wider, within the bound.
No kernel may reach another device: no remote copies, remote signals or barrier semaphores. Data moves between devices by JAX's collectives and lax.ppermute only.
A program may use at most 128 MiB of HBM per device.

v0:
```python
import jax
import jax.numpy as jnp
from jax import lax
from jax.sharding import PartitionSpec as P


def slot_table(expert_ids, experts, capacity):
    tok_rows, picks = expert_ids.shape
    flat_ids = expert_ids.reshape(-1)
    onehot = (flat_ids[:, None] == jnp.arange(experts, dtype=jnp.int32)[None, :]).astype(jnp.int32)
    before = jnp.cumsum(onehot, axis=0) - onehot
    slot_num = jnp.sum(before * onehot, axis=1)
    target = flat_ids * capacity + slot_num
    table = (target[:, None] == jnp.arange(experts * capacity, dtype=jnp.int32)[None, :]).astype(
        jnp.float32
    )
    return table.reshape(tok_rows, picks, experts * capacity)


def front_pass(rows_in, rows_cot, w_pair, w_down):
    pair = jnp.einsum("rd,pdc->prc", rows_in, w_pair, preferred_element_type=jnp.float32)
    gate_act = pair[0]
    up_act = pair[1]
    sig = jax.nn.sigmoid(gate_act)
    act = gate_act * sig
    hidden = (act * up_act).astype(jnp.bfloat16)
    hidden_grad = jnp.dot(rows_cot, w_down, preferred_element_type=jnp.float32)
    gate_grad = (hidden_grad * up_act * sig * (1.0 + gate_act * (1.0 - sig))).astype(jnp.bfloat16)
    up_grad = (hidden_grad * act).astype(jnp.bfloat16)
    return (hidden, jnp.stack([gate_grad, up_grad]))


def weight_terms(rows_in, rows_cot, hidden, both):
    pair_grad = jnp.einsum("rd,prc->pdc", rows_in, both, preferred_element_type=jnp.float32)
    down_grad = jnp.einsum("rd,rc->dc", rows_cot, hidden, preferred_element_type=jnp.float32)
    return jnp.concatenate([pair_grad, down_grad[None]], axis=0)


def on_device(tokens, cotangent, gates, expert_ids, dense_ffn, redrawn, redraw):
    experts = redrawn.shape[0]
    tok_rows, picks = expert_ids.shape
    capacity = max(3 * tok_rows // 8, picks * tok_rows // experts)
    quarters = lax.axis_size("mp")
    width = tokens.shape[1]
    own = lax.dynamic_index_in_dim(redrawn, lax.axis_index("expert"), 0, keepdims=False)
    half = own.shape[0] // 2
    fresh_rank = jnp.clip(jnp.cumsum(own) - 1, 0, half - 1)
    fresh = redraw[0]
    whole = lax.all_gather(dense_ffn, "expert", axis=1, tiled=True)
    weights = jnp.where(own[None, None, :] == 1, jnp.take(fresh, fresh_rank, axis=2), whole)
    table = slot_table(expert_ids, experts, capacity)
    pick_rows = jnp.sum(table, axis=1)
    in_slots = lax.dot_general(
        pick_rows.astype(jnp.bfloat16),
        tokens,
        (((0,), (0,)), ((), ())),
        preferred_element_type=jnp.float32,
    ).astype(jnp.bfloat16)
    scaled = (gates[:, :, None] * cotangent.astype(jnp.float32)[:, None, :]).astype(jnp.bfloat16)
    cot_slots = jnp.einsum(
        "tcr,tcd->rd", table.astype(jnp.bfloat16), scaled, preferred_element_type=jnp.float32
    ).astype(jnp.bfloat16)
    shaped = (experts * quarters, capacity // quarters, width)
    arrived = (
        lax.all_to_all(
            in_slots.reshape(shaped), ("expert", "mp"), split_axis=0, concat_axis=2, tiled=True
        ),
        lax.all_to_all(
            cot_slots.reshape(shaped), ("expert", "mp"), split_axis=0, concat_axis=2, tiled=True
        ),
    )
    w_pair = weights[:2]
    w_down = weights[2]
    rows_in = lax.all_gather(arrived[0], ("dp", "mp"), axis=1, tiled=True)[0]
    rows_cot = lax.all_gather(arrived[1], ("dp", "mp"), axis=1, tiled=True)[0]
    hidden, both = front_pass(rows_in, rows_cot, w_pair, w_down)
    out_rows = lax.dot_general(
        hidden, w_down, (((1,), (1,)), ((), ())), preferred_element_type=jnp.float32
    )
    grad_rows = jnp.einsum("prc,pdc->rd", both, w_pair, preferred_element_type=jnp.float32)
    grads = weight_terms(rows_in, rows_cot, hidden, both)
    outs = out_rows
    in_grads = grad_rows
    grads, outs, in_grads = (grads, outs, in_grads)
    summed = (
        lax.psum_scatter(
            outs.astype(jnp.bfloat16), ("dp", "mp"), scatter_dimension=0, tiled=True
        ).astype(jnp.float32),
        lax.psum_scatter(
            in_grads.astype(jnp.bfloat16), ("dp", "mp"), scatter_dimension=0, tiled=True
        ).astype(jnp.float32),
    )
    back = (
        lax.all_to_all(
            summed[0][None].astype(jnp.bfloat16),
            ("expert", "mp"),
            split_axis=2,
            concat_axis=0,
            tiled=True,
        ).astype(jnp.float32),
        lax.all_to_all(
            summed[1][None].astype(jnp.bfloat16),
            ("expert", "mp"),
            split_axis=2,
            concat_axis=0,
            tiled=True,
        ).astype(jnp.float32),
    )
    out_flat = back[0].reshape(experts * capacity, width)
    grad_flat = back[1].reshape(experts * capacity, width)
    weighted = jnp.sum(table * gates[:, :, None], axis=1)
    mixed = jnp.dot(weighted, out_flat, precision=lax.Precision.HIGHEST).astype(jnp.bfloat16)
    token_grad = jnp.dot(pick_rows, grad_flat, precision=lax.Precision.HIGHEST).astype(jnp.bfloat16)
    update = grads / (jnp.abs(grads) + 0.1)
    new_weights = (weights.astype(jnp.float32) * (1.0 - 0.0003) - 0.003 * update).astype(
        jnp.bfloat16
    )
    return (mixed, token_grad, new_weights[None])


def solution(mesh):
    return jax.shard_map(
        on_device,
        mesh=mesh,
        in_specs=(
            P("dp", ("expert", "mp")),
            P("dp", ("expert", "mp")),
            P("dp", None),
            P("dp", None),
            P(None, "expert", ("dp", "mp")),
            P(None, ("dp", "mp")),
            P("expert", None, None, ("dp", "mp")),
        ),
        out_specs=(
            P("dp", ("expert", "mp")),
            P("dp", ("expert", "mp")),
            P("expert", None, None, ("dp", "mp")),
        ),
        check_vma=False,
    )
```

profile of v0, /device:TPU:32, one launch (start us, length us, event | category | flops | bytes accessed | tf_op | source)
XLA Modules:
  0.0 756.3 jit_solution(2562464543629073388)
XLA Ops:
  7.2 2.5 copy.85
  9.8 0.8 copy.80
  12.0 0.7 multiply_add_fusion
  12.7 1.5 convert_reduce_fusion
  14.2 0.7 copy-done.3
  15.0 23.2 %all_to_all.68 = bf16[32,12,128]{2,1,0:T(8,128)(2,1)S(1)} all-to-all(bf16[32,12,128]{2,1,0:T(8,128)(2,1)S(1)} %reshape.140), channel_id=1, replica_groups=mesh['dp'=8,'expert'=8,'mp'=4] {'expert','mp'}, dimensions={0} | all-to-all | bytes 196608 | tf_op jit(solution)/shard_map/all_to_all | solution.py:65
  38.3 0.7 all_to_all.62
  39.0 0.8 convert_element_type.83
  39.8 1.0 fusion.17
  40.8 26.0 %all_to_all.69 = bf16[32,12,128]{2,1,0:T(8,128)(2,1)S(1)} all-to-all(bf16[32,12,128]{2,1,0:T(8,128)(2,1)S(1)} %reshape.142), channel_id=1, replica_groups=mesh['dp'=8,'expert'=8,'mp'=4] {'expert','mp'}, dimensions={0} | all-to-all | bytes 196608 | tf_op jit(solution)/shard_map/all_to_all | solution.py:68
  66.8 0.7 all_to_all.63
  67.6 5.3 copy.83
  72.9 0.7 compare_reduce_fusion
  74.2 15.2 %gather_fusion = bf16[256,3,4096]{2,1,0:T(4,128)(2,1)} fusion(bf16[3,4096,128]{1,0,2:T(4,128)(2,1)} %bitcast.145, s32[1024]{0:T(1024)S(1)} %pad_clamp_fusion), kind=kCustom, calls=%fused_computation | custom fusion | bytes 12583936 | tf_op jit(solution)/shard_map/jit(_take)/gather | solution.py:50
  89.4 72.3 %all-gather.4.cloned.1.call-done = bf16[3,4096,256]{1,2,0:T(8,128)(2,1)} async-done(((bf16[3,512,256]{1,2,0:T(8,128)(2,1)}), bf16[3,4096,256]{1,2,0:T(8,128)(2,1)}) %all-gather.4.cloned.1.call-update) | async-done | bytes 6291472 | tf_op jit(solution)/shard_map/all_gather | solution.py:49
  161.8 15.7 %bitcast_select_fusion = bf16[3,4096,256]{1,2,0:T(8,128)(2,1)} fusion(bf16[3,4096,256]{1,2,0:T(8,128)(2,1)} %all-gather.4.cloned.1.call-done, bf16[256,3,4096]{2,1,0:T(4,128)(2,1)} %gather_fusion, pred[256]{0:T(512)(128)(4,1)S(1)} %get-tuple-element.26, pred[256]{0:T(512)(128)(4,1)S(1)} %get-tuple-element.24), kind=kLoop, calls=%fused_computation.5 | loop fusion | flops 6291456 | bytes 18874880 | tf_op jit(solution)/shard_map/jit(_where)/select_n | solution.py:50
  177.5 74.9 %all-gather.6.cloned.1.call-done = bf16[1,384,4096]{2,0,1:T(2,128)(2,1)} async-done(((bf16[1,12,4096]{2,0,1:T(2,128)(2,1)}), bf16[1,384,4096]{2,0,1:T(2,128)(2,1)}) %all-gather.6.cloned.1.call-update) | async-done | bytes 3145744 | tf_op jit(solution)/shard_map/all_gather | solution.py:74
  252.4 8.6 %fusion.10 = f32[2,384,256]{1,2,0:T(8,128)S(1)} fusion(bf16[3,4096,256]{1,2,0:T(8,128)(2,1)} %bitcast_select_fusion, bf16[1,384,4096]{2,0,1:T(2,128)(2,1)} %all-gather.6.cloned.1.call-done), kind=kOutput, calls=%fused_computation.18 | convolution fusion | flops 1610612736 | bytes 10223616 | tf_op jit(solution)/shard_map/rd,pdc->prc/dot_general | solution.py:21
  261.1 0.9 copy-done.7
  262.1 2.6 convolution_convert_fusion
  264.7 83.3 %all-gather.8.cloned.1.call-done = bf16[1,384,4096]{2,0,1:T(2,128)(2,1)} async-done(((bf16[1,12,4096]{2,0,1:T(2,128)(2,1)}), bf16[1,384,4096]{2,0,1:T(2,128)(2,1)}) %all-gather.8.cloned.1.call-update) | async-done | bytes 3145744 | tf_op jit(solution)/shard_map/all_gather | solution.py:75
  347.9 7.3 fusion.31
  355.2 0.7 copy-done.8
  356.0 5.7 bitcast_convert_fusion
  361.6 181.8 %fusion.40 = (bf16[16,4096]{1,0:T(8,128)(2,1)S(1)}, bf16[16,4096]{1,0:T(8,128)(2,1)}) fusion(bf16[384,4096]{1,0:T(8,128)(2,1)S(1)} %convolution_convert_fusion, bf16[384,4096]{1,0:T(8,128)(2,1)} %bitcast_convert_fusion), kind=kCustom, calls=%all-reduce-scatter.2 | all-reduce-scatter fusion | flops 4194305 | bytes 6554624
  543.5 1.1 slice.41
  544.6 3.5 collective-permute-start.15
  548.0 4.5 collective-permute-start.14
  552.5 1.3 collective-permute-start.13
  553.8 5.2 collective-permute-start.12
  559.1 4.1 collective-permute-start.11
  563.2 1.3 collective-permute-start.7
  565.8 2.7 collective-permute-done.7
  568.4 4.5 collective-permute-start.10
  573.0 1.7 collective-permute-start.9
  574.7 3.6 collective-permute-start.8
  578.3 4.1 collective-permute-start.6
  582.4 3.6 collective-permute-start.5
  586.0 10.7 %convolution_bitcast_fusion = f32[2,4096,256]{1,2,0:T(8,128)} fusion(bf16[1,384,4096]{2,0,1:T(2,128)(2,1)} %all-gather.6.cloned.1.call-done, bf16[1,384,256]{1,2,0:T(8,128)(2,1)} %copy-done.9, bf16[1,384,256]{1,2,0:T(8,128)(2,1)} %copy-done.8), kind=kOutput, calls=%fused_computation.3 | convolution fusion | flops 1610809344 | bytes 11927552 | tf_op jit(solution)/shard_map/rd,prc->pdc/dot_general | solution.py:34
  596.7 3.3 collective-permute-start.4
  600.0 1.9 collective-permute-start.3
  602.0 2.2 collective-permute-start.2
  604.2 4.3 collective-permute-start.1
  608.5 2.2 collective-permute-start
  610.8 5.9 convolution_bitcast_fusion.1
  616.7 5.7 concatenate.5
  622.5 13.3 %concatenate.4 = bf16[140,4096]{1,0:T(8,128)(2,1)S(1)} concatenate(bf16[12,4096]{1,0:T(8,128)(2,1)S(1)} %collective-permute-done.7, bf16[16,4096]{1,0:T(8,128)(2,1)} %copy-done.10, bf16[16,4096]{1,0:T(8,128)(2,1)} %copy-done.12, bf16[16,4096]{1,0:T(8,128)(2,1)} %collective-permute-done.4, bf16[16,4096]{1,0:T(8,128)(2,1)} %collective-permute-done.3, ...), dimensions={0} | concatenate | bytes 2293760
  635.9 2.8 copy.88
  639.2 22.4 %reduce.6 = bf16[4096,12]{1,0:T(8,128)(2,1)S(1)} reduce(bf16[4096,1,12]{2,1,0:T(2,128)(2,1)S(1)} %bitcast.146, bf16[]{:T(256)} %broadcast.147), dimensions={1}, to_apply=%bitcast.130.reduce_sub_computation | reduce | bytes 196610
  661.6 2.7 reshape.161
  664.3 12.2 %all-to-all-start.1 = ((bf16[32,2,768]{2,1,0:T(2,128)(2,1)}), bf16[32,2,768]{2,1,0:T(2,128)(2,1)S(1)}, u32[]{:S(2)}, u32[]{:S(2)}) async-start(bf16[32,2,768]{2,1,0:T(2,128)(2,1)} %reshape.161), calls=%async_computation.1 | async-start | bytes 196608 | tf_op jit(solution)/shard_map/all_to_all | solution.py:94
  676.6 10.2 %fusion.2 = bf16[1,3,4096,256]{2,3,1,0:T(8,128)(2,1)} fusion(f32[1,4096,256]{1,2,0:T(8,128)} %convolution_bitcast_fusion.1, f32[2,4096,256]{1,2,0:T(8,128)} %convolution_bitcast_fusion, bf16[3,4096,256]{1,2,0:T(8,128)(2,1)} %bitcast_select_fusion), kind=kLoop, calls=%fused_computation.7 | loop fusion | flops 28311552 | bytes 25165824 | tf_op jit(solution)/shard_map/broadcast_in_dim | solution.py:118
  686.7 8.6 %copy.101 = bf16[1,3,4096,256]{3,2,1,0:T(8,128)(2,1)} copy(bf16[1,3,4096,256]{2,3,1,0:T(8,128)(2,1)} %fusion.2) | data formatting | bytes 12582912
  695.3 2.8 copy.97
  698.1 22.4 %reduce.7 = bf16[4096,12]{1,0:T(8,128)(2,1)S(1)} reduce(bf16[4096,1,12]{2,1,0:T(2,128)(2,1)S(1)} %bitcast.147, bf16[]{:T(256)} %broadcast.147), dimensions={1}, to_apply=%bitcast.132.reduce_sub_computation | reduce | bytes 196610
  720.5 2.7 reshape.163
  723.2 9.9 %all-to-all-start.3 = ((bf16[32,2,768]{2,1,0:T(2,128)(2,1)}), bf16[32,2,768]{2,1,0:T(2,128)(2,1)S(1)}, u32[]{:S(2)}, u32[]{:S(2)}) async-start(bf16[32,2,768]{2,1,0:T(2,128)(2,1)} %reshape.163), calls=%async_computation.3 | async-start | bytes 196608 | tf_op jit(solution)/shard_map/all_to_all | solution.py:101
  733.1 2.8 reshape.162
  735.9 2.1 copy.89
  738.2 4.4 all-to-all-done.3
  742.6 2.8 reshape.164
  745.3 2.1 copy.98
  747.6 1.0 convolution_convert_fusion.2
  748.6 1.0 convolution_convert_fusion.3
  (89 shorter events, 4.2 us)
Async XLA Ops:
  7.2 7.7 %copy-start = (bf16[128,128]{1,0:T(8,128)(2,1)S(1)}, bf16[128,128]{1,0:T(8,128)(2,1)}, u32[]{:S(2)}) copy-start(bf16[128,128]{1,0:T(8,128)(2,1)} %param.7) | copy-start | bytes 98308
  7.2 60.4 %copy-start.2 = (bf16[1,3,4096,128]{3,2,1,0:T(8,128)(2,1)S(1)}, bf16[1,3,4096,128]{3,2,1,0:T(8,128)(2,1)}, u32[]{:S(2)}) copy-start(bf16[1,3,4096,128]{3,2,1,0:T(8,128)(2,1)} %param.13) | copy-start | bytes 9437188
  7.2 154.6 %all-gather.4.cloned.1.call-start = ((), (), s32[]{:S(2)}) async-start(), calls=%async_computation.4 | async-start | bytes 7077888 | tf_op jit(solution)/shard_map/all_gather | solution.py:49
  9.7 242.7 %all-gather.6.cloned.1.call-start = ((), (), s32[]{:S(2)}) async-start(), calls=%async_computation.5 | async-start | bytes 6488064 | tf_op jit(solution)/shard_map/all_gather | solution.py:74
  14.2 0.7 copy-start.3
  39.0 309.0 %all-gather.8.cloned.1.call-start = ((), (), s32[]{:S(2)}) async-start(), calls=%async_computation.6 | async-start | bytes 6488064 | tf_op jit(solution)/shard_map/all_gather | solution.py:75
  261.0 0.9 copy-start.7
  355.2 0.7 copy-start.8
  355.2 0.7 copy-start.9
  356.0 208.5 %copy-start.14 = (u32[256]{0:T(256)S(1)}, u32[256]{0:T(256)}, u32[]{:S(2)}) copy-start(u32[256]{0:T(256)} %constant.57) | copy-start | bytes 3076
  543.5 67.3 %slice-start = ((s8[6291456]{0:T(1024)(128)(4,1)}), s8[2097152]{0:T(1024)(128)(4,1)S(1)}, s32[]{:S(2)}) async-start(s8[6291456]{0:T(1024)(128)(4,1)} %bitcast.150), calls=%async_computation.7 | async-start | bytes 4194304
  544.6 18.6 %collective-permute-start.15 = (bf16[12,4096]{1,0:T(8,128)(2,1)S(1)}, bf16[12,4096]{1,0:T(8,128)(2,1)S(1)}, u32[]{:S(2)}, u32[]{:S(2)}) collective-permute-start(bf16[12,4096]{1,0:T(8,128)(2,1)S(1)} %slice.41), channel_id=1, source_target_pairs={{0,64},{1,65},{2,66},{3,67},{32,96},{33,97},{34,98},{35,99},{64,12... | collective-permute-start | bytes 294920
  548.0 24.9 %collective-permute-start.14 = (bf16[16,4096]{1,0:T(8,128)(2,1)}, bf16[16,4096]{1,0:T(8,128)(2,1)S(1)}, u32[]{:S(2)}, u32[]{:S(2)}) collective-permute-start(bf16[16,4096]{1,0:T(8,128)(2,1)} %get-tuple-element.23), channel_id=1, source_target_pairs={{0,35},{1,64},{2,65},{3,66},{32,67},{33,96},{34,97},{35,98},{64,99... | collective-permute-start | bytes 393224
  552.5 22.1 %collective-permute-start.13 = (bf16[16,4096]{1,0:T(8,128)(2,1)}, bf16[16,4096]{1,0:T(8,128)(2,1)S(1)}, u32[]{:S(2)}, u32[]{:S(2)}) collective-permute-start(bf16[16,4096]{1,0:T(8,128)(2,1)} %get-tuple-element.23), channel_id=1, source_target_pairs={{0,34},{1,35},{2,64},{3,65},{32,66},{33,67},{34,96},{35,97},{64,98... | collective-permute-start | bytes 393224
  553.8 24.4 %collective-permute-start.12 = (bf16[16,4096]{1,0:T(8,128)(2,1)}, bf16[16,4096]{1,0:T(8,128)(2,1)S(1)}, u32[]{:S(2)}, u32[]{:S(2)}) collective-permute-start(bf16[16,4096]{1,0:T(8,128)(2,1)} %get-tuple-element.23), channel_id=1, source_target_pairs={{0,33},{1,34},{2,35},{3,64},{32,65},{33,66},{34,67},{35,96},{64,97... | collective-permute-start | bytes 393224
  559.1 23.3 %collective-permute-start.11 = (bf16[16,4096]{1,0:T(8,128)(2,1)}, bf16[16,4096]{1,0:T(8,128)(2,1)S(1)}, u32[]{:S(2)}, u32[]{:S(2)}) collective-permute-start(bf16[16,4096]{1,0:T(8,128)(2,1)} %get-tuple-element.23), channel_id=1, source_target_pairs={{0,32},{1,33},{2,34},{3,35},{32,64},{33,65},{34,66},{35,67},{64,96... | collective-permute-start | bytes 393224
  563.2 5.2 collective-permute-start.7
  565.8 45.0 %slice-start.1 = ((s8[6291456]{0:T(1024)(128)(4,1)}), s8[4194304]{0:T(1024)(128)(4,1)S(1)}, s32[]{:S(2)}) async-start(s8[6291456]{0:T(1024)(128)(4,1)} %bitcast.150), calls=%async_computation.8 | async-start | bytes 8388608
  568.4 28.3 %collective-permute-start.10 = (bf16[16,4096]{1,0:T(8,128)(2,1)}, bf16[16,4096]{1,0:T(8,128)(2,1)S(1)}, u32[]{:S(2)}, u32[]{:S(2)}) collective-permute-start(bf16[16,4096]{1,0:T(8,128)(2,1)} %get-tuple-element.23), channel_id=1, source_target_pairs={{0,3},{1,32},{2,33},{3,34},{32,35},{33,64},{34,65},{35,66},{64,67}... | collective-permute-start | bytes 393224
  573.0 27.1 %collective-permute-start.9 = (bf16[16,4096]{1,0:T(8,128)(2,1)}, bf16[16,4096]{1,0:T(8,128)(2,1)S(1)}, u32[]{:S(2)}, u32[]{:S(2)}) collective-permute-start(bf16[16,4096]{1,0:T(8,128)(2,1)} %get-tuple-element.23), channel_id=1, source_target_pairs={{0,2},{1,3},{2,32},{3,33},{32,34},{33,35},{34,64},{35,65},{64,66},... | collective-permute-start | bytes 393224
  574.7 27.3 %collective-permute-start.8 = (bf16[16,4096]{1,0:T(8,128)(2,1)}, bf16[16,4096]{1,0:T(8,128)(2,1)S(1)}, u32[]{:S(2)}, u32[]{:S(2)}) collective-permute-start(bf16[16,4096]{1,0:T(8,128)(2,1)} %get-tuple-element.23), channel_id=1, source_target_pairs={{0,1},{1,2},{2,3},{3,32},{32,33},{33,34},{34,35},{35,64},{64,65},{... | collective-permute-start | bytes 393224
  578.3 25.9 %collective-permute-start.6 = (bf16[16,4096]{1,0:T(8,128)(2,1)S(1)}, bf16[16,4096]{1,0:T(8,128)(2,1)S(1)}, u32[]{:S(2)}, u32[]{:S(2)}) collective-permute-start(bf16[16,4096]{1,0:T(8,128)(2,1)S(1)} %get-tuple-element.22), channel_id=1, source_target_pairs={{0,35},{1,64},{2,65},{3,66},{32,67},{33,96},{34,97},{35,98},{64,99... | collective-permute-start | bytes 393224
  582.4 26.1 %collective-permute-start.5 = (bf16[16,4096]{1,0:T(8,128)(2,1)S(1)}, bf16[16,4096]{1,0:T(8,128)(2,1)S(1)}, u32[]{:S(2)}, u32[]{:S(2)}) collective-permute-start(bf16[16,4096]{1,0:T(8,128)(2,1)S(1)} %get-tuple-element.22), channel_id=1, source_target_pairs={{0,34},{1,35},{2,64},{3,65},{32,66},{33,67},{34,96},{35,97},{64,98... | collective-permute-start | bytes 393224
  596.7 20.0 %copy-start.5 = (bf16[16,4096]{1,0:T(8,128)(2,1)S(1)}, bf16[16,4096]{1,0:T(8,128)(2,1)}, u32[]{:S(2)}) copy-start(bf16[16,4096]{1,0:T(8,128)(2,1)} %get-tuple-element.23) | copy-start | bytes 393220
  596.7 25.7 %collective-permute-start.4 = (bf16[16,4096]{1,0:T(8,128)(2,1)S(1)}, bf16[16,4096]{1,0:T(8,128)(2,1)}, u32[]{:S(2)}, u32[]{:S(2)}) collective-permute-start(bf16[16,4096]{1,0:T(8,128)(2,1)S(1)} %get-tuple-element.22), channel_id=1, source_target_pairs={{0,33},{1,34},{2,35},{3,64},{32,65},{33,66},{34,67},{35,96},{64,97... | collective-permute-start | bytes 393224
  600.0 10.7 %copy-start.11 = (bf16[16,4096]{1,0:T(8,128)(2,1)}, bf16[16,4096]{1,0:T(8,128)(2,1)S(1)}, u32[]{:S(2)}) copy-start(bf16[16,4096]{1,0:T(8,128)(2,1)S(1)} %collective-permute-done.9) | copy-start | bytes 393220
  600.0 22.4 %collective-permute-start.3 = (bf16[16,4096]{1,0:T(8,128)(2,1)S(1)}, bf16[16,4096]{1,0:T(8,128)(2,1)}, u32[]{:S(2)}, u32[]{:S(2)}) collective-permute-start(bf16[16,4096]{1,0:T(8,128)(2,1)S(1)} %get-tuple-element.22), channel_id=1, source_target_pairs={{0,32},{1,33},{2,34},{3,35},{32,64},{33,65},{34,66},{35,67},{64,96... | collective-permute-start | bytes 393224
  602.0 8.7 %copy-start.13 = (bf16[16,4096]{1,0:T(8,128)(2,1)}, bf16[16,4096]{1,0:T(8,128)(2,1)S(1)}, u32[]{:S(2)}) copy-start(bf16[16,4096]{1,0:T(8,128)(2,1)S(1)} %collective-permute-done.8) | copy-start | bytes 393220
  602.0 20.5 %collective-permute-start.2 = (bf16[16,4096]{1,0:T(8,128)(2,1)S(1)}, bf16[16,4096]{1,0:T(8,128)(2,1)}, u32[]{:S(2)}, u32[]{:S(2)}) collective-permute-start(bf16[16,4096]{1,0:T(8,128)(2,1)S(1)} %get-tuple-element.22), channel_id=1, source_target_pairs={{0,3},{1,32},{2,33},{3,34},{32,35},{33,64},{34,65},{35,66},{64,67}... | collective-permute-start | bytes 393224
  604.2 6.5 copy-start.10
  604.2 18.2 %collective-permute-start.1 = (bf16[16,4096]{1,0:T(8,128)(2,1)S(1)}, bf16[16,4096]{1,0:T(8,128)(2,1)}, u32[]{:S(2)}, u32[]{:S(2)}) collective-permute-start(bf16[16,4096]{1,0:T(8,128)(2,1)S(1)} %get-tuple-element.22), channel_id=1, source_target_pairs={{0,2},{1,3},{2,32},{3,33},{32,34},{33,35},{34,64},{35,65},{64,66},... | collective-permute-start | bytes 393224
  608.5 2.2 copy-start.12
  608.5 14.0 %collective-permute-start = (bf16[16,4096]{1,0:T(8,128)(2,1)S(1)}, bf16[16,4096]{1,0:T(8,128)(2,1)}, u32[]{:S(2)}, u32[]{:S(2)}) collective-permute-start(bf16[16,4096]{1,0:T(8,128)(2,1)S(1)} %get-tuple-element.22), channel_id=1, source_target_pairs={{0,1},{1,2},{2,3},{3,32},{32,33},{33,34},{34,35},{35,64},{64,65},{... | collective-permute-start | bytes 393224
  664.3 58.9 %all-to-all-start.1 = ((bf16[32,2,768]{2,1,0:T(2,128)(2,1)}), bf16[32,2,768]{2,1,0:T(2,128)(2,1)S(1)}, u32[]{:S(2)}, u32[]{:S(2)}) async-start(bf16[32,2,768]{2,1,0:T(2,128)(2,1)} %reshape.161), calls=%async_computation.1 | async-start | bytes 196608 | tf_op jit(solution)/shard_map/all_to_all | solution.py:94
  698.1 51.5 %copy-start.1 = (bf16[128,128]{1,0:T(8,128)(2,1)S(1)}, bf16[128,128]{1,0:T(8,128)(2,1)}, u32[]{:S(2)}) copy-start(bf16[128,128]{1,0:T(8,128)(2,1)} %param.7) | copy-start | bytes 98308
  720.5 27.1 %copy-start.4 = (f32[128,384]{0,1:T(8,128)S(1)}, f32[128,384]{0,1:T(8,128)}, u32[]{:S(2)}) copy-start(f32[128,384]{0,1:T(8,128)} %copy-done.3) | copy-start | bytes 589828
  723.2 25.4 %copy-start.6 = (f32[128,384]{0,1:T(8,128)S(1)}, f32[128,384]{0,1:T(8,128)}, u32[]{:S(2)}) copy-start(f32[128,384]{0,1:T(8,128)} %get-tuple-element.19) | copy-start | bytes 589828
  723.2 19.4 %all-to-all-start.3 = ((bf16[32,2,768]{2,1,0:T(2,128)(2,1)}), bf16[32,2,768]{2,1,0:T(2,128)(2,1)S(1)}, u32[]{:S(2)}, u32[]{:S(2)}) async-start(bf16[32,2,768]{2,1,0:T(2,128)(2,1)} %reshape.163), calls=%async_computation.3 | async-start | bytes 196608 | tf_op jit(solution)/shard_map/all_to_all | solution.py:101
Sparse Core Ops, SparseCore 0:
  10.5 151.2 all-gather.3
  163.6 88.7 all-gather.5
  254.2 93.6 all-gather.7
where the time goes:
time: 763 us; the launch traced here: 756 us
  waiting for transfers between devices  238 us (31%)
  blocking collectives  231 us (30%)
  local copies, waits for them, and re-layouts  79.3 us (10%)
  other arithmetic  75.6 us (10%)
  starting transfers between devices  73.5 us (10%)
  matrix products  43.9 us (6%)
  between operations  15.2 us (2%)
    unnamed x1, blocking collectives  182 us
    all_gather x1, waiting for transfers between devices, on_device(): rows_cot = lax.all_gather(arrived[1], ('dp', 'mp'), axis=1, tiled=True)[0]  83.3 us
    all_gather x1, waiting for transfers between devices, on_device(): rows_in = lax.all_gather(arrived[0], ('dp', 'mp'), axis=1, tiled=True)[0]  74.9 us
    all_gather x1, waiting for transfers between devices, on_device(): whole = lax.all_gather(dense_ffn, 'expert', axis=1, tiled=True)  72.3 us
    unnamed x50, local copies, waits for them, and re-layouts  51.6 us
    unnamed x16, starting transfers between devices  51.3 us
    unnamed x3, other arithmetic  44.8 us
    all_to_all x1, blocking collectives, on_device(): lax.all_to_all(cot_slots.reshape(shaped), ('expert', 'mp'), split_axis=0,...  26 us
  transfers between devices with their start and end apart: 21, of which 5 were waited for; matrix products, arithmetic and copies ran while one was open for 17% of the time, Pallas kernels for 0%

commit v1 on v0

v1 whole, which is shorter than its diff:
```python
import jax
import jax.numpy as jnp
from jax import lax
from jax.experimental import pallas as pl
from jax.experimental.pallas import tpu as pltpu
from jax.sharding import PartitionSpec as P

BF = jnp.bfloat16
F32 = jnp.float32
CAP = 48
N_E = 8
N_DP = 8
N_MP = 4
N_X = 4
LANE = 128
COLS = 256
HALF = 128
SLAB = 512
TOK = 128
ROWS = N_DP * CAP
VMEM_CAP = 56 * 1024 * 1024


def iota(shape, dim):
    return lax.broadcasted_iota(jnp.int32, shape, dim)


def dot_nn(a, b):
    return lax.dot_general(a, b, (((1,), (0,)), ((), ())), preferred_element_type=F32)


def dot_nt(a, b):
    return lax.dot_general(a, b, (((1,), (1,)), ((), ())), preferred_element_type=F32)


def dot_tn(a, b):
    return lax.dot_general(a, b, (((0,), (0,)), ((), ())), preferred_element_type=F32)


def tables(ids_ref):
    lane = iota((TOK, LANE), 1)
    hits = [(ids_ref[:, j : j + 1] == lane).astype(F32) for j in range(2)]
    earlier = (iota((TOK, TOK), 1) < iota((TOK, TOK), 0)).astype(BF)
    rank = dot_nn(earlier, (hits[0] + hits[1]).astype(BF))
    slot = iota((TOK, N_E * CAP), 1)
    out = []
    for j in range(2):
        place = jnp.sum(hits[j] * (rank + (lane * CAP).astype(F32)), axis=1, keepdims=True)
        out.append((slot == place.astype(jnp.int32)).astype(F32))
    return out


def dispatch_kernel(ids_ref, gates_ref, tok_ref, cot_ref, out_ref):
    t0, t1 = tables(ids_ref)
    rows_in = dot_tn((t0 + t1).astype(BF), tok_ref[...]).astype(BF)
    cot = cot_ref[...].astype(F32)
    scaled0 = (gates_ref[:, 0:1] * cot).astype(BF)
    scaled1 = (gates_ref[:, 1:2] * cot).astype(BF)
    rows_cot = (dot_tn(t0.astype(BF), scaled0) + dot_tn(t1.astype(BF), scaled1)).astype(BF)
    for e in range(N_E):
        out_ref[e, 0:CAP, :] = rows_in[e * CAP : (e + 1) * CAP]
        out_ref[e, CAP : 2 * CAP, :] = rows_cot[e * CAP : (e + 1) * CAP]


def combine_kernel(ids_ref, gates_ref, back_ref, mixed_ref, grad_ref):
    t0, t1 = tables(ids_ref)
    total = back_ref[:, 0].astype(F32)
    for q in range(1, N_MP):
        total = total + back_ref[:, q].astype(F32)
    out = total[:, 0:CAP].reshape(N_E * CAP, LANE)
    grad = total[:, CAP : 2 * CAP].reshape(N_E * CAP, LANE)
    high = lax.Precision.HIGHEST
    weighted = t0 * gates_ref[:, 0:1] + t1 * gates_ref[:, 1:2]
    mixed_ref[...] = jnp.dot(weighted, out, precision=high, preferred_element_type=F32).astype(BF)
    grad_ref[...] = jnp.dot(t0 + t1, grad, precision=high, preferred_element_type=F32).astype(BF)


def counts(marks_ref):
    upto = (iota((COLS, COLS), 0) <= iota((COLS, COLS), 1)).astype(BF)
    return dot_nn(marks_ref[...].astype(BF), upto)


def pick_row(values, row):
    return jnp.sum(jnp.where(iota(values.shape, 0) == row, values, 0.0), axis=0, keepdims=True)


def pack_kernel(where_ref, marks_ref, dense_ref, *outs):
    cum = counts(marks_ref)
    marks = marks_ref[...].astype(F32)
    col = iota((1, COLS), 1).astype(F32)
    dense = dense_ref[...]
    for k in range(N_X):
        expert = lax.rem(where_ref[0] + k, N_X) * 2 + where_ref[1]
        kept = jnp.where(pick_row(marks, expert) > 0.5, -1.0, col - pick_row(cum, expert))
        onehot = (iota((HALF, COLS), 0) == kept.astype(jnp.int32)).astype(BF)
        outs[k][...] = dot_nt(dense, onehot).astype(BF)


def weights_kernel(where_ref, marks_ref, fresh_ref, *refs):
    pieces, out_ref = refs[:-1], refs[-1]
    expert = where_ref[0] * 2 + where_ref[1]
    cum = pick_row(counts(marks_ref), expert)
    mark = pick_row(marks_ref[...].astype(F32), expert)
    col = iota((1, COLS), 1).astype(F32)
    source = jnp.where(mark > 0.5, HALF + cum - 1.0, col - cum).astype(jnp.int32)
    onehot = (iota((COLS, COLS), 0) == source).astype(BF)
    for s, piece in enumerate(pieces):
        side, k = divmod(s, N_X)
        slab = lax.rem(where_ref[0] + N_X - k, N_X) * 2 + (where_ref[1] if side == 0 else 1 - where_ref[1])
        place = pl.ds(pl.multiple_of(slab * SLAB, SLAB), SLAB)
        both = jnp.concatenate([piece[0], fresh_ref[0, place, :]], axis=1)
        out_ref[0, place, :] = dot_nn(both, onehot).astype(BF)


def expert_kernel(rows_ref, w_ref, acts_ref, out_ref, gate_acc, up_acc, down_acc):
    step = pl.program_id(0)

    @pl.when(step < N_MP)
    def _():
        rows = rows_ref[:, 0]
        rin = jnp.concatenate([rows[:, e, 0:CAP].reshape(ROWS, LANE) for e in range(N_E)], axis=1)
        rcot = jnp.concatenate(
            [rows[:, e, CAP : 2 * CAP].reshape(ROWS, LANE) for e in range(N_E)], axis=1
        )
        parts = (
            dot_nn(rin, w_ref[0, :, 0].reshape(N_E * LANE, COLS)),
            dot_nn(rin, w_ref[1, :, 0].reshape(N_E * LANE, COLS)),
            dot_nn(rcot, w_ref[2, :, 0].reshape(N_E * LANE, COLS)),
        )

        @pl.when(step == 0)
        def _():
            for acc, part in zip((gate_acc, up_acc, down_acc), parts):
                acc[...] = part

        @pl.when(step > 0)
        def _():
            for acc, part in zip((gate_acc, up_acc, down_acc), parts):
                acc[...] += part

        @pl.when(step == N_MP - 1)
        def _():
            gate, up, grad = gate_acc[...], up_acc[...], down_acc[...]
            sig = jax.nn.sigmoid(gate)
            act = gate * sig
            acts_ref[:, 0:COLS] = (grad * up * sig * (1.0 + gate * (1.0 - sig))).astype(BF)
            acts_ref[:, COLS : 2 * COLS] = (grad * act).astype(BF)
            acts_ref[:, 2 * COLS :] = (act * up).astype(BF)

    @pl.when(step >= N_MP)
    def _():
        pair = jnp.concatenate(
            [w_ref[p, :, 0].reshape(N_E * LANE, COLS) for p in range(2)], axis=1
        )
        out = dot_nt(acts_ref[:, 2 * COLS :], w_ref[2, :, 0].reshape(N_E * LANE, COLS)).astype(BF)
        grad = dot_nt(acts_ref[:, 0 : 2 * COLS], pair).astype(BF)
        for e in range(N_E):
            lanes = slice(e * LANE, (e + 1) * LANE)
            out_ref[:, e, 0, 0:CAP, :] = out[:, lanes].reshape(N_DP, CAP, LANE)
            out_ref[:, e, 0, CAP : 2 * CAP, :] = grad[:, lanes].reshape(N_DP, CAP, LANE)


def update_kernel(rows_ref, acts_ref, w_ref, new_ref):
    for e in range(N_E):
        rin = rows_ref[:, 0, e, 0:CAP].reshape(ROWS, LANE)
        rcot = rows_ref[:, 0, e, CAP : 2 * CAP].reshape(ROWS, LANE)
        pair = dot_tn(rin, acts_ref[:, 0 : 2 * COLS])
        grads = (pair[:, 0:COLS], pair[:, COLS:], dot_tn(rcot, acts_ref[:, 2 * COLS :]))
        for p in range(3):
            g = grads[p]
            new = w_ref[p, e, 0].astype(F32) * (1.0 - 0.0003) - 0.003 * (g / (jnp.abs(g) + 0.1))
            new_ref[p, e, 0] = new.astype(BF)


def call(kernel, outs, flops=0, nbytes=0, **kw):
    return pl.pallas_call(
        kernel,
        out_shape=outs,
        compiler_params=pltpu.CompilerParams(vmem_limit_bytes=VMEM_CAP),
        cost_estimate=pl.CostEstimate(flops=flops, bytes_accessed=nbytes, transcendentals=0),
        **kw,
    )


def sds(shape, dtype=BF):
    return jax.ShapeDtypeStruct(shape, dtype)


SMEM = pl.BlockSpec(memory_space=pltpu.SMEM)


def on_device(tokens, cotangent, gates, expert_ids, dense_ffn, redrawn, redraw):
    expert = lax.axis_index("expert")
    where = jnp.stack([expert // 2, expert % 2]).astype(jnp.int32)

    def along_x(piece, k):
        return lax.ppermute(
            piece, "expert", [(e, (e // 2 + k) % N_X * 2 + e % 2) for e in range(N_E)]
        )

    dense = dense_ffn.reshape(3 * SLAB, COLS)
    pack = call(
        pack_kernel,
        [sds((3 * SLAB, HALF))] * N_X,
        flops=2 * 3 * SLAB * COLS * HALF * N_X,
        nbytes=6 * 3 * SLAB * COLS,
        in_specs=[SMEM, pl.BlockSpec(), pl.BlockSpec()],
    )
    far = lax.ppermute(dense, "expert", [(e, e ^ 1) for e in range(N_E)])
    pieces = []
    for slab in (dense, far):
        packed = pack(where, redrawn, slab)
        pieces += [packed[0]] + [along_x(packed[k], k) for k in range(1, N_X)]
    pieces = [p.reshape(3, SLAB, HALF) for p in pieces]

    slots = call(dispatch_kernel, sds((N_E, 2 * CAP, LANE)), nbytes=400000)(
        expert_ids, gates, tokens, cotangent
    )
    rows = lax.all_to_all(
        slots.reshape(N_E * 2 * CAP, LANE), "expert", split_axis=0, concat_axis=0, tiled=True
    )
    rows = lax.all_gather(rows, "mp", axis=0, tiled=True)
    rows = lax.all_gather(rows, "dp", axis=0, tiled=True)
    rows = rows.reshape(N_DP, N_MP, N_E, 2 * CAP, LANE)

    weights = call(
        weights_kernel,
        sds((3, N_E * SLAB, COLS)),
        flops=2 * 3 * N_E * SLAB * COLS * COLS,
        nbytes=2 * 2 * 3 * N_E * SLAB * COLS,
        grid=(3,),
        in_specs=[
            SMEM,
            pl.BlockSpec((N_E, COLS), lambda p: (0, 0)),
            pl.BlockSpec((1, N_E * SLAB, HALF), lambda p: (p, 0, 0)),
        ]
        + [pl.BlockSpec((1, SLAB, HALF), lambda p: (p, 0, 0))] * (2 * N_X),
        out_specs=pl.BlockSpec((1, N_E * SLAB, COLS), lambda p: (p, 0, 0)),
    )(where, redrawn, redraw[0], *pieces)
    weights = weights.reshape(3, N_E, N_MP, LANE, COLS)

    flops = 2 * ROWS * N_E * SLAB * COLS * 3
    acts, outs = call(
        expert_kernel,
        [sds((ROWS, 3 * COLS)), sds((N_DP, N_E, N_MP, 2 * CAP, LANE))],
        flops=2 * flops,
        nbytes=25000000,
        grid=(2 * N_MP,),
        in_specs=[
            pl.BlockSpec(
                (N_DP, 1, N_E, 2 * CAP, LANE), lambda i: (0, jnp.minimum(i, N_MP - 1), 0, 0, 0)
            ),
            pl.BlockSpec((3, N_E, 1, LANE, COLS), lambda i: (0, 0, lax.rem(i, N_MP), 0, 0)),
        ],
        out_specs=[
            pl.BlockSpec((ROWS, 3 * COLS), lambda i: (0, 0)),
            pl.BlockSpec(
                (N_DP, N_E, 1, 2 * CAP, LANE), lambda i: (0, 0, jnp.maximum(i - N_MP, 0), 0, 0)
            ),
        ],
        scratch_shapes=[pltpu.VMEM((ROWS, COLS), F32)] * 3,
    )(rows, weights)

    part = lax.psum_scatter(
        outs.reshape(N_DP * N_E * N_MP * 2 * CAP, LANE), "dp", scatter_dimension=0, tiled=True
    )
    back = lax.all_to_all(part, ("expert", "mp"), split_axis=0, concat_axis=0, tiled=True)

    new_weights = call(
        update_kernel,
        sds((3, N_E, N_MP, LANE, COLS)),
        flops=flops,
        nbytes=19000000,
        grid=(N_MP,),
        in_specs=[
            pl.BlockSpec((N_DP, 1, N_E, 2 * CAP, LANE), lambda i: (0, i, 0, 0, 0)),
            pl.BlockSpec((ROWS, 3 * COLS), lambda i: (0, 0)),
            pl.BlockSpec((3, N_E, 1, LANE, COLS), lambda i: (0, 0, i, 0, 0)),
        ],
        out_specs=pl.BlockSpec((3, N_E, 1, LANE, COLS), lambda i: (0, 0, i, 0, 0)),
    )(rows, acts, weights)

    mixed, token_grad = call(combine_kernel, [sds((TOK, LANE))] * 2, nbytes=900000)(
        expert_ids, gates, back.reshape(N_E, N_MP, 2 * CAP, LANE)
    )
    return (mixed, token_grad, new_weights.reshape(1, 3, N_E * SLAB, COLS))


def solution(mesh):
    return jax.shard_map(
        on_device,
        mesh=mesh,
        in_specs=(
            P("dp", ("expert", "mp")),
            P("dp", ("expert", "mp")),
            P("dp", None),
            P("dp", None),
            P(None, "expert", ("dp", "mp")),
            P(None, ("dp", "mp")),
            P("expert", None, None, ("dp", "mp")),
        ),
        out_specs=(
            P("dp", ("expert", "mp")),
            P("dp", ("expert", "mp")),
            P("expert", None, None, ("dp", "mp")),
        ),
        check_vma=False,
    )
```

time: 763 us -> 221 us (0.29)
  blocking collectives: 231 us -> 39.6 us
  waiting for transfers between devices: 238 us -> 99.7 us
  other arithmetic: 75.6 us -> 0.65 us
  local copies, waits for them, and re-layouts: 79.3 us -> 5.34 us
  starting transfers between devices: 73.5 us -> 17.4 us
  matrix products: 43.9 us -> 0 us
  Pallas kernels: 0 us -> 43.2 us
    all_gather x3 -> x1, waiting for transfers between devices: 231 us -> 0.01 us  [on_device(): rows = lax.all_gather(rows, 'dp', axis=0, tiled=True)]
    unnamed x1 -> x0, blocking collectives: 182 us -> none
    unnamed x16 -> x0, starting transfers between devices: 51.3 us -> none
    reduce_scatter x0 -> x1, waiting for transfers between devices: none -> 48.8 us  [on_device(): lax.psum_scatter(outs.reshape(N_DP * N_E * N_MP * 2 * CAP, LANE), 'dp', s...]
    unnamed x50 -> x18, local copies, waits for them, and re-layouts: 51.6 us -> 5.34 us
    unnamed x3 -> x0, other arithmetic: 44.8 us -> none
    dot_general x10 -> x0, matrix products: 43.9 us -> none  [the longest x1 10.7 us: weight_terms(): jnp.einsum('rd,prc->pdc', rows_in, both, preferred_element_type=jnp.float32)]
    pallas_call x0 -> x7, Pallas kernels: none -> 43.2 us  [the longest x1 13.6 us: on_device(): call(expert_kernel, [sds((ROWS, 3 * COLS)), sds((N_DP, N_E, N_MP, 2 * CAP...]
  transfers between devices with their start and end apart: 21 -> 10, of which waited for: 5 -> 5; matrix products, arithmetic and copies ran while one was open for 17% -> 0% of each run, Pallas kernels for 0% -> 11%
where the time goes in v1:
time: 221 us; the launch traced here: 220 us
  waiting for transfers between devices  99.7 us (45%)
  Pallas kernels  43.2 us (20%)
  blocking collectives  39.6 us (18%)
  starting transfers between devices  17.4 us (8%)
  between operations  14.1 us (6%)
  local copies, waits for them, and re-layouts  5.34 us (2%)
    reduce_scatter x1, waiting for transfers between devices, on_device(): lax.psum_scatter(outs.reshape(N_DP * N_E * N_MP * 2 * CAP, LANE), 'dp', s...  48.8 us
    ppermute x1, waiting for transfers between devices, on_device(): far = lax.ppermute(dense, 'expert', [(e, e ^ 1) for e in range(N_E)])  26.1 us
    all_to_all x1, blocking collectives, on_device(): lax.all_to_all(slots.reshape(N_E * 2 * CAP, LANE), 'expert', split_axis=0...  22.6 us
    all_gather x1, blocking collectives, on_device(): rows = lax.all_gather(rows, 'mp', axis=0, tiled=True)  17 us
    pallas_call x1, Pallas kernels, on_device(): call(expert_kernel, [sds((ROWS, 3 * COLS)), sds((N_DP, N_E, N_MP, 2 * CAP...  13.6 us
    all_to_all x1, waiting for transfers between devices, on_device(): lax.all_to_all(part, ('expert', 'mp'), split_axis=0, concat_axis=0, tiled...  12.6 us
    ppermute x6, waiting for transfers between devices, along_x(): lax.ppermute(piece, 'expert', [(e, (e // 2 + k) % N_X * 2 + e % 2) for e...  12.3 us
    all_to_all x1, starting transfers between devices, on_device(): lax.all_to_all(part, ('expert', 'mp'), split_axis=0, concat_axis=0, tiled...  10.1 us
  transfers between devices with their start and end apart: 10, of which 5 were waited for; matrix products, arithmetic and copies ran while one was open for 0% of the time, Pallas kernels for 11%

profile of v1, /device:TPU:32, one launch (start us, length us, event | category | flops | bytes accessed | tf_op | source)
XLA Modules:
  0.0 220.0 jit_solution(10493802319756228918)
XLA Ops:
  7.2 0.0 all-gather.2.cloned.1.call-start
  7.2 1.4 copy.12.ids_ref
  8.6 1.4 copy.13.gates_ref
  10.0 2.2 shard_map.94
  12.2 22.6 %all_to_all.18 = bf16[8,96,128]{2,1,0:T(8,128)(2,1)S(1)} all-to-all(bf16[8,96,128]{2,1,0:T(8,128)(2,1)} %shard_map.94), channel_id=1, replica_groups=mesh['dp'=8,'expert'=8,'mp'=4] {'expert'}, dimensions={0} | all-to-all | bytes 393216 | tf_op jit(solution)/shard_map/all_to_all | solution.py:219
  34.8 17.0 %all_gather.6 = bf16[3072,128]{1,0:T(8,128)(2,1)} all-gather(bf16[768,128]{1,0:T(8,128)(2,1)S(1)} %bitcast.28), channel_id=1, replica_groups=mesh['dp'=8,'expert'=8,'mp'=4] {'mp'}, dimensions={0}, use_global_device_ids=true | all-gather | bytes 983040 | tf_op jit(solution)/shard_map/all_gather | solution.py:222
  51.8 0.0 all-gather.2.cloned.1.call-update
  51.8 0.0 reduce-scatter.2.cloned.1.call-start
  51.9 0.2 collective-permute-start.3
  52.1 0.7 pad_add_fusion.where_ref
  52.8 3.2 %shard_map.95 = (bf16[1536,128]{1,0:T(8,128)(2,1)}, bf16[1536,128]{1,0:T(8,128)(2,1)}, bf16[1536,128]{1,0:T(8,128)(2,1)}, bf16[1536,128]{1,0:T(8,128)(2,1)}) custom-call(s32[2]{0:T(128)} %pad_add_fusion.where_ref, s32[8,256]{1,0:T(8,128)} %marks_ref.5, bf16[1536,256]{1,0:T(8,128)(2,1)} %bitcast.38), custom_call_target="tpu_custom_call" | custom-call | flops 402653184 | bytes 2359296 | tf_op jit(solution)/shard_map/pallas_call | solution.py:212
  56.0 0.6 collective-permute-start
  56.5 2.1 collective-permute-start.1
  58.6 1.0 collective-permute-start.2
  59.7 26.1 %collective-permute-done.3.dense_ref = bf16[1536,256]{1,0:T(8,128)(2,1)S(1)} collective-permute-done((bf16[1536,256]{1,0:T(8,128)(2,1)}, bf16[1536,256]{1,0:T(8,128)(2,1)S(1)}, u32[]{:S(2)}, u32[]{:S(2)}) %collective-permute-start.3) | collective-permute-done | bytes 786464 | tf_op jit(solution)/shard_map/ppermute | solution.py:209
  85.8 0.0 copy-start.7
  85.8 0.9 copy-done.7
  86.6 3.2 %shard_map.96 = (bf16[1536,128]{1,0:T(8,128)(2,1)}, bf16[1536,128]{1,0:T(8,128)(2,1)}, bf16[1536,128]{1,0:T(8,128)(2,1)}, bf16[1536,128]{1,0:T(8,128)(2,1)}) custom-call(s32[2]{0:T(128)} %pad_add_fusion.where_ref, s32[8,256]{1,0:T(8,128)} %marks_ref.5, bf16[1536,256]{1,0:T(8,128)(2,1)} %copy-done.7), custom_call_target="tpu_custom_call" | custom-call | flops 402653184 | bytes 2359296 | tf_op jit(solution)/shard_map/pallas_call | solution.py:212
  89.8 0.0 collective-permute-start.4
  89.8 0.0 collective-permute-start.5
  89.8 0.0 collective-permute-done
  89.8 0.0 copy-start.1
  89.9 3.3 %collective-permute-start.6 = (bf16[1536,128]{1,0:T(8,128)(2,1)}, bf16[1536,128]{1,0:T(8,128)(2,1)S(1)}, u32[]{:S(2)}, u32[]{:S(2)}) collective-permute-start(bf16[1536,128]{1,0:T(8,128)(2,1)} %get-tuple-element.22), channel_id=1, source_target_pairs={{0,24},{4,28},{8,0},{12,4},{16,8},{20,12},{24,16},{28,20},{1,25},{... | collective-permute-start | bytes 1179656 | tf_op jit(solution)/shard_map/ppermute | solution.py:197
  93.2 0.0 collective-permute-done.1
  93.2 0.0 copy-start.2
  93.2 0.0 collective-permute-done.2
  93.2 0.0 copy-start.3
  93.2 11.6 %collective-permute-done.4 = bf16[1536,128]{1,0:T(8,128)(2,1)S(1)} collective-permute-done((bf16[1536,128]{1,0:T(8,128)(2,1)}, bf16[1536,128]{1,0:T(8,128)(2,1)S(1)}, u32[]{:S(2)}, u32[]{:S(2)}) %collective-permute-start.4) | collective-permute-done | bytes 393248 | tf_op jit(solution)/shard_map/ppermute | solution.py:197
  104.8 0.0 copy-start.4
  104.8 0.0 collective-permute-done.5
  104.8 0.0 copy-start.5
  104.8 0.7 collective-permute-done.6
  105.4 0.0 copy-start.6
  105.4 0.0 copy-done.1
  105.4 0.0 copy-done.2
  105.4 0.0 copy-done.3
  105.4 0.1 copy-done.4
  105.5 0.1 copy-done.5
  105.7 0.5 copy-done.6
  106.2 8.4 %shard_map.97 = bf16[3,4096,256]{2,1,0:T(8,128)(2,1)} custom-call(s32[2]{0:T(128)} %pad_add_fusion.where_ref, s32[8,256]{1,0:T(8,128)} %marks_ref.5, bf16[3,4096,128]{2,1,0:T(8,128)(2,1)} %bitcast.26, bf16[3,512,128]{2,1,0:T(8,128)(2,1)} %bitcast.29, bf16[3,512,128]{2,1,0:T(8,128)(2,1)} %bitcast.30, bf16[3,512,128]{2,1,0:T(8,128)(2,1)} %bitcast.31, ...), custom_call_target="tpu_custom_call" | custom-call | flops 1610612736 | bytes 12582912 | tf_op jit(solution)/shard_map/pallas_call | solution.py:226
  114.5 0.0 all-gather.2.cloned.1.call-done
  114.6 13.6 %shard_map.98 = (bf16[384,768]{1,0:T(8,128)(2,1)}, bf16[8,8,4,96,128]{4,3,2,1,0:T(8,128)(2,1)}) custom-call(bf16[8,4,8,96,128]{4,3,2,1,0:T(8,128)(2,1)} %bitcast.22, bf16[3,8,4,128,256]{4,3,2,1,0:T(8,128)(2,1)} %bitcast.19), custom_call_target="tpu_custom_call" | custom-call | flops 4831838208 | bytes 25000000 | tf_op jit(solution)/shard_map/pallas_call | solution.py:243
  128.1 0.0 reduce-scatter.2.cloned.1.call-update
  128.1 48.8 %reduce-scatter.2.cloned.1.call-done = bf16[3072,128]{1,0:T(8,128)(2,1)} async-done(((bf16[24576,128]{1,0:T(8,128)(2,1)}), bf16[3072,128]{1,0:T(8,128)(2,1)}) %reduce-scatter.2.cloned.1.call-update) | async-done | bytes 786448 | tf_op jit(solution)/shard_map/reduce_scatter | solution.py:264
  176.9 10.1 %all-to-all-start.1 = ((bf16[32,96,128]{2,1,0:T(8,128)(2,1)}), bf16[32,96,128]{2,1,0:T(8,128)(2,1)S(1)}, u32[]{:S(2)}, u32[]{:S(2)}) async-start(bf16[32,96,128]{2,1,0:T(8,128)(2,1)} %bitcast.27), calls=%async_computation.2 | async-start | bytes 1572864 | tf_op jit(solution)/shard_map/all_to_all | solution.py:267
  187.0 10.0 %shard_map.100 = bf16[3,8,4,128,256]{4,3,2,1,0:T(8,128)(2,1)} custom-call(bf16[8,4,8,96,128]{4,3,2,1,0:T(8,128)(2,1)} %bitcast.23, bf16[384,768]{1,0:T(8,128)(2,1)} %get-tuple-element.26.acts_ref, bf16[3,8,4,128,256]{4,3,2,1,0:T(8,128)(2,1)} %bitcast.20), custom_call_target="tpu_custom_call" | custom-call | flops 2415919104 | bytes 19000000 | tf_op jit(solution)/shard_map/pallas_call | solution.py:269
  197.0 12.6 %all-to-all-done.1 = bf16[32,96,128]{2,1,0:T(8,128)(2,1)S(1)} async-done(((bf16[32,96,128]{2,1,0:T(8,128)(2,1)}), bf16[32,96,128]{2,1,0:T(8,128)(2,1)S(1)}, u32[]{:S(2)}, u32[]{:S(2)}) %all-to-all-start.1) | async-done | bytes 786464 | tf_op jit(solution)/shard_map/all_to_all | solution.py:267
  209.6 0.0 copy-start
  209.6 0.9 copy-done
  210.5 2.7 %shard_map.99 = (bf16[128,128]{1,0:T(8,128)(2,1)}, bf16[128,128]{1,0:T(8,128)(2,1)}) custom-call(s32[128,2]{1,0:T(8,128)} %copy.12.ids_ref, f32[128,2]{1,0:T(8,128)} %copy.13.gates_ref, bf16[8,4,96,128]{3,2,1,0:T(8,128)(2,1)} %bitcast.25), custom_call_target="tpu_custom_call" | custom-call | bytes 900000 | tf_op jit(solution)/shard_map/pallas_call | solution.py:283
Async XLA Ops:
  7.2 107.4 %all-gather.2.cloned.1.call-start = ((), (), s32[]{:S(2)}) async-start(), calls=%async_computation.3 | async-start | bytes 7077888 | tf_op jit(solution)/shard_map/all_gather | solution.py:223
  51.8 125.1 %reduce-scatter.2.cloned.1.call-start = ((), (), s32[]{:S(2)}) async-start(), calls=%async_computation.4 | async-start | bytes 7077888 | tf_op jit(solution)/shard_map/reduce_scatter | solution.py:264
  51.9 33.9 %collective-permute-start.3 = (bf16[1536,256]{1,0:T(8,128)(2,1)}, bf16[1536,256]{1,0:T(8,128)(2,1)S(1)}, u32[]{:S(2)}, u32[]{:S(2)}) collective-permute-start(bf16[1536,256]{1,0:T(8,128)(2,1)} %bitcast.37), channel_id=1, source_target_pairs={{0,4},{4,0},{8,12},{12,8},{16,20},{20,16},{24,28},{28,24},{1,5},{5... | collective-permute-start | bytes 2359304 | tf_op jit(solution)/shard_map/ppermute | solution.py:209
  56.0 33.9 %collective-permute-start = (bf16[1536,128]{1,0:T(8,128)(2,1)}, bf16[1536,128]{1,0:T(8,128)(2,1)S(1)}, u32[]{:S(2)}, u32[]{:S(2)}) collective-permute-start(bf16[1536,128]{1,0:T(8,128)(2,1)} %get-tuple-element.16), channel_id=1, source_target_pairs={{0,8},{4,12},{8,16},{12,20},{16,24},{20,28},{24,0},{28,4},{1,9},{5... | collective-permute-start | bytes 1179656 | tf_op jit(solution)/shard_map/ppermute | solution.py:197
  56.5 36.6 %collective-permute-start.1 = (bf16[1536,128]{1,0:T(8,128)(2,1)}, bf16[1536,128]{1,0:T(8,128)(2,1)S(1)}, u32[]{:S(2)}, u32[]{:S(2)}) collective-permute-start(bf16[1536,128]{1,0:T(8,128)(2,1)} %get-tuple-element.17), channel_id=1, source_target_pairs={{0,16},{4,20},{8,24},{12,28},{16,0},{20,4},{24,8},{28,12},{1,17},{... | collective-permute-start | bytes 1179656 | tf_op jit(solution)/shard_map/ppermute | solution.py:197
  58.6 34.5 %collective-permute-start.2 = (bf16[1536,128]{1,0:T(8,128)(2,1)}, bf16[1536,128]{1,0:T(8,128)(2,1)S(1)}, u32[]{:S(2)}, u32[]{:S(2)}) collective-permute-start(bf16[1536,128]{1,0:T(8,128)(2,1)} %get-tuple-element.18), channel_id=1, source_target_pairs={{0,24},{4,28},{8,0},{12,4},{16,8},{20,12},{24,16},{28,20},{1,25},{... | collective-permute-start | bytes 1179656 | tf_op jit(solution)/shard_map/ppermute | solution.py:197
  85.8 0.9 copy-start.7
  89.8 14.9 %collective-permute-start.4 = (bf16[1536,128]{1,0:T(8,128)(2,1)}, bf16[1536,128]{1,0:T(8,128)(2,1)S(1)}, u32[]{:S(2)}, u32[]{:S(2)}) collective-permute-start(bf16[1536,128]{1,0:T(8,128)(2,1)} %get-tuple-element.20), channel_id=1, source_target_pairs={{0,8},{4,12},{8,16},{12,20},{16,24},{20,28},{24,0},{28,4},{1,9},{5... | collective-permute-start | bytes 1179656 | tf_op jit(solution)/shard_map/ppermute | solution.py:197
  89.8 14.9 %collective-permute-start.5 = (bf16[1536,128]{1,0:T(8,128)(2,1)}, bf16[1536,128]{1,0:T(8,128)(2,1)S(1)}, u32[]{:S(2)}, u32[]{:S(2)}) collective-permute-start(bf16[1536,128]{1,0:T(8,128)(2,1)} %get-tuple-element.21), channel_id=1, source_target_pairs={{0,16},{4,20},{8,24},{12,28},{16,0},{20,4},{24,8},{28,12},{1,17},{... | collective-permute-start | bytes 1179656 | tf_op jit(solution)/shard_map/ppermute | solution.py:197
  89.8 15.6 %copy-start.1 = (bf16[1536,128]{1,0:T(8,128)(2,1)}, bf16[1536,128]{1,0:T(8,128)(2,1)S(1)}, u32[]{:S(2)}) copy-start(bf16[1536,128]{1,0:T(8,128)(2,1)S(1)} %collective-permute-done) | copy-start | bytes 1179652
  89.9 15.6 %collective-permute-start.6 = (bf16[1536,128]{1,0:T(8,128)(2,1)}, bf16[1536,128]{1,0:T(8,128)(2,1)S(1)}, u32[]{:S(2)}, u32[]{:S(2)}) collective-permute-start(bf16[1536,128]{1,0:T(8,128)(2,1)} %get-tuple-element.22), channel_id=1, source_target_pairs={{0,24},{4,28},{8,0},{12,4},{16,8},{20,12},{24,16},{28,20},{1,25},{... | collective-permute-start | bytes 1179656 | tf_op jit(solution)/shard_map/ppermute | solution.py:197
  93.2 12.3 %copy-start.2 = (bf16[1536,128]{1,0:T(8,128)(2,1)}, bf16[1536,128]{1,0:T(8,128)(2,1)S(1)}, u32[]{:S(2)}) copy-start(bf16[1536,128]{1,0:T(8,128)(2,1)S(1)} %collective-permute-done.1) | copy-start | bytes 1179652
  93.2 12.3 %copy-start.3 = (bf16[1536,128]{1,0:T(8,128)(2,1)}, bf16[1536,128]{1,0:T(8,128)(2,1)S(1)}, u32[]{:S(2)}) copy-start(bf16[1536,128]{1,0:T(8,128)(2,1)S(1)} %collective-permute-done.2) | copy-start | bytes 1179652
  104.8 0.8 copy-start.4
  104.8 0.9 copy-start.5
  105.4 0.8 copy-start.6
  176.9 32.7 %all-to-all-start.1 = ((bf16[32,96,128]{2,1,0:T(8,128)(2,1)}), bf16[32,96,128]{2,1,0:T(8,128)(2,1)S(1)}, u32[]{:S(2)}, u32[]{:S(2)}) async-start(bf16[32,96,128]{2,1,0:T(8,128)(2,1)} %bitcast.27), calls=%async_computation.2 | async-start | bytes 1572864 | tf_op jit(solution)/shard_map/all_to_all | solution.py:267
  209.6 0.9 copy-start
Sparse Core Ops, SparseCore 0:
  52.0 41.2 all-gather.1
  128.3 48.6 reduce-scatter.1

commit v2 on v1

v2 whole, which is shorter than its diff:
```python
import jax
import jax.numpy as jnp
from jax import lax
from jax.experimental import pallas as pl
from jax.experimental.pallas import tpu as pltpu
from jax.sharding import PartitionSpec as P

BF = jnp.bfloat16
F32 = jnp.float32
CAP = 48
N_E = 8
N_DP = 8
N_X = 4
LANE = 128
COLS = 256
HALF = 128
SLAB = 512
TOK = 128
ROWS = N_DP * CAP
VMEM_CAP = 60 * 1024 * 1024
N_Y = 4
N_Q = 4
PIECE = N_E * N_Q * CAP


def iota(shape, dim):
    return lax.broadcasted_iota(jnp.int32, shape, dim)


def dot_nn(a, b):
    return lax.dot_general(a, b, (((1,), (0,)), ((), ())), preferred_element_type=F32)


def dot_nt(a, b):
    return lax.dot_general(a, b, (((1,), (1,)), ((), ())), preferred_element_type=F32)


def dot_tn(a, b):
    return lax.dot_general(a, b, (((0,), (0,)), ((), ())), preferred_element_type=F32)


def tables(ids_ref):
    ids = [ids_ref[j : j + 1, :] for j in range(2)]
    lane = iota((N_E, TOK), 0)
    hits = [(i == lane).astype(F32) for i in ids]
    earlier = (iota((TOK, TOK), 0) < iota((TOK, TOK), 1)).astype(BF)
    rank = dot_nn((hits[0] + hits[1]).astype(BF), earlier)
    slot = iota((N_E * CAP, TOK), 0)
    out = []
    for j in range(2):
        place = jnp.sum(hits[j] * rank, axis=0, keepdims=True).astype(jnp.int32) + ids[j] * CAP
        out.append((slot == place).astype(F32))
    return out


def dispatch_kernel(ids_ref, gates_ref, tok_ref, cot_ref, out_ref):
    t0, t1 = tables(ids_ref)
    rows_in = dot_nn((t0 + t1).astype(BF), tok_ref[...]).astype(BF)
    rows_cot = jnp.zeros((N_E * CAP, LANE), F32)
    for j, table in enumerate((t0, t1)):
        gate = jnp.sum(table * gates_ref[j : j + 1, :], axis=1, keepdims=True)
        rows_cot = rows_cot + gate * dot_nn(table.astype(BF), cot_ref[...])
    rows_cot = rows_cot.astype(BF)
    for e in range(N_E):
        for q in range(N_Q):
            out_ref[e, q, 0:CAP] = rows_in[e * CAP : (e + 1) * CAP]
            out_ref[e, q, CAP : 2 * CAP] = rows_cot[e * CAP : (e + 1) * CAP]


def combine_kernel(ids_ref, gates_ref, back_ref, mixed_ref, grad_ref):
    t0, t1 = tables(ids_ref)
    total = back_ref[:, 0].astype(F32)
    for q in range(1, N_Q):
        total = total + back_ref[:, q].astype(F32)
    weighted = t0 * gates_ref[0:1, :] + t1 * gates_ref[1:2, :]
    for table, first, out_ref in ((weighted, 0, mixed_ref), (t0 + t1, CAP, grad_ref)):
        out_ref[...] = lax.dot_general(
            table,
            total[:, first : first + CAP].reshape(N_E * CAP, LANE),
            (((0,), (0,)), ((), ())),
            precision=lax.Precision.HIGHEST,
            preferred_element_type=F32,
        ).astype(BF)


def counts(marks_ref):
    upto = (iota((COLS, COLS), 0) <= iota((COLS, COLS), 1)).astype(BF)
    return dot_nn(marks_ref[...].astype(BF), upto)


def pick_row(values, row):
    return jnp.sum(jnp.where(iota(values.shape, 0) == row, values, 0.0), axis=0, keepdims=True)


def pack_kernel(where_ref, marks_ref, dense_ref, *outs):
    cum = counts(marks_ref)
    marks = marks_ref[...].astype(F32)
    col = iota((1, COLS), 1).astype(F32)
    dense = dense_ref[...]
    for k in range(N_X):
        expert = lax.rem(where_ref[0] + k, N_X) * 2 + where_ref[1]
        kept = jnp.where(pick_row(marks, expert) > 0.5, -1.0, col - pick_row(cum, expert))
        onehot = (iota((HALF, COLS), 0) == kept.astype(jnp.int32)).astype(BF)
        outs[k][...] = dot_nt(dense, onehot).astype(BF)


def order_of_units(where_ref, marks_ref):
    expert = where_ref[0] * 2 + where_ref[1]
    cum = pick_row(counts(marks_ref), expert)
    mark = pick_row(marks_ref[...].astype(F32), expert)
    col = iota((1, COLS), 1).astype(F32)
    source = jnp.where(mark > 0.5, HALF + cum - 1.0, col - cum).astype(jnp.int32)
    return (iota((COLS, COLS), 0) == source).astype(BF)


def slab_rows(rows_ref, z, first):
    return jnp.concatenate(
        [
            rows_ref[:, 0, z, q, first : first + CAP].reshape(ROWS, LANE)
            for q in range(N_Q)
        ],
        axis=1,
    )


def accumulate(step, accs, parts):
    @pl.when(step == 0)
    def _():
        for acc, part in zip(accs, parts):
            acc[...] = part

    @pl.when(step > 0)
    def _():
        for acc, part in zip(accs, parts):
            acc[...] += part


def expert_kernel(where_ref, rows_ref, fresh_ref, *refs):
    near, far, refs = refs[:N_X], refs[N_X : 2 * N_X], refs[2 * N_X :]
    hidden_ref, both_ref, out_ref, held, gate_acc, up_acc, down_acc = refs
    step = pl.program_id(0)
    z, other_z = where_ref[1], 1 - where_ref[1]

    for k in range(N_X):

        @pl.when(step == k)
        def _():
            for p in range(3):
                for side, (at, piece) in enumerate(((z, near[k][p]), (other_z, far[k][p]))):
                    held[k, p, side * SLAB : (side + 1) * SLAB, :] = jnp.concatenate(
                        [piece, fresh_ref[p, 0, at]], axis=1
                    )

    @pl.when(step < N_X)
    def _():
        rows_in = jnp.concatenate([slab_rows(rows_ref, z, 0), slab_rows(rows_ref, other_z, 0)], axis=1)
        rows_cot = jnp.concatenate(
            [slab_rows(rows_ref, z, CAP), slab_rows(rows_ref, other_z, CAP)], axis=1
        )
        parts = [
            dot_nn(r, held[step, p]) for p, r in enumerate((rows_in, rows_in, rows_cot))
        ]
        accumulate(step, (gate_acc, up_acc, down_acc), parts)

    @pl.when(step == N_X - 1)
    def _():
        gate, up, grad = gate_acc[...], up_acc[...], down_acc[...]
        sig = jax.nn.sigmoid(gate)
        act = gate * sig
        hidden_ref[...] = (act * up).astype(BF)
        both_ref[:, 0:COLS] = (grad * up * sig * (1.0 + gate * (1.0 - sig))).astype(BF)
        both_ref[:, COLS:] = (grad * act).astype(BF)

    @pl.when(step >= N_X)
    def _():
        k = step - N_X
        pair = jnp.concatenate([held[k, 0], held[k, 1]], axis=1)
        outs = dot_nt(hidden_ref[...], held[k, 2]).astype(BF)
        grads = dot_nt(both_ref[...], pair).astype(BF)
        for first, values in ((0, outs), (CAP, grads)):
            for side, at in enumerate((z, other_z)):
                for q in range(N_Q):
                    lane = side * SLAB + q * LANE
                    out_ref[:, 0, at, q, first : first + CAP] = values[
                        :, lane : lane + LANE
                    ].reshape(N_DP, CAP, LANE)


def update_kernel(where_ref, rows_ref, fresh_ref, *refs):
    near, far, refs = refs[:N_X], refs[N_X : 2 * N_X], refs[2 * N_X :]
    hidden_ref, both_ref, marks_ref, new_ref, order, held = refs
    step = pl.program_id(0)

    @pl.when(step == 0)
    def _():
        order[...] = order_of_units(where_ref, marks_ref)

    for k in range(N_X):

        @pl.when(step == k)
        def _():
            for p in range(3):
                held[p, 0] = near[k][p]
                held[p, 1] = far[k][p]

    for side, z in enumerate((where_ref[1], 1 - where_ref[1])):
        pair = dot_tn(slab_rows(rows_ref, z, 0), both_ref[...])
        down = dot_tn(slab_rows(rows_ref, z, CAP), hidden_ref[...])
        for p, g in enumerate((pair[:, 0:COLS], pair[:, COLS:], down)):
            w = jnp.concatenate([held[p, side], fresh_ref[p, 0, z]], axis=1).astype(F32)
            new = w * (1.0 - 0.0003) - 0.003 * (g / (jnp.abs(g) + 0.1))
            new_ref[p, 0, z] = dot_nn(new.astype(BF), order[...]).astype(BF)


def call(kernel, outs, prefetch=0, scratch=(), **kw):
    if "grid" in kw:
        kw = dict(
            grid_spec=pltpu.PrefetchScalarGridSpec(
                num_scalar_prefetch=prefetch, scratch_shapes=list(scratch), **kw
            )
        )
    return pl.pallas_call(
        kernel,
        out_shape=outs,
        compiler_params=pltpu.CompilerParams(vmem_limit_bytes=VMEM_CAP),
        cost_estimate=pl.CostEstimate(flops=COST, bytes_accessed=COST, transcendentals=0),
        **kw,
    )


COST = 1024


def sds(shape, dtype=BF):
    return jax.ShapeDtypeStruct(shape, dtype)


SMEM = pl.BlockSpec(memory_space=pltpu.SMEM)
VIEW = (N_X, 2, N_Q, 2 * CAP, LANE)


def block_x(k, w):
    return lax.rem(w[0] + N_X - k, N_X)


def front_step(i):
    return jnp.minimum(i, N_X - 1)


def back_step(i):
    return jnp.maximum(i - N_X, 0)


def rows_spec(step):
    return pl.BlockSpec(
        (N_DP, 1) + VIEW[1:], lambda i, w: (0, block_x(step(i), w), 0, 0, 0, 0)
    )


def whole_spec(shape):
    return pl.BlockSpec(shape, lambda i, w: (0,) * len(shape))


FRESH_SPEC = pl.BlockSpec(
    (3, 1, 2, SLAB, HALF), lambda i, w: (0, block_x(front_step(i), w), 0, 0, 0)
)


def after(values, *first):
    return lax.optimization_barrier((values, first))[0]


def on_device(tokens, cotangent, gates, expert_ids, dense_ffn, redrawn, redraw):
    expert = lax.axis_index("expert")
    x, z = expert // 2, expert % 2
    where = jnp.stack([x, z]).astype(jnp.int32)

    def along_x(piece, k):
        return lax.ppermute(
            piece, "expert", [(e, (e // 2 + k) % N_X * 2 + e % 2) for e in range(N_E)]
        )

    def other_side(slab):
        return lax.ppermute(slab, "expert", [(e, e ^ 1) for e in range(N_E)])

    def exchange(rows):
        return lax.all_to_all(rows, ("expert", "mp"), split_axis=0, concat_axis=0, tiled=True)

    def pack(slab):
        rows = slab.shape[0]
        return call(
            pack_kernel,
            [sds((rows, HALF))] * N_X,
            in_specs=[SMEM, pl.BlockSpec(), pl.BlockSpec()],
        )(where, redrawn, slab)

    def to_holders(packed):
        return [packed[0]] + [along_x(packed[k], k) for k in range(1, N_X)]

    ids, weights = expert_ids.T, gates.T
    slots = call(dispatch_kernel, sds((N_E, N_Q, 2 * CAP, LANE)))(ids, weights, tokens, cotangent)
    mine = exchange(slots.reshape(2 * PIECE, LANE))

    rows = lax.all_gather(mine, "dp", axis=0, tiled=True).reshape((N_DP,) + VIEW)
    dense = dense_ffn.reshape(3 * SLAB, COLS)
    mine, dense, near = lax.optimization_barrier((mine, dense, pack(dense)))
    near = to_holders(near)
    far = to_holders(pack(other_side(dense)))
    pieces = [p.reshape(3, SLAB, HALF) for p in near + far]
    piece_specs = [whole_spec(p.shape) for p in pieces]
    fresh = redraw.reshape(3, N_X, 2, SLAB, HALF)

    acts = [sds((ROWS, COLS)), sds((ROWS, 2 * COLS))]
    act_specs = [whole_spec(a.shape) for a in acts]
    hidden, both, sums = call(
        expert_kernel,
        acts + [sds((N_DP,) + VIEW)],
        prefetch=1,
        scratch=[pltpu.VMEM((N_X, 3, 2 * SLAB, COLS), BF)] + [pltpu.VMEM((ROWS, COLS), F32)] * 3,
        grid=(2 * N_X,),
        in_specs=[rows_spec(front_step), FRESH_SPEC] + piece_specs,
        out_specs=act_specs + [rows_spec(back_step)],
    )(where, rows, fresh, *pieces)

    total = lax.psum_scatter(
        sums.reshape(N_DP * 2 * PIECE, LANE), "dp", scatter_dimension=0, tiled=True
    )
    new_weights = call(
        update_kernel,
        sds((3, N_X, 2, SLAB, COLS)),
        prefetch=1,
        scratch=[pltpu.VMEM((COLS, COLS), BF), pltpu.VMEM((3, 2, SLAB, HALF), BF)],
        grid=(N_X,),
        in_specs=[rows_spec(front_step), FRESH_SPEC]
        + piece_specs
        + act_specs
        + [whole_spec((N_E, COLS))],
        out_specs=pl.BlockSpec(
            (3, 1, 2, SLAB, COLS), lambda i, w: (0, block_x(i, w), 0, 0, 0)
        ),
    )(where, rows, fresh, *pieces, hidden, both, redrawn)
    back = exchange(total).reshape(N_E, N_Q, 2 * CAP, LANE)
    mixed, token_grad = call(combine_kernel, [sds((TOK, LANE))] * 2)(ids, weights, back)
    return (mixed, token_grad, new_weights.reshape(1, 3, N_E * SLAB, COLS))


def solution(mesh):
    return jax.shard_map(
        on_device,
        mesh=mesh,
        in_specs=(
            P("dp", ("expert", "mp")),
            P("dp", ("expert", "mp")),
            P("dp", None),
            P("dp", None),
            P(None, "expert", ("dp", "mp")),
            P(None, ("dp", "mp")),
            P("expert", None, None, ("dp", "mp")),
        ),
        out_specs=(
            P("dp", ("expert", "mp")),
            P("dp", ("expert", "mp")),
            P("expert", None, None, ("dp", "mp")),
        ),
        check_vma=False,
    )
```

time: 221 us -> 212 us (0.959)
  Pallas kernels: 43.2 us -> 37 us
  blocking collectives: 39.6 us -> 34.5 us
  starting transfers between devices: 17.4 us -> 20.7 us
  local copies, waits for them, and re-layouts: 5.34 us -> 2.5 us
  waiting for transfers between devices: 99.7 us -> 102 us
    all_gather x1 -> x0, blocking collectives: 17 us -> none  [on_device(): rows = lax.all_gather(rows, 'mp', axis=0, tiled=True)]
    all_to_all x1, blocking collectives: 22.6 us -> 34.5 us  [exchange(): lax.all_to_all(rows, ('expert', 'mp'), split_axis=0, concat_axis=0, tiled...]
    ppermute x1, waiting for transfers between devices: 26.1 us -> 32.4 us  [other_side(): return lax.ppermute(slab, 'expert', [(e, e ^ 1) for e in range(N_E)])]
    pallas_call x7 -> x6, Pallas kernels: 43.2 us -> 37 us  [the longest x1 13.8 us: on_device(): call(expert_kernel, acts + [sds((N_DP,) + VIEW)], prefetch=1, scratch=[pl...]
    reduce_scatter x1, waiting for transfers between devices: 48.8 us -> 43.3 us  [on_device(): lax.psum_scatter(sums.reshape(N_DP * 2 * PIECE, LANE), 'dp', scatter_dime...]
    ppermute x6, waiting for transfers between devices: 12.3 us -> 16.3 us  [along_x(): lax.ppermute(piece, 'expert', [(e, (e // 2 + k) % N_X * 2 + e % 2) for e...]
    unnamed x18 -> x16, local copies, waits for them, and re-layouts: 5.34 us -> 2.5 us
    ppermute x6, starting transfers between devices: 6.98 us -> 9.76 us  [along_x(): lax.ppermute(piece, 'expert', [(e, (e // 2 + k) % N_X * 2 + e % 2) for e...]
  transfers between devices with their start and end apart: 10 -> 10, of which waited for: 5 -> 5; matrix products, arithmetic and copies ran while one was open for 0% -> 0% of each run, Pallas kernels for 11% -> 9%
where the time goes in v2:
time: 212 us
  waiting for transfers between devices  102 us (48%)
  Pallas kernels  37 us (17%)
  blocking collectives  34.5 us (16%)
  starting transfers between devices  20.7 us (10%)
  between operations  14.1 us (7%)
  local copies, waits for them, and re-layouts  2.5 us (1%)
    reduce_scatter x1, waiting for transfers between devices, on_device(): lax.psum_scatter(sums.reshape(N_DP * 2 * PIECE, LANE), 'dp', scatter_dime...  43.3 us
    all_to_all x1, blocking collectives, exchange(): lax.all_to_all(rows, ('expert', 'mp'), split_axis=0, concat_axis=0, tiled...  34.5 us
    ppermute x1, waiting for transfers between devices, other_side(): return lax.ppermute(slab, 'expert', [(e, e ^ 1) for e in range(N_E)])  32.4 us
    ppermute x6, waiting for transfers between devices, along_x(): lax.ppermute(piece, 'expert', [(e, (e // 2 + k) % N_X * 2 + e % 2) for e...  16.3 us
    pallas_call x1, Pallas kernels, on_device(): call(expert_kernel, acts + [sds((N_DP,) + VIEW)], prefetch=1, scratch=[pl...  13.8 us
    pallas_call x1, Pallas kernels, on_device(): call(update_kernel, sds((3, N_X, 2, SLAB, COLS)), prefetch=1, scratch=[pl...  12.2 us
    all_to_all x1, waiting for transfers between devices, exchange(): lax.all_to_all(rows, ('expert', 'mp'), split_axis=0, concat_axis=0, tiled...  10.4 us
    all_to_all x1, starting transfers between devices, exchange(): lax.all_to_all(rows, ('expert', 'mp'), split_axis=0, concat_axis=0, tiled...  10 us
  transfers between devices with their start and end apart: 10, of which 5 were waited for; matrix products, arithmetic and copies ran while one was open for 0% of the time, Pallas kernels for 9%

profile of v2, /device:TPU:32, one launch (start us, length us, event | category | flops | bytes accessed | tf_op | source)
XLA Modules:
  0.0 211.8 jit_solution(13669136095712480754)
XLA Ops:
  7.2 0.0 all-gather.2.cloned.1.call-start
  7.2 2.1 shard_map.94
  9.3 34.5 %all_to_all.21 = bf16[32,96,128]{2,1,0:T(8,128)(2,1)} all-to-all(bf16[32,96,128]{2,1,0:T(8,128)(2,1)} %bitcast.29), channel_id=1, replica_groups=mesh['dp'=8,'expert'=8,'mp'=4] {'expert','mp'}, dimensions={0} | all-to-all | bytes 1572864 | tf_op jit(solution)/shard_map/all_to_all | solution.py:287
  43.7 0.0 all-gather.2.cloned.1.call-update
  43.8 0.0 reduce-scatter.2.cloned.1.call-start
  43.8 0.6 pad_add_fusion.where_ref
  44.4 3.3 %shard_map.95 = (bf16[1536,128]{1,0:T(8,128)(2,1)}, bf16[1536,128]{1,0:T(8,128)(2,1)}, bf16[1536,128]{1,0:T(8,128)(2,1)}, bf16[1536,128]{1,0:T(8,128)(2,1)}) custom-call(s32[2]{0:T(128)} %pad_add_fusion.where_ref, s32[8,256]{1,0:T(8,128)} %refs_10_.1, bf16[1536,256]{1,0:T(8,128)(2,1)} %bitcast.47), custom_call_target="tpu_custom_call" | custom-call | flops 1024 | bytes 1024 | tf_op jit(solution)/shard_map/pallas_call | solution.py:291
  47.7 0.8 collective-permute-start.3
  48.5 0.6 collective-permute-start
  49.2 2.6 %collective-permute-start.1 = (bf16[1536,128]{1,0:T(8,128)(2,1)}, bf16[1536,128]{1,0:T(8,128)(2,1)S(1)}, u32[]{:S(2)}, u32[]{:S(2)}) collective-permute-start(bf16[1536,128]{1,0:T(8,128)(2,1)} %get-tuple-element.27), channel_id=1, source_target_pairs={{0,16},{4,20},{8,24},{12,28},{16,0},{20,4},{24,8},{28,12},{1,17},{... | collective-permute-start | bytes 1179656 | tf_op jit(solution)/shard_map/ppermute | solution.py:279
  51.7 1.4 collective-permute-start.2
  53.2 32.4 %collective-permute-done.3.dense_ref = bf16[1536,256]{1,0:T(8,128)(2,1)S(1)} collective-permute-done((bf16[1536,256]{1,0:T(8,128)(2,1)}, bf16[1536,256]{1,0:T(8,128)(2,1)S(1)}, u32[]{:S(2)}, u32[]{:S(2)}) %collective-permute-start.3) | collective-permute-done | bytes 786464 | tf_op jit(solution)/shard_map/ppermute | solution.py:284
  85.6 0.0 copy-start.7
  85.6 0.9 copy-done.7
  86.4 3.2 %shard_map.96 = (bf16[1536,128]{1,0:T(8,128)(2,1)}, bf16[1536,128]{1,0:T(8,128)(2,1)}, bf16[1536,128]{1,0:T(8,128)(2,1)}, bf16[1536,128]{1,0:T(8,128)(2,1)}) custom-call(s32[2]{0:T(128)} %pad_add_fusion.where_ref, s32[8,256]{1,0:T(8,128)} %refs_10_.1, bf16[1536,256]{1,0:T(8,128)(2,1)} %copy-done.7), custom_call_target="tpu_custom_call" | custom-call | flops 1024 | bytes 1024 | tf_op jit(solution)/shard_map/pallas_call | solution.py:291
  89.6 1.1 collective-permute-start.4
  90.7 1.4 collective-permute-start.5
  92.1 0.0 collective-permute-done
  92.1 0.0 copy-start.1
  92.1 2.6 %collective-permute-start.6 = (bf16[1536,128]{1,0:T(8,128)(2,1)}, bf16[1536,128]{1,0:T(8,128)(2,1)S(1)}, u32[]{:S(2)}, u32[]{:S(2)}) collective-permute-start(bf16[1536,128]{1,0:T(8,128)(2,1)} %get-tuple-element.33), channel_id=1, source_target_pairs={{0,24},{4,28},{8,0},{12,4},{16,8},{20,12},{24,16},{28,20},{1,25},{... | collective-permute-start | bytes 1179656 | tf_op jit(solution)/shard_map/ppermute | solution.py:279
  94.8 0.0 collective-permute-done.1
  94.8 0.0 copy-start.2
  94.8 0.0 collective-permute-done.2
  94.8 0.0 copy-start.3
  94.8 15.7 %collective-permute-done.4 = bf16[1536,128]{1,0:T(8,128)(2,1)S(1)} collective-permute-done((bf16[1536,128]{1,0:T(8,128)(2,1)}, bf16[1536,128]{1,0:T(8,128)(2,1)S(1)}, u32[]{:S(2)}, u32[]{:S(2)}) %collective-permute-start.4) | collective-permute-done | bytes 393248 | tf_op jit(solution)/shard_map/ppermute | solution.py:279
  110.5 0.0 copy-start.4
  110.5 0.0 collective-permute-done.5
  110.5 0.0 copy-start.5
  110.5 0.6 collective-permute-done.6
  111.1 0.0 copy-start.6
  111.1 0.0 all-gather.2.cloned.1.call-done
  111.1 0.0 copy-done.1
  111.1 0.0 copy-done.2
  111.1 0.0 copy-done.3
  111.1 0.1 copy-done.4
  111.2 0.2 copy-done.5
  111.4 0.5 copy-done.6
  111.9 13.8 %shard_map.97 = (bf16[384,256]{1,0:T(8,128)(2,1)}, bf16[384,512]{1,0:T(8,128)(2,1)}, bf16[8,4,2,4,96,128]{5,4,3,2,1,0:T(8,128)(2,1)}) custom-call(s32[2]{0:T(128)} %pad_add_fusion.where_ref, bf16[8,4,2,4,96,128]{5,4,3,2,1,0:T(8,128)(2,1)} %bitcast.21, bf16[3,4,2,512,128]{4,3,2,1,0:T(8,128)(2,1)} %bitcast.23, bf16[3,512,128]{2,1,0:T(8,128)(2,1)} %bitcast.30, ...), custom_call_target="tpu_custom_call" | custom-call | flops 1024 | bytes 1024 | tf_op jit(solution)/shard_map/pallas_call | solution.py:315
  125.7 0.0 reduce-scatter.2.cloned.1.call-update
  125.7 43.3 %reduce-scatter.2.cloned.1.call-done = bf16[3072,128]{1,0:T(8,128)(2,1)} async-done(((bf16[24576,128]{1,0:T(8,128)(2,1)}), bf16[3072,128]{1,0:T(8,128)(2,1)}) %reduce-scatter.2.cloned.1.call-update) | async-done | bytes 786448 | tf_op jit(solution)/shard_map/reduce_scatter | solution.py:325
  169.0 10.0 %all-to-all-start.1 = ((bf16[32,96,128]{2,1,0:T(8,128)(2,1)}), bf16[32,96,128]{2,1,0:T(8,128)(2,1)S(1)}, u32[]{:S(2)}, u32[]{:S(2)}) async-start(bf16[32,96,128]{2,1,0:T(8,128)(2,1)} %bitcast.46), calls=%async_computation.2 | async-start | bytes 1572864 | tf_op jit(solution)/shard_map/all_to_all | solution.py:287
  179.0 12.2 %shard_map.99 = bf16[3,4,2,512,256]{4,3,2,1,0:T(8,128)(2,1)} custom-call(s32[2]{0:T(128)} %pad_add_fusion.where_ref, bf16[8,4,2,4,96,128]{5,4,3,2,1,0:T(8,128)(2,1)} %bitcast.22, bf16[3,4,2,512,128]{4,3,2,1,0:T(8,128)(2,1)} %bitcast.24, bf16[3,512,128]{2,1,0:T(8,128)(2,1)} %bitcast.31, bf16[3,512,128]{2,1,0:T(8,128)(2,1)} %bitcast.33, ...), custom_call_target="tpu_custom_call" | custom-call | flops 1024 | bytes 1024 | tf_op jit(solution)/shard_map/pallas_call | solution.py:328
  191.2 10.4 %all-to-all-done.1 = bf16[32,96,128]{2,1,0:T(8,128)(2,1)S(1)} async-done(((bf16[32,96,128]{2,1,0:T(8,128)(2,1)}), bf16[32,96,128]{2,1,0:T(8,128)(2,1)S(1)}, u32[]{:S(2)}, u32[]{:S(2)}) %all-to-all-start.1) | async-done | bytes 786464 | tf_op jit(solution)/shard_map/all_to_all | solution.py:287
  201.6 0.0 copy-start
  201.6 0.9 copy-done
  202.5 2.5 %shard_map.98 = (bf16[128,128]{1,0:T(8,128)(2,1)}, bf16[128,128]{1,0:T(8,128)(2,1)}) custom-call(s32[2,128]{1,0:T(2,128)} %bitcast.50, f32[2,128]{1,0:T(2,128)} %bitcast.52, bf16[8,4,96,128]{3,2,1,0:T(8,128)(2,1)} %bitcast.28), custom_call_target="tpu_custom_call" | custom-call | flops 1024 | bytes 1024 | tf_op jit(solution)/shard_map/pallas_call | solution.py:343
Async XLA Ops:
  7.2 103.9 %all-gather.2.cloned.1.call-start = ((), (), s32[]{:S(2)}) async-start(), calls=%async_computation.3 | async-start | bytes 7077888 | tf_op jit(solution)/shard_map/all_gather | solution.py:304
  43.8 125.2 %reduce-scatter.2.cloned.1.call-start = ((), (), s32[]{:S(2)}) async-start(), calls=%async_computation.4 | async-start | bytes 7077888 | tf_op jit(solution)/shard_map/reduce_scatter | solution.py:325
  47.7 37.8 %collective-permute-start.3 = (bf16[1536,256]{1,0:T(8,128)(2,1)}, bf16[1536,256]{1,0:T(8,128)(2,1)S(1)}, u32[]{:S(2)}, u32[]{:S(2)}) collective-permute-start(bf16[1536,256]{1,0:T(8,128)(2,1)} %bitcast.48), channel_id=1, source_target_pairs={{0,4},{4,0},{8,12},{12,8},{16,20},{20,16},{24,28},{28,24},{1,5},{5... | collective-permute-start | bytes 2359304 | tf_op jit(solution)/shard_map/ppermute | solution.py:284
  48.5 43.6 %collective-permute-start = (bf16[1536,128]{1,0:T(8,128)(2,1)}, bf16[1536,128]{1,0:T(8,128)(2,1)S(1)}, u32[]{:S(2)}, u32[]{:S(2)}) collective-permute-start(bf16[1536,128]{1,0:T(8,128)(2,1)} %get-tuple-element.26), channel_id=1, source_target_pairs={{0,8},{4,12},{8,16},{12,20},{16,24},{20,28},{24,0},{28,4},{1,9},{5... | collective-permute-start | bytes 1179656 | tf_op jit(solution)/shard_map/ppermute | solution.py:279
  49.2 45.6 %collective-permute-start.1 = (bf16[1536,128]{1,0:T(8,128)(2,1)}, bf16[1536,128]{1,0:T(8,128)(2,1)S(1)}, u32[]{:S(2)}, u32[]{:S(2)}) collective-permute-start(bf16[1536,128]{1,0:T(8,128)(2,1)} %get-tuple-element.27), channel_id=1, source_target_pairs={{0,16},{4,20},{8,24},{12,28},{16,0},{20,4},{24,8},{28,12},{1,17},{... | collective-permute-start | bytes 1179656 | tf_op jit(solution)/shard_map/ppermute | solution.py:279
  51.7 43.0 %collective-permute-start.2 = (bf16[1536,128]{1,0:T(8,128)(2,1)}, bf16[1536,128]{1,0:T(8,128)(2,1)S(1)}, u32[]{:S(2)}, u32[]{:S(2)}) collective-permute-start(bf16[1536,128]{1,0:T(8,128)(2,1)} %get-tuple-element.28), channel_id=1, source_target_pairs={{0,24},{4,28},{8,0},{12,4},{16,8},{20,12},{24,16},{28,20},{1,25},{... | collective-permute-start | bytes 1179656 | tf_op jit(solution)/shard_map/ppermute | solution.py:279
  85.6 0.9 copy-start.7
  89.6 20.9 %collective-permute-start.4 = (bf16[1536,128]{1,0:T(8,128)(2,1)}, bf16[1536,128]{1,0:T(8,128)(2,1)S(1)}, u32[]{:S(2)}, u32[]{:S(2)}) collective-permute-start(bf16[1536,128]{1,0:T(8,128)(2,1)} %get-tuple-element.31), channel_id=1, source_target_pairs={{0,8},{4,12},{8,16},{12,20},{16,24},{20,28},{24,0},{28,4},{1,9},{5... | collective-permute-start | bytes 1179656 | tf_op jit(solution)/shard_map/ppermute | solution.py:279
  90.7 19.8 %collective-permute-start.5 = (bf16[1536,128]{1,0:T(8,128)(2,1)}, bf16[1536,128]{1,0:T(8,128)(2,1)S(1)}, u32[]{:S(2)}, u32[]{:S(2)}) collective-permute-start(bf16[1536,128]{1,0:T(8,128)(2,1)} %get-tuple-element.32), channel_id=1, source_target_pairs={{0,16},{4,20},{8,24},{12,28},{16,0},{20,4},{24,8},{28,12},{1,17},{... | collective-permute-start | bytes 1179656 | tf_op jit(solution)/shard_map/ppermute | solution.py:279
  92.1 19.0 %copy-start.1 = (bf16[1536,128]{1,0:T(8,128)(2,1)}, bf16[1536,128]{1,0:T(8,128)(2,1)S(1)}, u32[]{:S(2)}) copy-start(bf16[1536,128]{1,0:T(8,128)(2,1)S(1)} %collective-permute-done) | copy-start | bytes 1179652
  92.1 19.0 %collective-permute-start.6 = (bf16[1536,128]{1,0:T(8,128)(2,1)}, bf16[1536,128]{1,0:T(8,128)(2,1)S(1)}, u32[]{:S(2)}, u32[]{:S(2)}) collective-permute-start(bf16[1536,128]{1,0:T(8,128)(2,1)} %get-tuple-element.33), channel_id=1, source_target_pairs={{0,24},{4,28},{8,0},{12,4},{16,8},{20,12},{24,16},{28,20},{1,25},{... | collective-permute-start | bytes 1179656 | tf_op jit(solution)/shard_map/ppermute | solution.py:279
  94.8 16.3 %copy-start.2 = (bf16[1536,128]{1,0:T(8,128)(2,1)}, bf16[1536,128]{1,0:T(8,128)(2,1)S(1)}, u32[]{:S(2)}) copy-start(bf16[1536,128]{1,0:T(8,128)(2,1)S(1)} %collective-permute-done.1) | copy-start | bytes 1179652
  94.8 16.3 %copy-start.3 = (bf16[1536,128]{1,0:T(8,128)(2,1)}, bf16[1536,128]{1,0:T(8,128)(2,1)S(1)}, u32[]{:S(2)}) copy-start(bf16[1536,128]{1,0:T(8,128)(2,1)S(1)} %collective-permute-done.2) | copy-start | bytes 1179652
  110.5 0.7 copy-start.4
  110.5 0.9 copy-start.5
  111.1 0.8 copy-start.6
  169.0 32.6 %all-to-all-start.1 = ((bf16[32,96,128]{2,1,0:T(8,128)(2,1)}), bf16[32,96,128]{2,1,0:T(8,128)(2,1)S(1)}, u32[]{:S(2)}, u32[]{:S(2)}) async-start(bf16[32,96,128]{2,1,0:T(8,128)(2,1)} %bitcast.46), calls=%async_computation.2 | async-start | bytes 1572864 | tf_op jit(solution)/shard_map/all_to_all | solution.py:287
  201.6 0.9 copy-start
Sparse Core Ops, SparseCore 0:
  43.9 39.8 all-gather.1
  125.8 43.1 reduce-scatter.1

commit v3 on v2

--- a/solution.py
+++ b/solution.py
@@ -135,8 +135,12 @@
             acc[...] += part
 
 
+def far_piece(far, p, k):
+    return far[k][0] if p == 0 else far[N_X + k][p - 1]
+
+
 def expert_kernel(where_ref, rows_ref, fresh_ref, *refs):
-    near, far, refs = refs[:N_X], refs[N_X : 2 * N_X], refs[2 * N_X :]
+    near, far, refs = refs[:N_X], refs[N_X : 3 * N_X], refs[3 * N_X :]
     hidden_ref, both_ref, out_ref, held, gate_acc, up_acc, down_acc = refs
     step = pl.program_id(0)
     z, other_z = where_ref[1], 1 - where_ref[1]
@@ -146,7 +150,7 @@
         @pl.when(step == k)
         def _():
             for p in range(3):
-                for side, (at, piece) in enumerate(((z, near[k][p]), (other_z, far[k][p]))):
+                for side, (at, piece) in enumerate(((z, near[k][p]), (other_z, far_piece(far, p, k)))):
                     held[k, p, side * SLAB : (side + 1) * SLAB, :] = jnp.concatenate(
                         [piece, fresh_ref[p, 0, at]], axis=1
                     )
@@ -187,7 +191,7 @@
 
 
 def update_kernel(where_ref, rows_ref, fresh_ref, *refs):
-    near, far, refs = refs[:N_X], refs[N_X : 2 * N_X], refs[2 * N_X :]
+    near, far, refs = refs[:N_X], refs[N_X : 3 * N_X], refs[3 * N_X :]
     hidden_ref, both_ref, marks_ref, new_ref, order, held = refs
     step = pl.program_id(0)
 
@@ -201,7 +205,7 @@
         def _():
             for p in range(3):
                 held[p, 0] = near[k][p]
-                held[p, 1] = far[k][p]
+                held[p, 1] = far_piece(far, p, k)
 
     for side, z in enumerate((where_ref[1], 1 - where_ref[1])):
         pair = dot_tn(slab_rows(rows_ref, z, 0), both_ref[...])
@@ -299,14 +303,21 @@
 
     ids, weights = expert_ids.T, gates.T
     slots = call(dispatch_kernel, sds((N_E, N_Q, 2 * CAP, LANE)))(ids, weights, tokens, cotangent)
-    mine = exchange(slots.reshape(2 * PIECE, LANE))
-
+    near = pack(dense_ffn.reshape(3 * SLAB, COLS))
+    mine = exchange(after(slots.reshape(2 * PIECE, LANE), *near))
+
+    near = to_holders(near)
+    rest = dense_ffn[1:].reshape(2 * SLAB, COLS)
+    mine, near, gate, rest = lax.optimization_barrier(
+        (mine, near, other_side(dense_ffn[0]), rest)
+    )
     rows = lax.all_gather(mine, "dp", axis=0, tiled=True).reshape((N_DP,) + VIEW)
-    dense = dense_ffn.reshape(3 * SLAB, COLS)
-    mine, dense, near = lax.optimization_barrier((mine, dense, pack(dense)))
-    near = to_holders(near)
-    far = to_holders(pack(other_side(dense)))
-    pieces = [p.reshape(3, SLAB, HALF) for p in near + far]
+    rest = other_side(rest)
+    gate, rest = lax.optimization_barrier((to_holders(pack(gate)), rest))
+    rest = to_holders(pack(rest))
+    pieces = [
+        p.reshape(n, SLAB, HALF) for n, part in ((3, near), (1, gate), (2, rest)) for p in part
+    ]
     piece_specs = [whole_spec(p.shape) for p in pieces]
     fresh = redraw.reshape(3, N_X, 2, SLAB, HALF)
 

time: 212 us -> 206 us (0.972)
  blocking collectives: 34.5 us -> 0 us
  starting transfers between devices: 20.7 us -> 45.5 us
  local copies, waits for them, and re-layouts: 2.5 us -> 5.44 us
    all_to_all x1 -> x0, blocking collectives: 34.5 us -> none  [exchange(): lax.all_to_all(rows, ('expert', 'mp'), split_axis=0, concat_axis=0, tiled...]
    all_to_all x1 -> x2, starting transfers between devices: 10 us -> 21.2 us  [exchange(): lax.all_to_all(rows, ('expert', 'mp'), split_axis=0, concat_axis=0, tiled...]
    ppermute x6 -> x9, starting transfers between devices: 9.76 us -> 18.1 us  [along_x(): lax.ppermute(piece, 'expert', [(e, (e // 2 + k) % N_X * 2 + e % 2) for e...]
    ppermute x1 -> x2, starting transfers between devices: 0.83 us -> 6.17 us  [other_side(): return lax.ppermute(slab, 'expert', [(e, e ^ 1) for e in range(N_E)])]
    pallas_call x2 -> x3, Pallas kernels: 6.44 us -> 8.24 us  [pack(): call(pack_kernel, [sds((rows, HALF))] * N_X, in_specs=[SMEM, pl.BlockSpec...]
    ppermute x6 -> x9, waiting for transfers between devices: 16.3 us -> 14.6 us  [along_x(): lax.ppermute(piece, 'expert', [(e, (e // 2 + k) % N_X * 2 + e % 2) for e...]
    ppermute x1 -> x2, waiting for transfers between devices: 32.4 us -> 33.1 us  [other_side(): return lax.ppermute(slab, 'expert', [(e, e ^ 1) for e in range(N_E)])]
    all_to_all x1 -> x2, waiting for transfers between devices: 10.4 us -> 10.4 us  [exchange(): lax.all_to_all(rows, ('expert', 'mp'), split_axis=0, concat_axis=0, tiled...]
  transfers between devices with their start and end apart: 10 -> 15, of which waited for: 5 -> 9; matrix products, arithmetic and copies ran while one was open for 0% -> 1% of each run, Pallas kernels for 9% -> 8%
where the time goes in v3:
time: 206 us; the launch traced here: 205 us
  waiting for transfers between devices  101 us (49%)
  starting transfers between devices  45.5 us (22%)
  Pallas kernels  38.8 us (19%)
  between operations  14.2 us (7%)
  local copies, waits for them, and re-layouts  5.44 us (3%)
    reduce_scatter x1, waiting for transfers between devices, on_device(): lax.psum_scatter(sums.reshape(N_DP * 2 * PIECE, LANE), 'dp', scatter_dime...  42.6 us
    ppermute x2, waiting for transfers between devices, other_side(): return lax.ppermute(slab, 'expert', [(e, e ^ 1) for e in range(N_E)])  33.1 us
    all_to_all x2, starting transfers between devices, exchange(): lax.all_to_all(rows, ('expert', 'mp'), split_axis=0, concat_axis=0, tiled...  21.2 us
    ppermute x9, starting transfers between devices, along_x(): lax.ppermute(piece, 'expert', [(e, (e // 2 + k) % N_X * 2 + e % 2) for e...  18.1 us
    ppermute x9, waiting for transfers between devices, along_x(): lax.ppermute(piece, 'expert', [(e, (e // 2 + k) % N_X * 2 + e % 2) for e...  14.6 us
    pallas_call x1, Pallas kernels, on_device(): call(expert_kernel, acts + [sds((N_DP,) + VIEW)], prefetch=1, scratch=[pl...  13.9 us
    pallas_call x1, Pallas kernels, on_device(): call(update_kernel, sds((3, N_X, 2, SLAB, COLS)), prefetch=1, scratch=[pl...  12.2 us
    all_to_all x2, waiting for transfers between devices, exchange(): lax.all_to_all(rows, ('expert', 'mp'), split_axis=0, concat_axis=0, tiled...  10.4 us
  transfers between devices with their start and end apart: 15, of which 9 were waited for; matrix products, arithmetic and copies ran while one was open for 1% of the time, Pallas kernels for 8%

profile of v3, /device:TPU:32, one launch (start us, length us, event | category | flops | bytes accessed | tf_op | source)
XLA Modules:
  0.0 205.4 jit_solution(16100194219213604001)
XLA Ops:
  7.2 0.6 pad_add_fusion.where_ref
  7.8 3.2 %shard_map.95 = (bf16[1536,128]{1,0:T(8,128)(2,1)}, bf16[1536,128]{1,0:T(8,128)(2,1)}, bf16[1536,128]{1,0:T(8,128)(2,1)}, bf16[1536,128]{1,0:T(8,128)(2,1)}) custom-call(s32[2]{0:T(128)} %pad_add_fusion.where_ref, s32[8,256]{1,0:T(8,128)} %refs_14_.1, bf16[1536,256]{1,0:T(8,128)(2,1)} %bitcast.38), custom_call_target="tpu_custom_call" | custom-call | flops 1024 | bytes 1024 | tf_op jit(solution)/shard_map/pallas_call | solution.py:295
  11.0 2.1 %shard_map.94 = bf16[8,4,96,128]{3,2,1,0:T(8,128)(2,1)} custom-call(s32[2,128]{1,0:T(2,128)} %bitcast.65, f32[2,128]{1,0:T(2,128)} %bitcast.67, bf16[128,128]{1,0:T(8,128)(2,1)} %tok_ref.1, bf16[128,128]{1,0:T(8,128)(2,1)} %cot_ref.1), custom_call_target="tpu_custom_call" | custom-call | flops 1024 | bytes 1024 | tf_op jit(solution)/shard_map/pallas_call | solution.py:305
  13.1 11.2 %all-to-all-start = ((bf16[32,96,128]{2,1,0:T(8,128)(2,1)}), bf16[32,96,128]{2,1,0:T(8,128)(2,1)S(1)}, u32[]{:S(2)}, u32[]{:S(2)}) async-start(bf16[32,96,128]{2,1,0:T(8,128)(2,1)} %bitcast.36), calls=%async_computation | async-start | bytes 1572864 | tf_op jit(solution)/shard_map/all_to_all | solution.py:291
  24.3 0.0 all-gather.2.cloned.1.call-start
  24.3 1.5 collective-permute-start
  25.9 2.7 %collective-permute-start.1 = (bf16[1536,128]{1,0:T(8,128)(2,1)}, bf16[1536,128]{1,0:T(8,128)(2,1)S(1)}, u32[]{:S(2)}, u32[]{:S(2)}) collective-permute-start(bf16[1536,128]{1,0:T(8,128)(2,1)} %get-tuple-element.35), channel_id=1, source_target_pairs={{0,16},{4,20},{8,24},{12,28},{16,0},{20,4},{24,8},{28,12},{1,17},{... | collective-permute-start | bytes 1179656 | tf_op jit(solution)/shard_map/ppermute | solution.py:283
  28.6 1.4 collective-permute-start.2
  30.0 1.0 slice_bitcast_fusion
  31.0 4.6 %collective-permute-start.3 = (bf16[512,256]{1,0:T(8,128)(2,1)S(1)}, bf16[512,256]{1,0:T(8,128)(2,1)S(1)}, u32[]{:S(2)}, u32[]{:S(2)}) collective-permute-start(bf16[512,256]{1,0:T(8,128)(2,1)S(1)} %slice_bitcast_fusion), channel_id=1, source_target_pairs={{0,4},{4,0},{8,12},{12,8},{16,20},{20,16},{24,28},{28,24},{1,5},{5... | collective-permute-start | bytes 786440 | tf_op jit(solution)/shard_map/ppermute | solution.py:288
  35.5 1.1 slice.7
  36.6 20.4 %collective-permute-done.3.dense_ref = bf16[512,256]{1,0:T(8,128)(2,1)S(1)} collective-permute-done((bf16[512,256]{1,0:T(8,128)(2,1)S(1)}, bf16[512,256]{1,0:T(8,128)(2,1)S(1)}, u32[]{:S(2)}, u32[]{:S(2)}) %collective-permute-start.3) | collective-permute-done | bytes 262176 | tf_op jit(solution)/shard_map/ppermute | solution.py:288
  57.1 0.0 copy-start.12
  57.1 0.0 collective-permute-done
  57.1 0.0 copy-start.2
  57.1 0.0 collective-permute-done.1
  57.1 0.0 copy-start.3
  57.1 0.0 collective-permute-done.2
  57.1 0.0 copy-start.4
  57.1 0.0 all-to-all-done
  57.1 0.0 copy-start
  57.1 1.0 copy-done
  58.1 0.0 all-gather.2.cloned.1.call-update
  58.1 0.0 reduce-scatter.2.cloned.1.call-start
  58.1 1.6 collective-permute-start.7
  59.7 0.0 copy-done.12
  59.7 2.3 %shard_map.96 = (bf16[512,128]{1,0:T(8,128)(2,1)}, bf16[512,128]{1,0:T(8,128)(2,1)}, bf16[512,128]{1,0:T(8,128)(2,1)}, bf16[512,128]{1,0:T(8,128)(2,1)}) custom-call(s32[2]{0:T(128)} %pad_add_fusion.where_ref, s32[8,256]{1,0:T(8,128)} %refs_14_.1, bf16[512,256]{1,0:T(8,128)(2,1)} %copy-done.12), custom_call_target="tpu_custom_call" | custom-call | flops 1024 | bytes 1024 | tf_op jit(solution)/shard_map/pallas_call | solution.py:295
  62.0 1.5 collective-permute-start.4
  63.5 2.7 %collective-permute-start.5 = (bf16[512,128]{1,0:T(8,128)(2,1)}, bf16[512,128]{1,0:T(8,128)(2,1)S(1)}, u32[]{:S(2)}, u32[]{:S(2)}) collective-permute-start(bf16[512,128]{1,0:T(8,128)(2,1)} %get-tuple-element.46), channel_id=1, source_target_pairs={{0,16},{4,20},{8,24},{12,28},{16,0},{20,4},{24,8},{28,12},{1,17},{... | collective-permute-start | bytes 393224 | tf_op jit(solution)/shard_map/ppermute | solution.py:283
  66.2 1.4 collective-permute-start.6
  67.6 2.2 %collective-permute-done.4 = bf16[512,128]{1,0:T(8,128)(2,1)S(1)} collective-permute-done((bf16[512,128]{1,0:T(8,128)(2,1)}, bf16[512,128]{1,0:T(8,128)(2,1)S(1)}, u32[]{:S(2)}, u32[]{:S(2)}) %collective-permute-start.4) | collective-permute-done | bytes 131104 | tf_op jit(solution)/shard_map/ppermute | solution.py:283
  69.8 0.0 copy-start.9
  69.8 1.6 collective-permute-done.5
  71.4 0.0 copy-start.10
  71.4 0.1 collective-permute-done.6
  71.5 0.0 copy-start.11
  71.5 12.6 %collective-permute-done.7.dense_ref = bf16[1024,256]{1,0:T(8,128)(2,1)S(1)} collective-permute-done((bf16[1024,256]{1,0:T(8,128)(2,1)S(1)}, bf16[1024,256]{1,0:T(8,128)(2,1)S(1)}, u32[]{:S(2)}, u32[]{:S(2)}) %collective-permute-start.7) | collective-permute-done | bytes 524320 | tf_op jit(solution)/shard_map/ppermute | solution.py:288
  84.1 0.8 copy-done.8
  84.9 2.7 %shard_map.97 = (bf16[1024,128]{1,0:T(8,128)(2,1)}, bf16[1024,128]{1,0:T(8,128)(2,1)}, bf16[1024,128]{1,0:T(8,128)(2,1)}, bf16[1024,128]{1,0:T(8,128)(2,1)}) custom-call(s32[2]{0:T(128)} %pad_add_fusion.where_ref, s32[8,256]{1,0:T(8,128)} %refs_14_.1, bf16[1024,256]{1,0:T(8,128)(2,1)} %copy-done.8), custom_call_target="tpu_custom_call" | custom-call | flops 1024 | bytes 1024 | tf_op jit(solution)/shard_map/pallas_call | solution.py:295
  87.6 2.9 %collective-permute-start.8 = (bf16[1024,128]{1,0:T(8,128)(2,1)}, bf16[1024,128]{1,0:T(8,128)(2,1)S(1)}, u32[]{:S(2)}, u32[]{:S(2)}) collective-permute-start(bf16[1024,128]{1,0:T(8,128)(2,1)} %get-tuple-element.55), channel_id=1, source_target_pairs={{0,8},{4,12},{8,16},{12,20},{16,24},{20,28},{24,0},{28,4},{1,9},{5... | collective-permute-start | bytes 786440 | tf_op jit(solution)/shard_map/ppermute | solution.py:283
  90.5 2.7 %collective-permute-start.9 = (bf16[1024,128]{1,0:T(8,128)(2,1)}, bf16[1024,128]{1,0:T(8,128)(2,1)S(1)}, u32[]{:S(2)}, u32[]{:S(2)}) collective-permute-start(bf16[1024,128]{1,0:T(8,128)(2,1)} %get-tuple-element.56), channel_id=1, source_target_pairs={{0,16},{4,20},{8,24},{12,28},{16,0},{20,4},{24,8},{28,12},{1,17},{... | collective-permute-start | bytes 786440 | tf_op jit(solution)/shard_map/ppermute | solution.py:283
  93.2 1.3 collective-permute-start.10
  94.4 4.0 %collective-permute-done.8 = bf16[1024,128]{1,0:T(8,128)(2,1)S(1)} collective-permute-done((bf16[1024,128]{1,0:T(8,128)(2,1)}, bf16[1024,128]{1,0:T(8,128)(2,1)S(1)}, u32[]{:S(2)}, u32[]{:S(2)}) %collective-permute-start.8) | collective-permute-done | bytes 262176 | tf_op jit(solution)/shard_map/ppermute | solution.py:283
  98.4 0.0 copy-start.5
  98.4 6.8 %collective-permute-done.9 = bf16[1024,128]{1,0:T(8,128)(2,1)S(1)} collective-permute-done((bf16[1024,128]{1,0:T(8,128)(2,1)}, bf16[1024,128]{1,0:T(8,128)(2,1)S(1)}, u32[]{:S(2)}, u32[]{:S(2)}) %collective-permute-start.9) | collective-permute-done | bytes 262176 | tf_op jit(solution)/shard_map/ppermute | solution.py:283
  105.2 0.0 collective-permute-done.10
  105.2 0.0 all-gather.2.cloned.1.call-done
  105.2 0.0 copy-done.2
  105.2 0.0 copy-done.3
  105.2 0.0 copy-done.4
  105.2 0.0 copy-done.9
  105.3 0.0 copy-done.10
  105.3 0.0 copy-done.11
  105.3 0.0 copy-done.5
  105.3 0.6 copy-done.6
  105.9 0.1 copy-done.7
  106.0 13.9 %shard_map.98 = (bf16[384,256]{1,0:T(8,128)(2,1)}, bf16[384,512]{1,0:T(8,128)(2,1)}, bf16[8,4,2,4,96,128]{5,4,3,2,1,0:T(8,128)(2,1)}) custom-call(s32[2]{0:T(128)} %pad_add_fusion.where_ref, bf16[8,4,2,4,96,128]{5,4,3,2,1,0:T(8,128)(2,1)} %bitcast.29, bf16[3,4,2,512,128]{4,3,2,1,0:T(8,128)(2,1)} %bitcast.31, bf16[3,512,128]{2,1,0:T(8,128)(2,1)} %bitcast.39, ...), custom_call_target="tpu_custom_call" | custom-call | flops 1024 | bytes 1024 | tf_op jit(solution)/shard_map/pallas_call | solution.py:326
  119.9 0.0 reduce-scatter.2.cloned.1.call-update
  119.9 42.6 %reduce-scatter.2.cloned.1.call-done = bf16[3072,128]{1,0:T(8,128)(2,1)} async-done(((bf16[24576,128]{1,0:T(8,128)(2,1)}), bf16[3072,128]{1,0:T(8,128)(2,1)}) %reduce-scatter.2.cloned.1.call-update) | async-done | bytes 786448 | tf_op jit(solution)/shard_map/reduce_scatter | solution.py:336
  162.5 10.0 %all-to-all-start.1 = ((bf16[32,96,128]{2,1,0:T(8,128)(2,1)}), bf16[32,96,128]{2,1,0:T(8,128)(2,1)S(1)}, u32[]{:S(2)}, u32[]{:S(2)}) async-start(bf16[32,96,128]{2,1,0:T(8,128)(2,1)} %bitcast.55), calls=%async_computation.2 | async-start | bytes 1572864 | tf_op jit(solution)/shard_map/all_to_all | solution.py:291
  172.6 12.2 %shard_map.100 = bf16[3,4,2,512,256]{4,3,2,1,0:T(8,128)(2,1)} custom-call(s32[2]{0:T(128)} %pad_add_fusion.where_ref, bf16[8,4,2,4,96,128]{5,4,3,2,1,0:T(8,128)(2,1)} %bitcast.30, bf16[3,4,2,512,128]{4,3,2,1,0:T(8,128)(2,1)} %bitcast.32, bf16[3,512,128]{2,1,0:T(8,128)(2,1)} %bitcast.40, bf16[3,512,128]{2,1,0:T(8,128)(2,1)} %bitcast.42, ...), custom_call_target="tpu_custom_call" | custom-call | flops 1024 | bytes 1024 | tf_op jit(solution)/shard_map/pallas_call | solution.py:339
  184.7 10.4 %all-to-all-done.1 = bf16[32,96,128]{2,1,0:T(8,128)(2,1)S(1)} async-done(((bf16[32,96,128]{2,1,0:T(8,128)(2,1)}), bf16[32,96,128]{2,1,0:T(8,128)(2,1)S(1)}, u32[]{:S(2)}, u32[]{:S(2)}) %all-to-all-start.1) | async-done | bytes 786464 | tf_op jit(solution)/shard_map/all_to_all | solution.py:291
  195.2 0.9 copy-done.1
  196.1 2.5 %shard_map.99 = (bf16[128,128]{1,0:T(8,128)(2,1)}, bf16[128,128]{1,0:T(8,128)(2,1)}) custom-call(s32[2,128]{1,0:T(2,128)} %bitcast.66, f32[2,128]{1,0:T(2,128)} %bitcast.68, bf16[8,4,96,128]{3,2,1,0:T(8,128)(2,1)} %bitcast.37), custom_call_target="tpu_custom_call" | custom-call | flops 1024 | bytes 1024 | tf_op jit(solution)/shard_map/pallas_call | solution.py:354
  (4 shorter events, 0.0 us)
Async XLA Ops:
  13.1 44.0 %all-to-all-start = ((bf16[32,96,128]{2,1,0:T(8,128)(2,1)}), bf16[32,96,128]{2,1,0:T(8,128)(2,1)S(1)}, u32[]{:S(2)}, u32[]{:S(2)}) async-start(bf16[32,96,128]{2,1,0:T(8,128)(2,1)} %bitcast.36), calls=%async_computation | async-start | bytes 1572864 | tf_op jit(solution)/shard_map/all_to_all | solution.py:291
  24.3 80.9 %all-gather.2.cloned.1.call-start = ((), (), s32[]{:S(2)}) async-start(), calls=%async_computation.3 | async-start | bytes 7077888 | tf_op jit(solution)/shard_map/all_gather | solution.py:314
  24.3 32.7 %collective-permute-start = (bf16[1536,128]{1,0:T(8,128)(2,1)}, bf16[1536,128]{1,0:T(8,128)(2,1)S(1)}, u32[]{:S(2)}, u32[]{:S(2)}) collective-permute-start(bf16[1536,128]{1,0:T(8,128)(2,1)} %get-tuple-element.34), channel_id=1, source_target_pairs={{0,8},{4,12},{8,16},{12,20},{16,24},{20,28},{24,0},{28,4},{1,9},{5... | collective-permute-start | bytes 1179656 | tf_op jit(solution)/shard_map/ppermute | solution.py:283
  25.9 31.2 %collective-permute-start.1 = (bf16[1536,128]{1,0:T(8,128)(2,1)}, bf16[1536,128]{1,0:T(8,128)(2,1)S(1)}, u32[]{:S(2)}, u32[]{:S(2)}) collective-permute-start(bf16[1536,128]{1,0:T(8,128)(2,1)} %get-tuple-element.35), channel_id=1, source_target_pairs={{0,16},{4,20},{8,24},{12,28},{16,0},{20,4},{24,8},{28,12},{1,17},{... | collective-permute-start | bytes 1179656 | tf_op jit(solution)/shard_map/ppermute | solution.py:283
  28.6 28.5 %collective-permute-start.2 = (bf16[1536,128]{1,0:T(8,128)(2,1)}, bf16[1536,128]{1,0:T(8,128)(2,1)S(1)}, u32[]{:S(2)}, u32[]{:S(2)}) collective-permute-start(bf16[1536,128]{1,0:T(8,128)(2,1)} %get-tuple-element.36), channel_id=1, source_target_pairs={{0,24},{4,28},{8,0},{12,4},{16,8},{20,12},{24,16},{28,20},{1,25},{... | collective-permute-start | bytes 1179656 | tf_op jit(solution)/shard_map/ppermute | solution.py:283
  31.0 26.1 %collective-permute-start.3 = (bf16[512,256]{1,0:T(8,128)(2,1)S(1)}, bf16[512,256]{1,0:T(8,128)(2,1)S(1)}, u32[]{:S(2)}, u32[]{:S(2)}) collective-permute-start(bf16[512,256]{1,0:T(8,128)(2,1)S(1)} %slice_bitcast_fusion), channel_id=1, source_target_pairs={{0,4},{4,0},{8,12},{12,8},{16,20},{20,16},{24,28},{28,24},{1,5},{5... | collective-permute-start | bytes 786440 | tf_op jit(solution)/shard_map/ppermute | solution.py:288
  57.1 2.7 %copy-start.12 = (bf16[512,256]{1,0:T(8,128)(2,1)}, bf16[512,256]{1,0:T(8,128)(2,1)S(1)}, u32[]{:S(2)}) copy-start(bf16[512,256]{1,0:T(8,128)(2,1)S(1)} %collective-permute-done.3.dense_ref) | copy-start | bytes 786436
  57.1 48.2 %copy-start.2 = (bf16[1536,128]{1,0:T(8,128)(2,1)}, bf16[1536,128]{1,0:T(8,128)(2,1)S(1)}, u32[]{:S(2)}) copy-start(bf16[1536,128]{1,0:T(8,128)(2,1)S(1)} %collective-permute-done) | copy-start | bytes 1179652
  57.1 48.2 %copy-start.3 = (bf16[1536,128]{1,0:T(8,128)(2,1)}, bf16[1536,128]{1,0:T(8,128)(2,1)S(1)}, u32[]{:S(2)}) copy-start(bf16[1536,128]{1,0:T(8,128)(2,1)S(1)} %collective-permute-done.1) | copy-start | bytes 1179652
  57.1 48.2 %copy-start.4 = (bf16[1536,128]{1,0:T(8,128)(2,1)}, bf16[1536,128]{1,0:T(8,128)(2,1)S(1)}, u32[]{:S(2)}) copy-start(bf16[1536,128]{1,0:T(8,128)(2,1)S(1)} %collective-permute-done.2) | copy-start | bytes 1179652
  57.1 1.0 copy-start
  58.1 104.4 %reduce-scatter.2.cloned.1.call-start = ((), (), s32[]{:S(2)}) async-start(), calls=%async_computation.4 | async-start | bytes 7077888 | tf_op jit(solution)/shard_map/reduce_scatter | solution.py:336
  58.1 25.9 %collective-permute-start.7 = (bf16[1024,256]{1,0:T(8,128)(2,1)S(1)}, bf16[1024,256]{1,0:T(8,128)(2,1)S(1)}, u32[]{:S(2)}, u32[]{:S(2)}) collective-permute-start(bf16[1024,256]{1,0:T(8,128)(2,1)S(1)} %bitcast.56), channel_id=1, source_target_pairs={{0,4},{4,0},{8,12},{12,8},{16,20},{20,16},{24,28},{28,24},{1,5},{5... | collective-permute-start | bytes 1572872 | tf_op jit(solution)/shard_map/ppermute | solution.py:288
  62.0 7.8 %collective-permute-start.4 = (bf16[512,128]{1,0:T(8,128)(2,1)}, bf16[512,128]{1,0:T(8,128)(2,1)S(1)}, u32[]{:S(2)}, u32[]{:S(2)}) collective-permute-start(bf16[512,128]{1,0:T(8,128)(2,1)} %get-tuple-element.45), channel_id=1, source_target_pairs={{0,8},{4,12},{8,16},{12,20},{16,24},{20,28},{24,0},{28,4},{1,9},{5... | collective-permute-start | bytes 393224 | tf_op jit(solution)/shard_map/ppermute | solution.py:283
  63.5 7.9 %collective-permute-start.5 = (bf16[512,128]{1,0:T(8,128)(2,1)}, bf16[512,128]{1,0:T(8,128)(2,1)S(1)}, u32[]{:S(2)}, u32[]{:S(2)}) collective-permute-start(bf16[512,128]{1,0:T(8,128)(2,1)} %get-tuple-element.46), channel_id=1, source_target_pairs={{0,16},{4,20},{8,24},{12,28},{16,0},{20,4},{24,8},{28,12},{1,17},{... | collective-permute-start | bytes 393224 | tf_op jit(solution)/shard_map/ppermute | solution.py:283
  66.2 5.2 %collective-permute-start.6 = (bf16[512,128]{1,0:T(8,128)(2,1)}, bf16[512,128]{1,0:T(8,128)(2,1)S(1)}, u32[]{:S(2)}, u32[]{:S(2)}) collective-permute-start(bf16[512,128]{1,0:T(8,128)(2,1)} %get-tuple-element.47), channel_id=1, source_target_pairs={{0,24},{4,28},{8,0},{12,4},{16,8},{20,12},{24,16},{28,20},{1,25},{... | collective-permute-start | bytes 393224 | tf_op jit(solution)/shard_map/ppermute | solution.py:283
  69.8 35.4 %copy-start.9 = (bf16[512,128]{1,0:T(8,128)(2,1)}, bf16[512,128]{1,0:T(8,128)(2,1)S(1)}, u32[]{:S(2)}) copy-start(bf16[512,128]{1,0:T(8,128)(2,1)S(1)} %collective-permute-done.4) | copy-start | bytes 393220
  71.4 33.9 %copy-start.10 = (bf16[512,128]{1,0:T(8,128)(2,1)}, bf16[512,128]{1,0:T(8,128)(2,1)S(1)}, u32[]{:S(2)}) copy-start(bf16[512,128]{1,0:T(8,128)(2,1)S(1)} %collective-permute-done.5) | copy-start | bytes 393220
  71.5 33.8 %copy-start.11 = (bf16[512,128]{1,0:T(8,128)(2,1)}, bf16[512,128]{1,0:T(8,128)(2,1)S(1)}, u32[]{:S(2)}) copy-start(bf16[512,128]{1,0:T(8,128)(2,1)S(1)} %collective-permute-done.6) | copy-start | bytes 393220
  84.1 0.8 copy-start.8
  87.6 10.7 %collective-permute-start.8 = (bf16[1024,128]{1,0:T(8,128)(2,1)}, bf16[1024,128]{1,0:T(8,128)(2,1)S(1)}, u32[]{:S(2)}, u32[]{:S(2)}) collective-permute-start(bf16[1024,128]{1,0:T(8,128)(2,1)} %get-tuple-element.55), channel_id=1, source_target_pairs={{0,8},{4,12},{8,16},{12,20},{16,24},{20,28},{24,0},{28,4},{1,9},{5... | collective-permute-start | bytes 786440 | tf_op jit(solution)/shard_map/ppermute | solution.py:283
  90.5 14.7 %collective-permute-start.9 = (bf16[1024,128]{1,0:T(8,128)(2,1)}, bf16[1024,128]{1,0:T(8,128)(2,1)S(1)}, u32[]{:S(2)}, u32[]{:S(2)}) collective-permute-start(bf16[1024,128]{1,0:T(8,128)(2,1)} %get-tuple-element.56), channel_id=1, source_target_pairs={{0,16},{4,20},{8,24},{12,28},{16,0},{20,4},{24,8},{28,12},{1,17},{... | collective-permute-start | bytes 786440 | tf_op jit(solution)/shard_map/ppermute | solution.py:283
  93.2 12.0 %collective-permute-start.10 = (bf16[1024,128]{1,0:T(8,128)(2,1)}, bf16[1024,128]{1,0:T(8,128)(2,1)S(1)}, u32[]{:S(2)}, u32[]{:S(2)}) collective-permute-start(bf16[1024,128]{1,0:T(8,128)(2,1)} %get-tuple-element.57), channel_id=1, source_target_pairs={{0,24},{4,28},{8,0},{12,4},{16,8},{20,12},{24,16},{28,20},{1,25},{... | collective-permute-start | bytes 786440 | tf_op jit(solution)/shard_map/ppermute | solution.py:283
  98.4 6.9 %copy-start.5 = (bf16[1024,128]{1,0:T(8,128)(2,1)}, bf16[1024,128]{1,0:T(8,128)(2,1)S(1)}, u32[]{:S(2)}) copy-start(bf16[1024,128]{1,0:T(8,128)(2,1)S(1)} %collective-permute-done.8) | copy-start | bytes 786436
  105.2 0.7 copy-start.6
  105.2 0.8 copy-start.7
  162.5 32.7 %all-to-all-start.1 = ((bf16[32,96,128]{2,1,0:T(8,128)(2,1)}), bf16[32,96,128]{2,1,0:T(8,128)(2,1)S(1)}, u32[]{:S(2)}, u32[]{:S(2)}) async-start(bf16[32,96,128]{2,1,0:T(8,128)(2,1)} %bitcast.55), calls=%async_computation.2 | async-start | bytes 1572864 | tf_op jit(solution)/shard_map/all_to_all | solution.py:291
  195.2 0.9 copy-start.1
Sparse Core Ops, SparseCore 0:
  58.2 40.8 all-gather.1
  120.0 42.4 reduce-scatter.1

commit v4 on v2

--- a/solution.py
+++ b/solution.py
@@ -135,8 +135,12 @@
             acc[...] += part
 
 
+def far_piece(far, p, k):
+    return far[p * N_X + k][...]
+
+
 def expert_kernel(where_ref, rows_ref, fresh_ref, *refs):
-    near, far, refs = refs[:N_X], refs[N_X : 2 * N_X], refs[2 * N_X :]
+    near, far, refs = refs[:N_X], refs[N_X : 4 * N_X], refs[4 * N_X :]
     hidden_ref, both_ref, out_ref, held, gate_acc, up_acc, down_acc = refs
     step = pl.program_id(0)
     z, other_z = where_ref[1], 1 - where_ref[1]
@@ -146,7 +150,7 @@
         @pl.when(step == k)
         def _():
             for p in range(3):
-                for side, (at, piece) in enumerate(((z, near[k][p]), (other_z, far[k][p]))):
+                for side, (at, piece) in enumerate(((z, near[k][p]), (other_z, far_piece(far, p, k)))):
                     held[k, p, side * SLAB : (side + 1) * SLAB, :] = jnp.concatenate(
                         [piece, fresh_ref[p, 0, at]], axis=1
                     )
@@ -187,7 +191,7 @@
 
 
 def update_kernel(where_ref, rows_ref, fresh_ref, *refs):
-    near, far, refs = refs[:N_X], refs[N_X : 2 * N_X], refs[2 * N_X :]
+    near, far, refs = refs[:N_X], refs[N_X : 4 * N_X], refs[4 * N_X :]
     hidden_ref, both_ref, marks_ref, new_ref, order, held = refs
     step = pl.program_id(0)
 
@@ -201,7 +205,7 @@
         def _():
             for p in range(3):
                 held[p, 0] = near[k][p]
-                held[p, 1] = far[k][p]
+                held[p, 1] = far_piece(far, p, k)
 
     for side, z in enumerate((where_ref[1], 1 - where_ref[1])):
         pair = dot_tn(slab_rows(rows_ref, z, 0), both_ref[...])
@@ -299,14 +303,19 @@
 
     ids, weights = expert_ids.T, gates.T
     slots = call(dispatch_kernel, sds((N_E, N_Q, 2 * CAP, LANE)))(ids, weights, tokens, cotangent)
+    parts = [dense_ffn[p] for p in range(3)]
+    near = pack(dense_ffn.reshape(3 * SLAB, COLS))
+    slots, parts = lax.optimization_barrier((slots, parts))
     mine = exchange(slots.reshape(2 * PIECE, LANE))
 
+    gate = other_side(parts[0])
+    near = to_holders(near)
+    mine, near, gate, parts = lax.optimization_barrier((mine, near, gate, parts))
     rows = lax.all_gather(mine, "dp", axis=0, tiled=True).reshape((N_DP,) + VIEW)
-    dense = dense_ffn.reshape(3 * SLAB, COLS)
-    mine, dense, near = lax.optimization_barrier((mine, dense, pack(dense)))
-    near = to_holders(near)
-    far = to_holders(pack(other_side(dense)))
-    pieces = [p.reshape(3, SLAB, HALF) for p in near + far]
+    up, down = other_side(parts[1]), other_side(parts[2])
+    gate, up = lax.optimization_barrier((to_holders(pack(gate)), up))
+    up, down = lax.optimization_barrier((to_holders(pack(up)), down))
+    pieces = [p.reshape(3, SLAB, HALF) for p in near] + gate + up + to_holders(pack(down))
     piece_specs = [whole_spec(p.shape) for p in pieces]
     fresh = redraw.reshape(3, N_X, 2, SLAB, HALF)
 

time: 212 us -> 203 us (0.958)
  blocking collectives: 34.5 us -> 0 us
  starting transfers between devices: 20.7 us -> 53.1 us
  waiting for transfers between devices: 102 us -> 89.2 us
  Pallas kernels: 37 us -> 40.9 us
    all_to_all x1 -> x0, blocking collectives: 34.5 us -> none  [exchange(): lax.all_to_all(rows, ('expert', 'mp'), split_axis=0, concat_axis=0, tiled...]
    ppermute x6 -> x12, starting transfers between devices: 9.76 us -> 21 us  [along_x(): lax.ppermute(piece, 'expert', [(e, (e // 2 + k) % N_X * 2 + e % 2) for e...]
    all_to_all x1 -> x2, starting transfers between devices: 10 us -> 21.2 us  [exchange(): lax.all_to_all(rows, ('expert', 'mp'), split_axis=0, concat_axis=0, tiled...]
    ppermute x1 -> x3, starting transfers between devices: 0.83 us -> 10.7 us  [other_side(): return lax.ppermute(slab, 'expert', [(e, e ^ 1) for e in range(N_E)])]
    ppermute x1 -> x3, waiting for transfers between devices: 32.4 us -> 26.3 us  [other_side(): return lax.ppermute(slab, 'expert', [(e, e ^ 1) for e in range(N_E)])]
    ppermute x6 -> x12, waiting for transfers between devices: 16.3 us -> 10.4 us  [along_x(): lax.ppermute(piece, 'expert', [(e, (e // 2 + k) % N_X * 2 + e % 2) for e...]
    pallas_call x2 -> x4, Pallas kernels: 6.44 us -> 10.1 us  [pack(): call(pack_kernel, [sds((rows, HALF))] * N_X, in_specs=[SMEM, pl.BlockSpec...]
    all_to_all x1 -> x2, waiting for transfers between devices: 10.4 us -> 10.3 us  [exchange(): lax.all_to_all(rows, ('expert', 'mp'), split_axis=0, concat_axis=0, tiled...]
  transfers between devices with their start and end apart: 10 -> 19, of which waited for: 5 -> 9; matrix products, arithmetic and copies ran while one was open for 0% -> 0% of each run, Pallas kernels for 9% -> 11%
where the time goes in v4:
time: 203 us; the launch traced here: 202 us
  waiting for transfers between devices  89.2 us (44%)
  starting transfers between devices  53.1 us (26%)
  Pallas kernels  40.9 us (20%)
  between operations  14.2 us (7%)
  local copies, waits for them, and re-layouts  4.32 us (2%)
    reduce_scatter x1, waiting for transfers between devices, on_device(): lax.psum_scatter(sums.reshape(N_DP * 2 * PIECE, LANE), 'dp', scatter_dime...  42.2 us
    ppermute x3, waiting for transfers between devices, other_side(): return lax.ppermute(slab, 'expert', [(e, e ^ 1) for e in range(N_E)])  26.3 us
    all_to_all x2, starting transfers between devices, exchange(): lax.all_to_all(rows, ('expert', 'mp'), split_axis=0, concat_axis=0, tiled...  21.2 us
    ppermute x12, starting transfers between devices, along_x(): lax.ppermute(piece, 'expert', [(e, (e // 2 + k) % N_X * 2 + e % 2) for e...  21 us
    pallas_call x1, Pallas kernels, on_device(): call(expert_kernel, acts + [sds((N_DP,) + VIEW)], prefetch=1, scratch=[pl...  13.9 us
    pallas_call x1, Pallas kernels, on_device(): call(update_kernel, sds((3, N_X, 2, SLAB, COLS)), prefetch=1, scratch=[pl...  12.2 us
    ppermute x3, starting transfers between devices, other_side(): return lax.ppermute(slab, 'expert', [(e, e ^ 1) for e in range(N_E)])  10.7 us
    ppermute x12, waiting for transfers between devices, along_x(): lax.ppermute(piece, 'expert', [(e, (e // 2 + k) % N_X * 2 + e % 2) for e...  10.4 us
  transfers between devices with their start and end apart: 19, of which 9 were waited for; matrix products, arithmetic and copies ran while one was open for 0% of the time, Pallas kernels for 11%

profile of v4, /device:TPU:32, one launch (start us, length us, event | category | flops | bytes accessed | tf_op | source)
XLA Modules:
  0.0 202.3 jit_solution(726329861845597808)
XLA Ops:
  7.2 1.2 slice_bitcast_fusion
  8.3 2.1 %shard_map.94 = bf16[8,4,96,128]{3,2,1,0:T(8,128)(2,1)} custom-call(s32[2,128]{1,0:T(2,128)} %bitcast.42, f32[2,128]{1,0:T(2,128)} %bitcast.44, bf16[128,128]{1,0:T(8,128)(2,1)} %tok_ref.1, bf16[128,128]{1,0:T(8,128)(2,1)} %cot_ref.1), custom_call_target="tpu_custom_call" | custom-call | flops 1024 | bytes 1024 | tf_op jit(solution)/shard_map/pallas_call | solution.py:305
  10.4 11.2 %all-to-all-start = ((bf16[32,96,128]{2,1,0:T(8,128)(2,1)}), bf16[32,96,128]{2,1,0:T(8,128)(2,1)S(1)}, u32[]{:S(2)}, u32[]{:S(2)}) async-start(bf16[32,96,128]{2,1,0:T(8,128)(2,1)} %bitcast.31), calls=%async_computation | async-start | bytes 1572864 | tf_op jit(solution)/shard_map/all_to_all | solution.py:291
  21.6 0.0 all-gather.2.cloned.1.call-start
  21.7 0.7 pad_add_fusion.where_ref
  22.3 3.2 %shard_map.95 = (bf16[1536,128]{1,0:T(8,128)(2,1)}, bf16[1536,128]{1,0:T(8,128)(2,1)}, bf16[1536,128]{1,0:T(8,128)(2,1)}, bf16[1536,128]{1,0:T(8,128)(2,1)}) custom-call(s32[2]{0:T(128)} %pad_add_fusion.where_ref, s32[8,256]{1,0:T(8,128)} %refs_18_.1, bf16[1536,256]{1,0:T(8,128)(2,1)} %bitcast.29), custom_call_target="tpu_custom_call" | custom-call | flops 1024 | bytes 1024 | tf_op jit(solution)/shard_map/pallas_call | solution.py:295
  25.5 1.5 collective-permute-start
  27.0 2.7 %collective-permute-start.1 = (bf16[1536,128]{1,0:T(8,128)(2,1)}, bf16[1536,128]{1,0:T(8,128)(2,1)S(1)}, u32[]{:S(2)}, u32[]{:S(2)}) collective-permute-start(bf16[1536,128]{1,0:T(8,128)(2,1)} %get-tuple-element.49), channel_id=1, source_target_pairs={{0,16},{4,20},{8,24},{12,28},{16,0},{20,4},{24,8},{28,12},{1,17},{... | collective-permute-start | bytes 1179656 | tf_op jit(solution)/shard_map/ppermute | solution.py:283
  29.7 1.4 collective-permute-start.2
  31.1 4.5 %collective-permute-start.3 = (bf16[512,256]{1,0:T(8,128)(2,1)S(1)}, bf16[512,256]{1,0:T(8,128)(2,1)S(1)}, u32[]{:S(2)}, u32[]{:S(2)}) collective-permute-start(bf16[512,256]{1,0:T(8,128)(2,1)S(1)} %get-tuple-element.51), channel_id=1, source_target_pairs={{0,4},{4,0},{8,12},{12,8},{16,20},{20,16},{24,28},{28,24},{1,5},{5... | collective-permute-start | bytes 786440 | tf_op jit(solution)/shard_map/ppermute | solution.py:288
  35.6 18.8 %collective-permute-done.3.dense_ref = bf16[512,256]{1,0:T(8,128)(2,1)S(1)} collective-permute-done((bf16[512,256]{1,0:T(8,128)(2,1)S(1)}, bf16[512,256]{1,0:T(8,128)(2,1)S(1)}, u32[]{:S(2)}, u32[]{:S(2)}) %collective-permute-start.3) | collective-permute-done | bytes 262176 | tf_op jit(solution)/shard_map/ppermute | solution.py:288
  54.4 0.0 collective-permute-done
  54.4 0.0 collective-permute-done.1
  54.4 0.0 copy-start.3
  54.4 0.0 collective-permute-done.2
  54.4 0.0 copy-start.4
  54.4 0.0 all-to-all-done
  54.4 0.0 copy-start
  54.4 0.9 copy-done
  55.4 0.0 all-gather.2.cloned.1.call-update
  55.4 0.0 reduce-scatter.2.cloned.1.call-start
  55.5 1.8 collective-permute-start.7
  57.2 0.0 copy-done.16
  57.2 2.3 %shard_map.96 = (bf16[512,128]{1,0:T(8,128)(2,1)}, bf16[512,128]{1,0:T(8,128)(2,1)}, bf16[512,128]{1,0:T(8,128)(2,1)}, bf16[512,128]{1,0:T(8,128)(2,1)}) custom-call(s32[2]{0:T(128)} %pad_add_fusion.where_ref, s32[8,256]{1,0:T(8,128)} %refs_18_.1, bf16[512,256]{1,0:T(8,128)(2,1)} %copy-done.16), custom_call_target="tpu_custom_call" | custom-call | flops 1024 | bytes 1024 | tf_op jit(solution)/shard_map/pallas_call | solution.py:295
  59.5 1.3 collective-permute-start.4
  60.8 2.7 %collective-permute-start.5 = (bf16[512,128]{1,0:T(8,128)(2,1)}, bf16[512,128]{1,0:T(8,128)(2,1)S(1)}, u32[]{:S(2)}, u32[]{:S(2)}) collective-permute-start(bf16[512,128]{1,0:T(8,128)(2,1)} %get-tuple-element.62), channel_id=1, source_target_pairs={{0,16},{4,20},{8,24},{12,28},{16,0},{20,4},{24,8},{28,12},{1,17},{... | collective-permute-start | bytes 393224 | tf_op jit(solution)/shard_map/ppermute | solution.py:283
  63.5 1.4 collective-permute-start.6
  65.0 4.4 %collective-permute-start.11 = (bf16[512,256]{1,0:T(8,128)(2,1)S(1)}, bf16[512,256]{1,0:T(8,128)(2,1)S(1)}, u32[]{:S(2)}, u32[]{:S(2)}) collective-permute-start(bf16[512,256]{1,0:T(8,128)(2,1)S(1)} %get-tuple-element.74), channel_id=1, source_target_pairs={{0,4},{4,0},{8,12},{12,8},{16,20},{20,16},{24,28},{28,24},{1,5},{5... | collective-permute-start | bytes 786440 | tf_op jit(solution)/shard_map/ppermute | solution.py:288
  69.4 0.0 collective-permute-done.4.refs_5_
  69.4 0.0 collective-permute-done.5.refs_6_
  69.4 0.0 copy-start.6
  69.4 0.0 collective-permute-done.6.refs_7_
  69.4 0.0 copy-start.7
  69.4 7.5 %collective-permute-done.7.dense_ref = bf16[512,256]{1,0:T(8,128)(2,1)S(1)} collective-permute-done((bf16[512,256]{1,0:T(8,128)(2,1)S(1)}, bf16[512,256]{1,0:T(8,128)(2,1)S(1)}, u32[]{:S(2)}, u32[]{:S(2)}) %collective-permute-start.7) | collective-permute-done | bytes 262176 | tf_op jit(solution)/shard_map/ppermute | solution.py:288
  76.9 0.7 copy-done.15
  77.7 2.3 %shard_map.97 = (bf16[512,128]{1,0:T(8,128)(2,1)}, bf16[512,128]{1,0:T(8,128)(2,1)}, bf16[512,128]{1,0:T(8,128)(2,1)}, bf16[512,128]{1,0:T(8,128)(2,1)}) custom-call(s32[2]{0:T(128)} %pad_add_fusion.where_ref, s32[8,256]{1,0:T(8,128)} %refs_18_.1, bf16[512,256]{1,0:T(8,128)(2,1)} %copy-done.15), custom_call_target="tpu_custom_call" | custom-call | flops 1024 | bytes 1024 | tf_op jit(solution)/shard_map/pallas_call | solution.py:295
  80.0 0.0 collective-permute-start.8
  80.0 6.0 %collective-permute-start.9 = (bf16[512,128]{1,0:T(8,128)(2,1)}, bf16[512,128]{1,0:T(8,128)(2,1)S(1)}, u32[]{:S(2)}, u32[]{:S(2)}) collective-permute-start(bf16[512,128]{1,0:T(8,128)(2,1)} %get-tuple-element.72), channel_id=1, source_target_pairs={{0,16},{4,20},{8,24},{12,28},{16,0},{20,4},{24,8},{28,12},{1,17},{... | collective-permute-start | bytes 393224 | tf_op jit(solution)/shard_map/ppermute | solution.py:283
  85.9 0.0 collective-permute-start.10
  85.9 0.0 collective-permute-done.11.dense_ref
  86.0 3.0 %collective-permute-done.8.refs_9_ = bf16[512,128]{1,0:T(8,128)(2,1)S(1)} collective-permute-done((bf16[512,128]{1,0:T(8,128)(2,1)}, bf16[512,128]{1,0:T(8,128)(2,1)S(1)}, u32[]{:S(2)}, u32[]{:S(2)}) %collective-permute-start.8) | collective-permute-done | bytes 131104 | tf_op jit(solution)/shard_map/ppermute | solution.py:283
  89.0 2.3 %collective-permute-done.9.refs_10_ = bf16[512,128]{1,0:T(8,128)(2,1)S(1)} collective-permute-done((bf16[512,128]{1,0:T(8,128)(2,1)}, bf16[512,128]{1,0:T(8,128)(2,1)S(1)}, u32[]{:S(2)}, u32[]{:S(2)}) %collective-permute-start.9) | collective-permute-done | bytes 131104 | tf_op jit(solution)/shard_map/ppermute | solution.py:283
  91.2 0.1 collective-permute-done.10.refs_11_
  91.3 0.0 copy-done.14
  91.3 2.3 %shard_map.98 = (bf16[512,128]{1,0:T(8,128)(2,1)}, bf16[512,128]{1,0:T(8,128)(2,1)}, bf16[512,128]{1,0:T(8,128)(2,1)}, bf16[512,128]{1,0:T(8,128)(2,1)}) custom-call(s32[2]{0:T(128)} %pad_add_fusion.where_ref, s32[8,256]{1,0:T(8,128)} %refs_18_.1, bf16[512,256]{1,0:T(8,128)(2,1)} %copy-done.14), custom_call_target="tpu_custom_call" | custom-call | flops 1024 | bytes 1024 | tf_op jit(solution)/shard_map/pallas_call | solution.py:295
  93.6 0.0 collective-permute-start.12
  93.7 3.5 %collective-permute-start.13 = (bf16[512,128]{1,0:T(8,128)(2,1)}, bf16[512,128]{1,0:T(8,128)(2,1)S(1)}, u32[]{:S(2)}, u32[]{:S(2)}) collective-permute-start(bf16[512,128]{1,0:T(8,128)(2,1)} %get-tuple-element.82), channel_id=1, source_target_pairs={{0,16},{4,20},{8,24},{12,28},{16,0},{20,4},{24,8},{28,12},{1,17},{... | collective-permute-start | bytes 393224 | tf_op jit(solution)/shard_map/ppermute | solution.py:283
  97.1 0.5 collective-permute-start.14
  97.7 4.4 %collective-permute-done.12.refs_13_ = bf16[512,128]{1,0:T(8,128)(2,1)S(1)} collective-permute-done((bf16[512,128]{1,0:T(8,128)(2,1)}, bf16[512,128]{1,0:T(8,128)(2,1)S(1)}, u32[]{:S(2)}, u32[]{:S(2)}) %collective-permute-start.12) | collective-permute-done | bytes 131104 | tf_op jit(solution)/shard_map/ppermute | solution.py:283
  102.1 0.0 collective-permute-done.13.refs_14_
  102.1 0.6 collective-permute-done.14.refs_15_
  102.7 0.0 copy-done.2
  102.7 0.0 copy-done.3
  102.7 0.0 copy-done.4
  102.8 0.0 copy-done.12
  102.8 0.5 copy-done.13
  103.4 13.9 %shard_map.99 = (bf16[384,256]{1,0:T(8,128)(2,1)}, bf16[384,512]{1,0:T(8,128)(2,1)}, bf16[8,4,2,4,96,128]{5,4,3,2,1,0:T(8,128)(2,1)}) custom-call(s32[2]{0:T(128)} %pad_add_fusion.where_ref, bf16[8,4,2,4,96,128]{5,4,3,2,1,0:T(8,128)(2,1)} %bitcast.23, bf16[3,4,2,512,128]{4,3,2,1,0:T(8,128)(2,1)} %bitcast.25, bf16[3,512,128]{2,1,0:T(8,128)(2,1)} %bitcast.33, ...), custom_call_target="tpu_custom_call" | custom-call | flops 1024 | bytes 1024 | tf_op jit(solution)/shard_map/pallas_call | solution.py:324
  117.3 0.0 reduce-scatter.2.cloned.1.call-update
  117.3 42.2 %reduce-scatter.2.cloned.1.call-done = bf16[3072,128]{1,0:T(8,128)(2,1)} async-done(((bf16[24576,128]{1,0:T(8,128)(2,1)}), bf16[3072,128]{1,0:T(8,128)(2,1)}) %reduce-scatter.2.cloned.1.call-update) | async-done | bytes 786448 | tf_op jit(solution)/shard_map/reduce_scatter | solution.py:334
  159.5 10.1 %all-to-all-start.1 = ((bf16[32,96,128]{2,1,0:T(8,128)(2,1)}), bf16[32,96,128]{2,1,0:T(8,128)(2,1)S(1)}, u32[]{:S(2)}, u32[]{:S(2)}) async-start(bf16[32,96,128]{2,1,0:T(8,128)(2,1)} %bitcast.41), calls=%async_computation.2 | async-start | bytes 1572864 | tf_op jit(solution)/shard_map/all_to_all | solution.py:291
  169.5 12.2 %shard_map.101 = bf16[3,4,2,512,256]{4,3,2,1,0:T(8,128)(2,1)} custom-call(s32[2]{0:T(128)} %pad_add_fusion.where_ref, bf16[8,4,2,4,96,128]{5,4,3,2,1,0:T(8,128)(2,1)} %bitcast.24, bf16[3,4,2,512,128]{4,3,2,1,0:T(8,128)(2,1)} %bitcast.26, bf16[3,512,128]{2,1,0:T(8,128)(2,1)} %bitcast.34, bf16[3,512,128]{2,1,0:T(8,128)(2,1)} %bitcast.36, ...), custom_call_target="tpu_custom_call" | custom-call | flops 1024 | bytes 1024 | tf_op jit(solution)/shard_map/pallas_call | solution.py:337
  181.8 10.3 %all-to-all-done.1 = bf16[32,96,128]{2,1,0:T(8,128)(2,1)S(1)} async-done(((bf16[32,96,128]{2,1,0:T(8,128)(2,1)}), bf16[32,96,128]{2,1,0:T(8,128)(2,1)S(1)}, u32[]{:S(2)}, u32[]{:S(2)}) %all-to-all-start.1) | async-done | bytes 786464 | tf_op jit(solution)/shard_map/all_to_all | solution.py:291
  192.1 0.9 copy-done.1
  193.0 2.5 %shard_map.100 = (bf16[128,128]{1,0:T(8,128)(2,1)}, bf16[128,128]{1,0:T(8,128)(2,1)}) custom-call(s32[2,128]{1,0:T(2,128)} %bitcast.43, f32[2,128]{1,0:T(2,128)} %bitcast.45, bf16[8,4,96,128]{3,2,1,0:T(8,128)(2,1)} %bitcast.32), custom_call_target="tpu_custom_call" | custom-call | flops 1024 | bytes 1024 | tf_op jit(solution)/shard_map/pallas_call | solution.py:352
  (20 shorter events, 0.0 us)
Async XLA Ops:
  10.4 44.0 %all-to-all-start = ((bf16[32,96,128]{2,1,0:T(8,128)(2,1)}), bf16[32,96,128]{2,1,0:T(8,128)(2,1)S(1)}, u32[]{:S(2)}, u32[]{:S(2)}) async-start(bf16[32,96,128]{2,1,0:T(8,128)(2,1)} %bitcast.31), calls=%async_computation | async-start | bytes 1572864 | tf_op jit(solution)/shard_map/all_to_all | solution.py:291
  21.6 81.1 %all-gather.2.cloned.1.call-start = ((), (), s32[]{:S(2)}) async-start(), calls=%async_computation.3 | async-start | bytes 7077888 | tf_op jit(solution)/shard_map/all_gather | solution.py:314
  25.5 28.9 %collective-permute-start = (bf16[1536,128]{1,0:T(8,128)(2,1)}, bf16[1536,128]{1,0:T(8,128)(2,1)S(1)}, u32[]{:S(2)}, u32[]{:S(2)}) collective-permute-start(bf16[1536,128]{1,0:T(8,128)(2,1)} %get-tuple-element.48), channel_id=1, source_target_pairs={{0,8},{4,12},{8,16},{12,20},{16,24},{20,28},{24,0},{28,4},{1,9},{5... | collective-permute-start | bytes 1179656 | tf_op jit(solution)/shard_map/ppermute | solution.py:283
  27.0 27.4 %collective-permute-start.1 = (bf16[1536,128]{1,0:T(8,128)(2,1)}, bf16[1536,128]{1,0:T(8,128)(2,1)S(1)}, u32[]{:S(2)}, u32[]{:S(2)}) collective-permute-start(bf16[1536,128]{1,0:T(8,128)(2,1)} %get-tuple-element.49), channel_id=1, source_target_pairs={{0,16},{4,20},{8,24},{12,28},{16,0},{20,4},{24,8},{28,12},{1,17},{... | collective-permute-start | bytes 1179656 | tf_op jit(solution)/shard_map/ppermute | solution.py:283
  29.7 24.7 %collective-permute-start.2 = (bf16[1536,128]{1,0:T(8,128)(2,1)}, bf16[1536,128]{1,0:T(8,128)(2,1)S(1)}, u32[]{:S(2)}, u32[]{:S(2)}) collective-permute-start(bf16[1536,128]{1,0:T(8,128)(2,1)} %get-tuple-element.50), channel_id=1, source_target_pairs={{0,24},{4,28},{8,0},{12,4},{16,8},{20,12},{24,16},{28,20},{1,25},{... | collective-permute-start | bytes 1179656 | tf_op jit(solution)/shard_map/ppermute | solution.py:283
  31.1 23.3 %collective-permute-start.3 = (bf16[512,256]{1,0:T(8,128)(2,1)S(1)}, bf16[512,256]{1,0:T(8,128)(2,1)S(1)}, u32[]{:S(2)}, u32[]{:S(2)}) collective-permute-start(bf16[512,256]{1,0:T(8,128)(2,1)S(1)} %get-tuple-element.51), channel_id=1, source_target_pairs={{0,4},{4,0},{8,12},{12,8},{16,20},{20,16},{24,28},{28,24},{1,5},{5... | collective-permute-start | bytes 786440 | tf_op jit(solution)/shard_map/ppermute | solution.py:288
  54.4 2.8 %copy-start.16 = (bf16[512,256]{1,0:T(8,128)(2,1)}, bf16[512,256]{1,0:T(8,128)(2,1)S(1)}, u32[]{:S(2)}) copy-start(bf16[512,256]{1,0:T(8,128)(2,1)S(1)} %collective-permute-done.3.dense_ref) | copy-start | bytes 786436
  54.4 48.3 %copy-start.2 = (bf16[1536,128]{1,0:T(8,128)(2,1)}, bf16[1536,128]{1,0:T(8,128)(2,1)S(1)}, u32[]{:S(2)}) copy-start(bf16[1536,128]{1,0:T(8,128)(2,1)S(1)} %collective-permute-done) | copy-start | bytes 1179652
  54.4 48.3 %copy-start.3 = (bf16[1536,128]{1,0:T(8,128)(2,1)}, bf16[1536,128]{1,0:T(8,128)(2,1)S(1)}, u32[]{:S(2)}) copy-start(bf16[1536,128]{1,0:T(8,128)(2,1)S(1)} %collective-permute-done.1) | copy-start | bytes 1179652
  54.4 48.3 %copy-start.4 = (bf16[1536,128]{1,0:T(8,128)(2,1)}, bf16[1536,128]{1,0:T(8,128)(2,1)S(1)}, u32[]{:S(2)}) copy-start(bf16[1536,128]{1,0:T(8,128)(2,1)S(1)} %collective-permute-done.2) | copy-start | bytes 1179652
  54.4 0.9 copy-start
  55.4 104.0 %reduce-scatter.2.cloned.1.call-start = ((), (), s32[]{:S(2)}) async-start(), calls=%async_computation.4 | async-start | bytes 7077888 | tf_op jit(solution)/shard_map/reduce_scatter | solution.py:334
  55.5 21.5 %collective-permute-start.7 = (bf16[512,256]{1,0:T(8,128)(2,1)S(1)}, bf16[512,256]{1,0:T(8,128)(2,1)S(1)}, u32[]{:S(2)}, u32[]{:S(2)}) collective-permute-start(bf16[512,256]{1,0:T(8,128)(2,1)S(1)} %get-tuple-element.64), channel_id=1, source_target_pairs={{0,4},{4,0},{8,12},{12,8},{16,20},{20,16},{24,28},{28,24},{1,5},{5... | collective-permute-start | bytes 786440 | tf_op jit(solution)/shard_map/ppermute | solution.py:288
  59.5 9.9 %collective-permute-start.4 = (bf16[512,128]{1,0:T(8,128)(2,1)}, bf16[512,128]{1,0:T(8,128)(2,1)S(1)}, u32[]{:S(2)}, u32[]{:S(2)}) collective-permute-start(bf16[512,128]{1,0:T(8,128)(2,1)} %get-tuple-element.61), channel_id=1, source_target_pairs={{0,8},{4,12},{8,16},{12,20},{16,24},{20,28},{24,0},{28,4},{1,9},{5... | collective-permute-start | bytes 393224 | tf_op jit(solution)/shard_map/ppermute | solution.py:283
  60.8 8.6 %collective-permute-start.5 = (bf16[512,128]{1,0:T(8,128)(2,1)}, bf16[512,128]{1,0:T(8,128)(2,1)S(1)}, u32[]{:S(2)}, u32[]{:S(2)}) collective-permute-start(bf16[512,128]{1,0:T(8,128)(2,1)} %get-tuple-element.62), channel_id=1, source_target_pairs={{0,16},{4,20},{8,24},{12,28},{16,0},{20,4},{24,8},{28,12},{1,17},{... | collective-permute-start | bytes 393224 | tf_op jit(solution)/shard_map/ppermute | solution.py:283
  63.5 5.9 %collective-permute-start.6 = (bf16[512,128]{1,0:T(8,128)(2,1)}, bf16[512,128]{1,0:T(8,128)(2,1)S(1)}, u32[]{:S(2)}, u32[]{:S(2)}) collective-permute-start(bf16[512,128]{1,0:T(8,128)(2,1)} %get-tuple-element.63), channel_id=1, source_target_pairs={{0,24},{4,28},{8,0},{12,4},{16,8},{20,12},{24,16},{28,20},{1,25},{... | collective-permute-start | bytes 393224 | tf_op jit(solution)/shard_map/ppermute | solution.py:283
  65.0 21.0 %collective-permute-start.11 = (bf16[512,256]{1,0:T(8,128)(2,1)S(1)}, bf16[512,256]{1,0:T(8,128)(2,1)S(1)}, u32[]{:S(2)}, u32[]{:S(2)}) collective-permute-start(bf16[512,256]{1,0:T(8,128)(2,1)S(1)} %get-tuple-element.74), channel_id=1, source_target_pairs={{0,4},{4,0},{8,12},{12,8},{16,20},{20,16},{24,28},{28,24},{1,5},{5... | collective-permute-start | bytes 786440 | tf_op jit(solution)/shard_map/ppermute | solution.py:288
  69.4 33.3 %copy-start.5 = (bf16[512,128]{1,0:T(8,128)(2,1)}, bf16[512,128]{1,0:T(8,128)(2,1)S(1)}, u32[]{:S(2)}) copy-start(bf16[512,128]{1,0:T(8,128)(2,1)S(1)} %collective-permute-done.4.refs_5_) | copy-start | bytes 393220
  69.4 33.3 %copy-start.6 = (bf16[512,128]{1,0:T(8,128)(2,1)}, bf16[512,128]{1,0:T(8,128)(2,1)S(1)}, u32[]{:S(2)}) copy-start(bf16[512,128]{1,0:T(8,128)(2,1)S(1)} %collective-permute-done.5.refs_6_) | copy-start | bytes 393220
  69.4 33.3 %copy-start.7 = (bf16[512,128]{1,0:T(8,128)(2,1)}, bf16[512,128]{1,0:T(8,128)(2,1)S(1)}, u32[]{:S(2)}) copy-start(bf16[512,128]{1,0:T(8,128)(2,1)S(1)} %collective-permute-done.6.refs_7_) | copy-start | bytes 393220
  76.9 0.7 copy-start.15
  80.0 9.0 %collective-permute-start.8 = (bf16[512,128]{1,0:T(8,128)(2,1)}, bf16[512,128]{1,0:T(8,128)(2,1)S(1)}, u32[]{:S(2)}, u32[]{:S(2)}) collective-permute-start(bf16[512,128]{1,0:T(8,128)(2,1)} %get-tuple-element.71), channel_id=1, source_target_pairs={{0,8},{4,12},{8,16},{12,20},{16,24},{20,28},{24,0},{28,4},{1,9},{5... | collective-permute-start | bytes 393224 | tf_op jit(solution)/shard_map/ppermute | solution.py:283
  80.0 11.3 %collective-permute-start.9 = (bf16[512,128]{1,0:T(8,128)(2,1)}, bf16[512,128]{1,0:T(8,128)(2,1)S(1)}, u32[]{:S(2)}, u32[]{:S(2)}) collective-permute-start(bf16[512,128]{1,0:T(8,128)(2,1)} %get-tuple-element.72), channel_id=1, source_target_pairs={{0,16},{4,20},{8,24},{12,28},{16,0},{20,4},{24,8},{28,12},{1,17},{... | collective-permute-start | bytes 393224 | tf_op jit(solution)/shard_map/ppermute | solution.py:283
  85.9 5.4 %collective-permute-start.10 = (bf16[512,128]{1,0:T(8,128)(2,1)}, bf16[512,128]{1,0:T(8,128)(2,1)S(1)}, u32[]{:S(2)}, u32[]{:S(2)}) collective-permute-start(bf16[512,128]{1,0:T(8,128)(2,1)} %get-tuple-element.73), channel_id=1, source_target_pairs={{0,24},{4,28},{8,0},{12,4},{16,8},{20,12},{24,16},{28,20},{1,25},{... | collective-permute-start | bytes 393224 | tf_op jit(solution)/shard_map/ppermute | solution.py:283
  85.9 5.4 %copy-start.14 = (bf16[512,256]{1,0:T(8,128)(2,1)}, bf16[512,256]{1,0:T(8,128)(2,1)S(1)}, u32[]{:S(2)}) copy-start(bf16[512,256]{1,0:T(8,128)(2,1)S(1)} %collective-permute-done.11.dense_ref) | copy-start | bytes 786436
  88.9 13.8 %copy-start.8 = (bf16[512,128]{1,0:T(8,128)(2,1)}, bf16[512,128]{1,0:T(8,128)(2,1)S(1)}, u32[]{:S(2)}) copy-start(bf16[512,128]{1,0:T(8,128)(2,1)S(1)} %collective-permute-done.8.refs_9_) | copy-start | bytes 393220
  91.2 11.5 %copy-start.9 = (bf16[512,128]{1,0:T(8,128)(2,1)}, bf16[512,128]{1,0:T(8,128)(2,1)S(1)}, u32[]{:S(2)}) copy-start(bf16[512,128]{1,0:T(8,128)(2,1)S(1)} %collective-permute-done.9.refs_10_) | copy-start | bytes 393220
  91.3 11.5 %copy-start.10 = (bf16[512,128]{1,0:T(8,128)(2,1)}, bf16[512,128]{1,0:T(8,128)(2,1)S(1)}, u32[]{:S(2)}) copy-start(bf16[512,128]{1,0:T(8,128)(2,1)S(1)} %collective-permute-done.10.refs_11_) | copy-start | bytes 393220
  93.6 8.5 %collective-permute-start.12 = (bf16[512,128]{1,0:T(8,128)(2,1)}, bf16[512,128]{1,0:T(8,128)(2,1)S(1)}, u32[]{:S(2)}, u32[]{:S(2)}) collective-permute-start(bf16[512,128]{1,0:T(8,128)(2,1)} %get-tuple-element.81), channel_id=1, source_target_pairs={{0,8},{4,12},{8,16},{12,20},{16,24},{20,28},{24,0},{28,4},{1,9},{5... | collective-permute-start | bytes 393224 | tf_op jit(solution)/shard_map/ppermute | solution.py:283
  93.7 8.5 %collective-permute-start.13 = (bf16[512,128]{1,0:T(8,128)(2,1)}, bf16[512,128]{1,0:T(8,128)(2,1)S(1)}, u32[]{:S(2)}, u32[]{:S(2)}) collective-permute-start(bf16[512,128]{1,0:T(8,128)(2,1)} %get-tuple-element.82), channel_id=1, source_target_pairs={{0,16},{4,20},{8,24},{12,28},{16,0},{20,4},{24,8},{28,12},{1,17},{... | collective-permute-start | bytes 393224 | tf_op jit(solution)/shard_map/ppermute | solution.py:283
  97.1 5.6 %collective-permute-start.14 = (bf16[512,128]{1,0:T(8,128)(2,1)}, bf16[512,128]{1,0:T(8,128)(2,1)S(1)}, u32[]{:S(2)}, u32[]{:S(2)}) collective-permute-start(bf16[512,128]{1,0:T(8,128)(2,1)} %get-tuple-element.83), channel_id=1, source_target_pairs={{0,24},{4,28},{8,0},{12,4},{16,8},{20,12},{24,16},{28,20},{1,25},{... | collective-permute-start | bytes 393224 | tf_op jit(solution)/shard_map/ppermute | solution.py:283
  102.1 0.7 copy-start.11
  102.1 0.7 copy-start.12
  102.7 0.6 copy-start.13
  159.5 32.7 %all-to-all-start.1 = ((bf16[32,96,128]{2,1,0:T(8,128)(2,1)}), bf16[32,96,128]{2,1,0:T(8,128)(2,1)S(1)}, u32[]{:S(2)}, u32[]{:S(2)}) async-start(bf16[32,96,128]{2,1,0:T(8,128)(2,1)} %bitcast.41), calls=%async_computation.2 | async-start | bytes 1572864 | tf_op jit(solution)/shard_map/all_to_all | solution.py:291
  192.1 0.9 copy-start.1
Sparse Core Ops, SparseCore 0:
  55.5 41.6 all-gather.1
  117.4 41.9 reduce-scatter.1

commit v5 on v4

--- a/solution.py
+++ b/solution.py
@@ -314,7 +314,8 @@
     rows = lax.all_gather(mine, "dp", axis=0, tiled=True).reshape((N_DP,) + VIEW)
     up, down = other_side(parts[1]), other_side(parts[2])
     gate, up = lax.optimization_barrier((to_holders(pack(gate)), up))
-    up, down = lax.optimization_barrier((to_holders(pack(up)), down))
+    up = to_holders(pack(up))
+    up[1], down = lax.optimization_barrier((up[1], down))
     pieces = [p.reshape(3, SLAB, HALF) for p in near] + gate + up + to_holders(pack(down))
     piece_specs = [whole_spec(p.shape) for p in pieces]
     fresh = redraw.reshape(3, N_X, 2, SLAB, HALF)

time: 203 us -> 200 us (0.985)
  transfers between devices with their start and end apart: 19 -> 19, of which waited for: 9 -> 7; matrix products, arithmetic and copies ran while one was open for 0% -> 0% of each run, Pallas kernels for 11% -> 11%
where the time goes in v5:
time: 200 us
  waiting for transfers between devices  87.3 us (44%)
  starting transfers between devices  52.3 us (26%)
  Pallas kernels  40.8 us (20%)
  between operations  14.3 us (7%)
  local copies, waits for them, and re-layouts  4.31 us (2%)
    reduce_scatter x1, waiting for transfers between devices, on_device(): lax.psum_scatter(sums.reshape(N_DP * 2 * PIECE, LANE), 'dp', scatter_dime...  42.2 us
    ppermute x3, waiting for transfers between devices, other_side(): return lax.ppermute(slab, 'expert', [(e, e ^ 1) for e in range(N_E)])  26.3 us
    all_to_all x2, starting transfers between devices, exchange(): lax.all_to_all(rows, ('expert', 'mp'), split_axis=0, concat_axis=0, tiled...  21.2 us
    ppermute x12, starting transfers between devices, along_x(): lax.ppermute(piece, 'expert', [(e, (e // 2 + k) % N_X * 2 + e % 2) for e...  20.3 us
    pallas_call x1, Pallas kernels, on_device(): call(expert_kernel, acts + [sds((N_DP,) + VIEW)], prefetch=1, scratch=[pl...  13.9 us
    pallas_call x1, Pallas kernels, on_device(): call(update_kernel, sds((3, N_X, 2, SLAB, COLS)), prefetch=1, scratch=[pl...  12.2 us
    ppermute x3, starting transfers between devices, other_side(): return lax.ppermute(slab, 'expert', [(e, e ^ 1) for e in range(N_E)])  10.7 us
    all_to_all x2, waiting for transfers between devices, exchange(): lax.all_to_all(rows, ('expert', 'mp'), split_axis=0, concat_axis=0, tiled...  10.4 us
  transfers between devices with their start and end apart: 19, of which 7 were waited for; matrix products, arithmetic and copies ran while one was open for 0% of the time, Pallas kernels for 11%

profile of v5, /device:TPU:32, one launch (start us, length us, event | category | flops | bytes accessed | tf_op | source)
XLA Modules:
  0.0 199.7 jit_solution(9661365941724937250)
XLA Ops:
  7.2 1.2 slice_bitcast_fusion
  8.3 2.1 %shard_map.94 = bf16[8,4,96,128]{3,2,1,0:T(8,128)(2,1)} custom-call(s32[2,128]{1,0:T(2,128)} %bitcast.42, f32[2,128]{1,0:T(2,128)} %bitcast.44, bf16[128,128]{1,0:T(8,128)(2,1)} %tok_ref.1, bf16[128,128]{1,0:T(8,128)(2,1)} %cot_ref.1), custom_call_target="tpu_custom_call" | custom-call | flops 1024 | bytes 1024 | tf_op jit(solution)/shard_map/pallas_call | solution.py:305
  10.4 11.2 %all-to-all-start = ((bf16[32,96,128]{2,1,0:T(8,128)(2,1)}), bf16[32,96,128]{2,1,0:T(8,128)(2,1)S(1)}, u32[]{:S(2)}, u32[]{:S(2)}) async-start(bf16[32,96,128]{2,1,0:T(8,128)(2,1)} %bitcast.31), calls=%async_computation | async-start | bytes 1572864 | tf_op jit(solution)/shard_map/all_to_all | solution.py:291
  21.6 0.0 all-gather.2.cloned.1.call-start
  21.7 0.7 pad_add_fusion.where_ref
  22.3 3.2 %shard_map.95 = (bf16[1536,128]{1,0:T(8,128)(2,1)}, bf16[1536,128]{1,0:T(8,128)(2,1)}, bf16[1536,128]{1,0:T(8,128)(2,1)}, bf16[1536,128]{1,0:T(8,128)(2,1)}) custom-call(s32[2]{0:T(128)} %pad_add_fusion.where_ref, s32[8,256]{1,0:T(8,128)} %refs_18_.1, bf16[1536,256]{1,0:T(8,128)(2,1)} %bitcast.29), custom_call_target="tpu_custom_call" | custom-call | flops 1024 | bytes 1024 | tf_op jit(solution)/shard_map/pallas_call | solution.py:295
  25.5 1.5 collective-permute-start
  27.0 2.7 %collective-permute-start.1 = (bf16[1536,128]{1,0:T(8,128)(2,1)}, bf16[1536,128]{1,0:T(8,128)(2,1)S(1)}, u32[]{:S(2)}, u32[]{:S(2)}) collective-permute-start(bf16[1536,128]{1,0:T(8,128)(2,1)} %get-tuple-element.46), channel_id=1, source_target_pairs={{0,16},{4,20},{8,24},{12,28},{16,0},{20,4},{24,8},{28,12},{1,17},{... | collective-permute-start | bytes 1179656 | tf_op jit(solution)/shard_map/ppermute | solution.py:283
  29.7 1.4 collective-permute-start.2
  31.1 4.5 %collective-permute-start.3 = (bf16[512,256]{1,0:T(8,128)(2,1)S(1)}, bf16[512,256]{1,0:T(8,128)(2,1)S(1)}, u32[]{:S(2)}, u32[]{:S(2)}) collective-permute-start(bf16[512,256]{1,0:T(8,128)(2,1)S(1)} %get-tuple-element.48), channel_id=1, source_target_pairs={{0,4},{4,0},{8,12},{12,8},{16,20},{20,16},{24,28},{28,24},{1,5},{5... | collective-permute-start | bytes 786440 | tf_op jit(solution)/shard_map/ppermute | solution.py:288
  35.6 18.8 %collective-permute-done.3.dense_ref = bf16[512,256]{1,0:T(8,128)(2,1)S(1)} collective-permute-done((bf16[512,256]{1,0:T(8,128)(2,1)S(1)}, bf16[512,256]{1,0:T(8,128)(2,1)S(1)}, u32[]{:S(2)}, u32[]{:S(2)}) %collective-permute-start.3) | collective-permute-done | bytes 262176 | tf_op jit(solution)/shard_map/ppermute | solution.py:288
  54.4 0.0 collective-permute-done
  54.4 0.0 collective-permute-done.1
  54.4 0.0 copy-start.3
  54.4 0.0 collective-permute-done.2
  54.4 0.0 copy-start.4
  54.4 0.0 all-to-all-done
  54.4 0.0 copy-start
  54.4 0.9 copy-done
  55.4 0.0 all-gather.2.cloned.1.call-update
  55.4 0.0 reduce-scatter.2.cloned.1.call-start
  55.5 1.8 collective-permute-start.7
  57.2 0.0 copy-done.16
  57.2 2.3 %shard_map.96 = (bf16[512,128]{1,0:T(8,128)(2,1)}, bf16[512,128]{1,0:T(8,128)(2,1)}, bf16[512,128]{1,0:T(8,128)(2,1)}, bf16[512,128]{1,0:T(8,128)(2,1)}) custom-call(s32[2]{0:T(128)} %pad_add_fusion.where_ref, s32[8,256]{1,0:T(8,128)} %refs_18_.1, bf16[512,256]{1,0:T(8,128)(2,1)} %copy-done.16), custom_call_target="tpu_custom_call" | custom-call | flops 1024 | bytes 1024 | tf_op jit(solution)/shard_map/pallas_call | solution.py:295
  59.5 1.3 collective-permute-start.4
  60.8 2.7 %collective-permute-start.5 = (bf16[512,128]{1,0:T(8,128)(2,1)}, bf16[512,128]{1,0:T(8,128)(2,1)S(1)}, u32[]{:S(2)}, u32[]{:S(2)}) collective-permute-start(bf16[512,128]{1,0:T(8,128)(2,1)} %get-tuple-element.59), channel_id=1, source_target_pairs={{0,16},{4,20},{8,24},{12,28},{16,0},{20,4},{24,8},{28,12},{1,17},{... | collective-permute-start | bytes 393224 | tf_op jit(solution)/shard_map/ppermute | solution.py:283
  63.5 1.4 collective-permute-start.6
  65.0 4.4 %collective-permute-start.9 = (bf16[512,256]{1,0:T(8,128)(2,1)S(1)}, bf16[512,256]{1,0:T(8,128)(2,1)S(1)}, u32[]{:S(2)}, u32[]{:S(2)}) collective-permute-start(bf16[512,256]{1,0:T(8,128)(2,1)S(1)} %get-tuple-element.69), channel_id=1, source_target_pairs={{0,4},{4,0},{8,12},{12,8},{16,20},{20,16},{24,28},{28,24},{1,5},{5... | collective-permute-start | bytes 786440 | tf_op jit(solution)/shard_map/ppermute | solution.py:288
  69.4 0.0 collective-permute-done.4.refs_5_
  69.4 0.0 collective-permute-done.5.refs_6_
  69.4 0.0 copy-start.6
  69.4 0.0 collective-permute-done.6.refs_7_
  69.4 0.0 copy-start.7
  69.4 7.5 %collective-permute-done.7.dense_ref = bf16[512,256]{1,0:T(8,128)(2,1)S(1)} collective-permute-done((bf16[512,256]{1,0:T(8,128)(2,1)S(1)}, bf16[512,256]{1,0:T(8,128)(2,1)S(1)}, u32[]{:S(2)}, u32[]{:S(2)}) %collective-permute-start.7) | collective-permute-done | bytes 262176 | tf_op jit(solution)/shard_map/ppermute | solution.py:288
  76.9 0.7 copy-done.15
  77.7 2.3 %shard_map.97 = (bf16[512,128]{1,0:T(8,128)(2,1)}, bf16[512,128]{1,0:T(8,128)(2,1)}, bf16[512,128]{1,0:T(8,128)(2,1)}, bf16[512,128]{1,0:T(8,128)(2,1)}) custom-call(s32[2]{0:T(128)} %pad_add_fusion.where_ref, s32[8,256]{1,0:T(8,128)} %refs_18_.1, bf16[512,256]{1,0:T(8,128)(2,1)} %copy-done.15), custom_call_target="tpu_custom_call" | custom-call | flops 1024 | bytes 1024 | tf_op jit(solution)/shard_map/pallas_call | solution.py:295
  80.0 0.0 collective-permute-start.8
  80.0 6.0 %collective-permute-start.10 = (bf16[512,128]{1,0:T(8,128)(2,1)}, bf16[512,128]{1,0:T(8,128)(2,1)S(1)}, u32[]{:S(2)}, u32[]{:S(2)}) collective-permute-start(bf16[512,128]{1,0:T(8,128)(2,1)} %get-tuple-element.71), channel_id=1, source_target_pairs={{0,16},{4,20},{8,24},{12,28},{16,0},{20,4},{24,8},{28,12},{1,17},{... | collective-permute-start | bytes 393224 | tf_op jit(solution)/shard_map/ppermute | solution.py:283
  85.9 0.0 collective-permute-start.11
  85.9 0.0 collective-permute-done.9.dense_ref
  86.0 3.0 %collective-permute-done.8.refs_9_ = bf16[512,128]{1,0:T(8,128)(2,1)S(1)} collective-permute-done((bf16[512,128]{1,0:T(8,128)(2,1)}, bf16[512,128]{1,0:T(8,128)(2,1)S(1)}, u32[]{:S(2)}, u32[]{:S(2)}) %collective-permute-start.8) | collective-permute-done | bytes 131104 | tf_op jit(solution)/shard_map/ppermute | solution.py:283
  88.9 0.0 copy-done.14
  89.0 2.3 %shard_map.98 = (bf16[512,128]{1,0:T(8,128)(2,1)}, bf16[512,128]{1,0:T(8,128)(2,1)}, bf16[512,128]{1,0:T(8,128)(2,1)}, bf16[512,128]{1,0:T(8,128)(2,1)}) custom-call(s32[2]{0:T(128)} %pad_add_fusion.where_ref, s32[8,256]{1,0:T(8,128)} %refs_18_.1, bf16[512,256]{1,0:T(8,128)(2,1)} %copy-done.14), custom_call_target="tpu_custom_call" | custom-call | flops 1024 | bytes 1024 | tf_op jit(solution)/shard_map/pallas_call | solution.py:295
  91.3 0.0 collective-permute-start.12
  91.3 3.0 %collective-permute-start.13 = (bf16[512,128]{1,0:T(8,128)(2,1)}, bf16[512,128]{1,0:T(8,128)(2,1)S(1)}, u32[]{:S(2)}, u32[]{:S(2)}) collective-permute-start(bf16[512,128]{1,0:T(8,128)(2,1)} %get-tuple-element.76), channel_id=1, source_target_pairs={{0,16},{4,20},{8,24},{12,28},{16,0},{20,4},{24,8},{28,12},{1,17},{... | collective-permute-start | bytes 393224 | tf_op jit(solution)/shard_map/ppermute | solution.py:283
  94.3 0.3 collective-permute-start.14
  94.5 0.0 collective-permute-done.10.refs_10_
  94.5 0.0 collective-permute-done.11.refs_11_
  94.5 0.0 copy-start.10
  94.6 4.5 %collective-permute-done.12.refs_13_ = bf16[512,128]{1,0:T(8,128)(2,1)S(1)} collective-permute-done((bf16[512,128]{1,0:T(8,128)(2,1)}, bf16[512,128]{1,0:T(8,128)(2,1)S(1)}, u32[]{:S(2)}, u32[]{:S(2)}) %collective-permute-start.12) | collective-permute-done | bytes 131104 | tf_op jit(solution)/shard_map/ppermute | solution.py:283
  99.1 0.0 collective-permute-done.13.refs_14_
  99.1 0.9 collective-permute-done.14.refs_15_
  100.0 0.0 copy-done.2
  100.0 0.0 copy-done.3
  100.0 0.0 copy-done.4
  100.1 0.5 copy-done.13
  100.6 13.9 %shard_map.99 = (bf16[384,256]{1,0:T(8,128)(2,1)}, bf16[384,512]{1,0:T(8,128)(2,1)}, bf16[8,4,2,4,96,128]{5,4,3,2,1,0:T(8,128)(2,1)}) custom-call(s32[2]{0:T(128)} %pad_add_fusion.where_ref, bf16[8,4,2,4,96,128]{5,4,3,2,1,0:T(8,128)(2,1)} %bitcast.23, bf16[3,4,2,512,128]{4,3,2,1,0:T(8,128)(2,1)} %bitcast.25, bf16[3,512,128]{2,1,0:T(8,128)(2,1)} %bitcast.33, ...), custom_call_target="tpu_custom_call" | custom-call | flops 1024 | bytes 1024 | tf_op jit(solution)/shard_map/pallas_call | solution.py:325
  114.5 0.0 reduce-scatter.2.cloned.1.call-update
  114.6 42.2 %reduce-scatter.2.cloned.1.call-done = bf16[3072,128]{1,0:T(8,128)(2,1)} async-done(((bf16[24576,128]{1,0:T(8,128)(2,1)}), bf16[3072,128]{1,0:T(8,128)(2,1)}) %reduce-scatter.2.cloned.1.call-update) | async-done | bytes 786448 | tf_op jit(solution)/shard_map/reduce_scatter | solution.py:335
  156.8 10.1 %all-to-all-start.1 = ((bf16[32,96,128]{2,1,0:T(8,128)(2,1)}), bf16[32,96,128]{2,1,0:T(8,128)(2,1)S(1)}, u32[]{:S(2)}, u32[]{:S(2)}) async-start(bf16[32,96,128]{2,1,0:T(8,128)(2,1)} %bitcast.41), calls=%async_computation.2 | async-start | bytes 1572864 | tf_op jit(solution)/shard_map/all_to_all | solution.py:291
  166.8 12.2 %shard_map.101 = bf16[3,4,2,512,256]{4,3,2,1,0:T(8,128)(2,1)} custom-call(s32[2]{0:T(128)} %pad_add_fusion.where_ref, bf16[8,4,2,4,96,128]{5,4,3,2,1,0:T(8,128)(2,1)} %bitcast.24, bf16[3,4,2,512,128]{4,3,2,1,0:T(8,128)(2,1)} %bitcast.26, bf16[3,512,128]{2,1,0:T(8,128)(2,1)} %bitcast.34, bf16[3,512,128]{2,1,0:T(8,128)(2,1)} %bitcast.36, ...), custom_call_target="tpu_custom_call" | custom-call | flops 1024 | bytes 1024 | tf_op jit(solution)/shard_map/pallas_call | solution.py:338
  179.1 10.4 %all-to-all-done.1 = bf16[32,96,128]{2,1,0:T(8,128)(2,1)S(1)} async-done(((bf16[32,96,128]{2,1,0:T(8,128)(2,1)}), bf16[32,96,128]{2,1,0:T(8,128)(2,1)S(1)}, u32[]{:S(2)}, u32[]{:S(2)}) %all-to-all-start.1) | async-done | bytes 786464 | tf_op jit(solution)/shard_map/all_to_all | solution.py:291
  189.4 0.9 copy-done.1
  190.3 2.5 %shard_map.100 = (bf16[128,128]{1,0:T(8,128)(2,1)}, bf16[128,128]{1,0:T(8,128)(2,1)}) custom-call(s32[2,128]{1,0:T(2,128)} %bitcast.43, f32[2,128]{1,0:T(2,128)} %bitcast.45, bf16[8,4,96,128]{3,2,1,0:T(8,128)(2,1)} %bitcast.32), custom_call_target="tpu_custom_call" | custom-call | flops 1024 | bytes 1024 | tf_op jit(solution)/shard_map/pallas_call | solution.py:353
  (20 shorter events, 0.0 us)
Async XLA Ops:
  10.4 44.0 %all-to-all-start = ((bf16[32,96,128]{2,1,0:T(8,128)(2,1)}), bf16[32,96,128]{2,1,0:T(8,128)(2,1)S(1)}, u32[]{:S(2)}, u32[]{:S(2)}) async-start(bf16[32,96,128]{2,1,0:T(8,128)(2,1)} %bitcast.31), calls=%async_computation | async-start | bytes 1572864 | tf_op jit(solution)/shard_map/all_to_all | solution.py:291
  21.6 78.4 %all-gather.2.cloned.1.call-start = ((), (), s32[]{:S(2)}) async-start(), calls=%async_computation.3 | async-start | bytes 7077888 | tf_op jit(solution)/shard_map/all_gather | solution.py:314
  25.5 28.9 %collective-permute-start = (bf16[1536,128]{1,0:T(8,128)(2,1)}, bf16[1536,128]{1,0:T(8,128)(2,1)S(1)}, u32[]{:S(2)}, u32[]{:S(2)}) collective-permute-start(bf16[1536,128]{1,0:T(8,128)(2,1)} %get-tuple-element.45), channel_id=1, source_target_pairs={{0,8},{4,12},{8,16},{12,20},{16,24},{20,28},{24,0},{28,4},{1,9},{5... | collective-permute-start | bytes 1179656 | tf_op jit(solution)/shard_map/ppermute | solution.py:283
  27.0 27.4 %collective-permute-start.1 = (bf16[1536,128]{1,0:T(8,128)(2,1)}, bf16[1536,128]{1,0:T(8,128)(2,1)S(1)}, u32[]{:S(2)}, u32[]{:S(2)}) collective-permute-start(bf16[1536,128]{1,0:T(8,128)(2,1)} %get-tuple-element.46), channel_id=1, source_target_pairs={{0,16},{4,20},{8,24},{12,28},{16,0},{20,4},{24,8},{28,12},{1,17},{... | collective-permute-start | bytes 1179656 | tf_op jit(solution)/shard_map/ppermute | solution.py:283
  29.7 24.7 %collective-permute-start.2 = (bf16[1536,128]{1,0:T(8,128)(2,1)}, bf16[1536,128]{1,0:T(8,128)(2,1)S(1)}, u32[]{:S(2)}, u32[]{:S(2)}) collective-permute-start(bf16[1536,128]{1,0:T(8,128)(2,1)} %get-tuple-element.47), channel_id=1, source_target_pairs={{0,24},{4,28},{8,0},{12,4},{16,8},{20,12},{24,16},{28,20},{1,25},{... | collective-permute-start | bytes 1179656 | tf_op jit(solution)/shard_map/ppermute | solution.py:283
  31.1 23.3 %collective-permute-start.3 = (bf16[512,256]{1,0:T(8,128)(2,1)S(1)}, bf16[512,256]{1,0:T(8,128)(2,1)S(1)}, u32[]{:S(2)}, u32[]{:S(2)}) collective-permute-start(bf16[512,256]{1,0:T(8,128)(2,1)S(1)} %get-tuple-element.48), channel_id=1, source_target_pairs={{0,4},{4,0},{8,12},{12,8},{16,20},{20,16},{24,28},{28,24},{1,5},{5... | collective-permute-start | bytes 786440 | tf_op jit(solution)/shard_map/ppermute | solution.py:288
  54.4 2.8 %copy-start.16 = (bf16[512,256]{1,0:T(8,128)(2,1)}, bf16[512,256]{1,0:T(8,128)(2,1)S(1)}, u32[]{:S(2)}) copy-start(bf16[512,256]{1,0:T(8,128)(2,1)S(1)} %collective-permute-done.3.dense_ref) | copy-start | bytes 786436
  54.4 45.6 %copy-start.2 = (bf16[1536,128]{1,0:T(8,128)(2,1)}, bf16[1536,128]{1,0:T(8,128)(2,1)S(1)}, u32[]{:S(2)}) copy-start(bf16[1536,128]{1,0:T(8,128)(2,1)S(1)} %collective-permute-done) | copy-start | bytes 1179652
  54.4 45.6 %copy-start.3 = (bf16[1536,128]{1,0:T(8,128)(2,1)}, bf16[1536,128]{1,0:T(8,128)(2,1)S(1)}, u32[]{:S(2)}) copy-start(bf16[1536,128]{1,0:T(8,128)(2,1)S(1)} %collective-permute-done.1) | copy-start | bytes 1179652
  54.4 45.6 %copy-start.4 = (bf16[1536,128]{1,0:T(8,128)(2,1)}, bf16[1536,128]{1,0:T(8,128)(2,1)S(1)}, u32[]{:S(2)}) copy-start(bf16[1536,128]{1,0:T(8,128)(2,1)S(1)} %collective-permute-done.2) | copy-start | bytes 1179652
  54.4 0.9 copy-start
  55.4 101.4 %reduce-scatter.2.cloned.1.call-start = ((), (), s32[]{:S(2)}) async-start(), calls=%async_computation.4 | async-start | bytes 7077888 | tf_op jit(solution)/shard_map/reduce_scatter | solution.py:335
  55.5 21.5 %collective-permute-start.7 = (bf16[512,256]{1,0:T(8,128)(2,1)S(1)}, bf16[512,256]{1,0:T(8,128)(2,1)S(1)}, u32[]{:S(2)}, u32[]{:S(2)}) collective-permute-start(bf16[512,256]{1,0:T(8,128)(2,1)S(1)} %get-tuple-element.61), channel_id=1, source_target_pairs={{0,4},{4,0},{8,12},{12,8},{16,20},{20,16},{24,28},{28,24},{1,5},{5... | collective-permute-start | bytes 786440 | tf_op jit(solution)/shard_map/ppermute | solution.py:288
  59.5 9.9 %collective-permute-start.4 = (bf16[512,128]{1,0:T(8,128)(2,1)}, bf16[512,128]{1,0:T(8,128)(2,1)S(1)}, u32[]{:S(2)}, u32[]{:S(2)}) collective-permute-start(bf16[512,128]{1,0:T(8,128)(2,1)} %get-tuple-element.58), channel_id=1, source_target_pairs={{0,8},{4,12},{8,16},{12,20},{16,24},{20,28},{24,0},{28,4},{1,9},{5... | collective-permute-start | bytes 393224 | tf_op jit(solution)/shard_map/ppermute | solution.py:283
  60.8 8.6 %collective-permute-start.5 = (bf16[512,128]{1,0:T(8,128)(2,1)}, bf16[512,128]{1,0:T(8,128)(2,1)S(1)}, u32[]{:S(2)}, u32[]{:S(2)}) collective-permute-start(bf16[512,128]{1,0:T(8,128)(2,1)} %get-tuple-element.59), channel_id=1, source_target_pairs={{0,16},{4,20},{8,24},{12,28},{16,0},{20,4},{24,8},{28,12},{1,17},{... | collective-permute-start | bytes 393224 | tf_op jit(solution)/shard_map/ppermute | solution.py:283
  63.5 5.9 %collective-permute-start.6 = (bf16[512,128]{1,0:T(8,128)(2,1)}, bf16[512,128]{1,0:T(8,128)(2,1)S(1)}, u32[]{:S(2)}, u32[]{:S(2)}) collective-permute-start(bf16[512,128]{1,0:T(8,128)(2,1)} %get-tuple-element.60), channel_id=1, source_target_pairs={{0,24},{4,28},{8,0},{12,4},{16,8},{20,12},{24,16},{28,20},{1,25},{... | collective-permute-start | bytes 393224 | tf_op jit(solution)/shard_map/ppermute | solution.py:283
  65.0 21.0 %collective-permute-start.9 = (bf16[512,256]{1,0:T(8,128)(2,1)S(1)}, bf16[512,256]{1,0:T(8,128)(2,1)S(1)}, u32[]{:S(2)}, u32[]{:S(2)}) collective-permute-start(bf16[512,256]{1,0:T(8,128)(2,1)S(1)} %get-tuple-element.69), channel_id=1, source_target_pairs={{0,4},{4,0},{8,12},{12,8},{16,20},{20,16},{24,28},{28,24},{1,5},{5... | collective-permute-start | bytes 786440 | tf_op jit(solution)/shard_map/ppermute | solution.py:288
  69.4 30.6 %copy-start.5 = (bf16[512,128]{1,0:T(8,128)(2,1)}, bf16[512,128]{1,0:T(8,128)(2,1)S(1)}, u32[]{:S(2)}) copy-start(bf16[512,128]{1,0:T(8,128)(2,1)S(1)} %collective-permute-done.4.refs_5_) | copy-start | bytes 393220
  69.4 30.6 %copy-start.6 = (bf16[512,128]{1,0:T(8,128)(2,1)}, bf16[512,128]{1,0:T(8,128)(2,1)S(1)}, u32[]{:S(2)}) copy-start(bf16[512,128]{1,0:T(8,128)(2,1)S(1)} %collective-permute-done.5.refs_6_) | copy-start | bytes 393220
  69.4 30.6 %copy-start.7 = (bf16[512,128]{1,0:T(8,128)(2,1)}, bf16[512,128]{1,0:T(8,128)(2,1)S(1)}, u32[]{:S(2)}) copy-start(bf16[512,128]{1,0:T(8,128)(2,1)S(1)} %collective-permute-done.6.refs_7_) | copy-start | bytes 393220
  76.9 0.7 copy-start.15
  80.0 9.0 %collective-permute-start.8 = (bf16[512,128]{1,0:T(8,128)(2,1)}, bf16[512,128]{1,0:T(8,128)(2,1)S(1)}, u32[]{:S(2)}, u32[]{:S(2)}) collective-permute-start(bf16[512,128]{1,0:T(8,128)(2,1)} %get-tuple-element.68), channel_id=1, source_target_pairs={{0,8},{4,12},{8,16},{12,20},{16,24},{20,28},{24,0},{28,4},{1,9},{5... | collective-permute-start | bytes 393224 | tf_op jit(solution)/shard_map/ppermute | solution.py:283
  80.0 14.6 %collective-permute-start.10 = (bf16[512,128]{1,0:T(8,128)(2,1)}, bf16[512,128]{1,0:T(8,128)(2,1)S(1)}, u32[]{:S(2)}, u32[]{:S(2)}) collective-permute-start(bf16[512,128]{1,0:T(8,128)(2,1)} %get-tuple-element.71), channel_id=1, source_target_pairs={{0,16},{4,20},{8,24},{12,28},{16,0},{20,4},{24,8},{28,12},{1,17},{... | collective-permute-start | bytes 393224 | tf_op jit(solution)/shard_map/ppermute | solution.py:283
  85.9 8.6 %collective-permute-start.11 = (bf16[512,128]{1,0:T(8,128)(2,1)}, bf16[512,128]{1,0:T(8,128)(2,1)S(1)}, u32[]{:S(2)}, u32[]{:S(2)}) collective-permute-start(bf16[512,128]{1,0:T(8,128)(2,1)} %get-tuple-element.72), channel_id=1, source_target_pairs={{0,24},{4,28},{8,0},{12,4},{16,8},{20,12},{24,16},{28,20},{1,25},{... | collective-permute-start | bytes 393224 | tf_op jit(solution)/shard_map/ppermute | solution.py:283
  85.9 3.0 %copy-start.14 = (bf16[512,256]{1,0:T(8,128)(2,1)}, bf16[512,256]{1,0:T(8,128)(2,1)S(1)}, u32[]{:S(2)}) copy-start(bf16[512,256]{1,0:T(8,128)(2,1)S(1)} %collective-permute-done.9.dense_ref) | copy-start | bytes 786436
  89.0 11.1 %copy-start.8 = (bf16[512,128]{1,0:T(8,128)(2,1)}, bf16[512,128]{1,0:T(8,128)(2,1)S(1)}, u32[]{:S(2)}) copy-start(bf16[512,128]{1,0:T(8,128)(2,1)S(1)} %collective-permute-done.8.refs_9_) | copy-start | bytes 393220
  91.3 7.8 %collective-permute-start.12 = (bf16[512,128]{1,0:T(8,128)(2,1)}, bf16[512,128]{1,0:T(8,128)(2,1)S(1)}, u32[]{:S(2)}, u32[]{:S(2)}) collective-permute-start(bf16[512,128]{1,0:T(8,128)(2,1)} %get-tuple-element.75), channel_id=1, source_target_pairs={{0,8},{4,12},{8,16},{12,20},{16,24},{20,28},{24,0},{28,4},{1,9},{5... | collective-permute-start | bytes 393224 | tf_op jit(solution)/shard_map/ppermute | solution.py:283
  91.3 7.8 %collective-permute-start.13 = (bf16[512,128]{1,0:T(8,128)(2,1)}, bf16[512,128]{1,0:T(8,128)(2,1)S(1)}, u32[]{:S(2)}, u32[]{:S(2)}) collective-permute-start(bf16[512,128]{1,0:T(8,128)(2,1)} %get-tuple-element.76), channel_id=1, source_target_pairs={{0,16},{4,20},{8,24},{12,28},{16,0},{20,4},{24,8},{28,12},{1,17},{... | collective-permute-start | bytes 393224 | tf_op jit(solution)/shard_map/ppermute | solution.py:283
  94.3 5.7 %collective-permute-start.14 = (bf16[512,128]{1,0:T(8,128)(2,1)}, bf16[512,128]{1,0:T(8,128)(2,1)S(1)}, u32[]{:S(2)}, u32[]{:S(2)}) collective-permute-start(bf16[512,128]{1,0:T(8,128)(2,1)} %get-tuple-element.77), channel_id=1, source_target_pairs={{0,24},{4,28},{8,0},{12,4},{16,8},{20,12},{24,16},{28,20},{1,25},{... | collective-permute-start | bytes 393224 | tf_op jit(solution)/shard_map/ppermute | solution.py:283
  94.5 5.5 %copy-start.9 = (bf16[512,128]{1,0:T(8,128)(2,1)}, bf16[512,128]{1,0:T(8,128)(2,1)S(1)}, u32[]{:S(2)}) copy-start(bf16[512,128]{1,0:T(8,128)(2,1)S(1)} %collective-permute-done.10.refs_10_) | copy-start | bytes 393220
  94.5 5.5 %copy-start.10 = (bf16[512,128]{1,0:T(8,128)(2,1)}, bf16[512,128]{1,0:T(8,128)(2,1)S(1)}, u32[]{:S(2)}) copy-start(bf16[512,128]{1,0:T(8,128)(2,1)S(1)} %collective-permute-done.11.refs_11_) | copy-start | bytes 393220
  99.1 1.0 copy-start.11
  99.1 1.0 copy-start.12
  100.0 0.6 copy-start.13
  156.8 32.7 %all-to-all-start.1 = ((bf16[32,96,128]{2,1,0:T(8,128)(2,1)}), bf16[32,96,128]{2,1,0:T(8,128)(2,1)S(1)}, u32[]{:S(2)}, u32[]{:S(2)}) async-start(bf16[32,96,128]{2,1,0:T(8,128)(2,1)} %bitcast.41), calls=%async_computation.2 | async-start | bytes 1572864 | tf_op jit(solution)/shard_map/all_to_all | solution.py:291
  189.4 0.9 copy-start.1
Sparse Core Ops, SparseCore 0:
  55.5 41.6 all-gather.1
  114.7 42.0 reduce-scatter.1

commit v6 on v5

--- a/solution.py
+++ b/solution.py
@@ -310,7 +310,7 @@
 
     gate = other_side(parts[0])
     near = to_holders(near)
-    mine, near, gate, parts = lax.optimization_barrier((mine, near, gate, parts))
+    mine, near, gate, parts[2] = lax.optimization_barrier((mine, near, gate, parts[2]))
     rows = lax.all_gather(mine, "dp", axis=0, tiled=True).reshape((N_DP,) + VIEW)
     up, down = other_side(parts[1]), other_side(parts[2])
     gate, up = lax.optimization_barrier((to_holders(pack(gate)), up))

time: 200 us -> 201 us (level)
  no operation moved by 1% of the time
where the time goes in v6:
time: 201 us; the launch traced here: 200 us
  waiting for transfers between devices  87.4 us (43%)
  starting transfers between devices  52.3 us (26%)
  Pallas kernels  40.8 us (20%)
  between operations  14.3 us (7%)
  local copies, waits for them, and re-layouts  5.01 us (2%)
    reduce_scatter x1, waiting for transfers between devices, on_device(): lax.psum_scatter(sums.reshape(N_DP * 2 * PIECE, LANE), 'dp', scatter_dime...  42.2 us
    ppermute x3, waiting for transfers between devices, other_side(): return lax.ppermute(slab, 'expert', [(e, e ^ 1) for e in range(N_E)])  26.3 us
    all_to_all x2, starting transfers between devices, exchange(): lax.all_to_all(rows, ('expert', 'mp'), split_axis=0, concat_axis=0, tiled...  21.2 us
    ppermute x12, starting transfers between devices, along_x(): lax.ppermute(piece, 'expert', [(e, (e // 2 + k) % N_X * 2 + e % 2) for e...  20.3 us
    pallas_call x1, Pallas kernels, on_device(): call(expert_kernel, acts + [sds((N_DP,) + VIEW)], prefetch=1, scratch=[pl...  13.9 us
    pallas_call x1, Pallas kernels, on_device(): call(update_kernel, sds((3, N_X, 2, SLAB, COLS)), prefetch=1, scratch=[pl...  12.2 us
    ppermute x3, starting transfers between devices, other_side(): return lax.ppermute(slab, 'expert', [(e, e ^ 1) for e in range(N_E)])  10.7 us
    all_to_all x2, waiting for transfers between devices, exchange(): lax.all_to_all(rows, ('expert', 'mp'), split_axis=0, concat_axis=0, tiled...  10.4 us
  transfers between devices with their start and end apart: 19, of which 7 were waited for; matrix products, arithmetic and copies ran while one was open for 0% of the time, Pallas kernels for 11%

profile of v6, /device:TPU:32, one launch (start us, length us, event | category | flops | bytes accessed | tf_op | source)
XLA Modules:
  0.0 200.4 jit_solution(3106711139904472650)
XLA Ops:
  7.2 1.2 slice_bitcast_fusion
  8.3 2.1 %shard_map.94 = bf16[8,4,96,128]{3,2,1,0:T(8,128)(2,1)} custom-call(s32[2,128]{1,0:T(2,128)} %bitcast.42, f32[2,128]{1,0:T(2,128)} %bitcast.44, bf16[128,128]{1,0:T(8,128)(2,1)} %tok_ref.1, bf16[128,128]{1,0:T(8,128)(2,1)} %cot_ref.1), custom_call_target="tpu_custom_call" | custom-call | flops 1024 | bytes 1024 | tf_op jit(solution)/shard_map/pallas_call | solution.py:305
  10.4 11.2 %all-to-all-start = ((bf16[32,96,128]{2,1,0:T(8,128)(2,1)}), bf16[32,96,128]{2,1,0:T(8,128)(2,1)S(1)}, u32[]{:S(2)}, u32[]{:S(2)}) async-start(bf16[32,96,128]{2,1,0:T(8,128)(2,1)} %bitcast.31), calls=%async_computation | async-start | bytes 1572864 | tf_op jit(solution)/shard_map/all_to_all | solution.py:291
  21.6 0.0 all-gather.2.cloned.1.call-start
  21.7 0.7 pad_add_fusion.where_ref
  22.3 3.2 %shard_map.95 = (bf16[1536,128]{1,0:T(8,128)(2,1)}, bf16[1536,128]{1,0:T(8,128)(2,1)}, bf16[1536,128]{1,0:T(8,128)(2,1)}, bf16[1536,128]{1,0:T(8,128)(2,1)}) custom-call(s32[2]{0:T(128)} %pad_add_fusion.where_ref, s32[8,256]{1,0:T(8,128)} %refs_18_.1, bf16[1536,256]{1,0:T(8,128)(2,1)} %bitcast.29), custom_call_target="tpu_custom_call" | custom-call | flops 1024 | bytes 1024 | tf_op jit(solution)/shard_map/pallas_call | solution.py:295
  25.5 1.5 collective-permute-start
  27.0 2.7 %collective-permute-start.1 = (bf16[1536,128]{1,0:T(8,128)(2,1)}, bf16[1536,128]{1,0:T(8,128)(2,1)S(1)}, u32[]{:S(2)}, u32[]{:S(2)}) collective-permute-start(bf16[1536,128]{1,0:T(8,128)(2,1)} %get-tuple-element.45), channel_id=1, source_target_pairs={{0,16},{4,20},{8,24},{12,28},{16,0},{20,4},{24,8},{28,12},{1,17},{... | collective-permute-start | bytes 1179656 | tf_op jit(solution)/shard_map/ppermute | solution.py:283
  29.7 1.4 collective-permute-start.2
  31.1 4.5 %collective-permute-start.3 = (bf16[512,256]{1,0:T(8,128)(2,1)S(1)}, bf16[512,256]{1,0:T(8,128)(2,1)S(1)}, u32[]{:S(2)}, u32[]{:S(2)}) collective-permute-start(bf16[512,256]{1,0:T(8,128)(2,1)S(1)} %get-tuple-element.47), channel_id=1, source_target_pairs={{0,4},{4,0},{8,12},{12,8},{16,20},{20,16},{24,28},{28,24},{1,5},{5... | collective-permute-start | bytes 786440 | tf_op jit(solution)/shard_map/ppermute | solution.py:288
  35.6 18.8 %collective-permute-done.3.dense_ref = bf16[512,256]{1,0:T(8,128)(2,1)S(1)} collective-permute-done((bf16[512,256]{1,0:T(8,128)(2,1)S(1)}, bf16[512,256]{1,0:T(8,128)(2,1)S(1)}, u32[]{:S(2)}, u32[]{:S(2)}) %collective-permute-start.3) | collective-permute-done | bytes 262176 | tf_op jit(solution)/shard_map/ppermute | solution.py:288
  54.4 0.0 collective-permute-done
  54.4 0.0 collective-permute-done.1
  54.4 0.0 collective-permute-done.2
  54.4 0.0 all-to-all-done
  54.4 0.0 copy-start
  54.4 0.9 copy-done
  55.4 0.0 all-gather.2.cloned.1.call-update
  55.4 0.0 reduce-scatter.2.cloned.1.call-start
  55.5 1.8 collective-permute-start.7
  57.2 2.3 %shard_map.96 = (bf16[512,128]{1,0:T(8,128)(2,1)}, bf16[512,128]{1,0:T(8,128)(2,1)}, bf16[512,128]{1,0:T(8,128)(2,1)}, bf16[512,128]{1,0:T(8,128)(2,1)}) custom-call(s32[2]{0:T(128)} %pad_add_fusion.where_ref, s32[8,256]{1,0:T(8,128)} %refs_18_.1, bf16[512,256]{1,0:T(8,128)(2,1)} %copy-done.16), custom_call_target="tpu_custom_call" | custom-call | flops 1024 | bytes 1024 | tf_op jit(solution)/shard_map/pallas_call | solution.py:295
  59.5 1.3 collective-permute-start.4
  60.8 2.7 %collective-permute-start.5 = (bf16[512,128]{1,0:T(8,128)(2,1)}, bf16[512,128]{1,0:T(8,128)(2,1)S(1)}, u32[]{:S(2)}, u32[]{:S(2)}) collective-permute-start(bf16[512,128]{1,0:T(8,128)(2,1)} %get-tuple-element.57), channel_id=1, source_target_pairs={{0,16},{4,20},{8,24},{12,28},{16,0},{20,4},{24,8},{28,12},{1,17},{... | collective-permute-start | bytes 393224 | tf_op jit(solution)/shard_map/ppermute | solution.py:283
  63.5 1.4 collective-permute-start.6
  65.0 4.4 %collective-permute-start.9 = (bf16[512,256]{1,0:T(8,128)(2,1)S(1)}, bf16[512,256]{1,0:T(8,128)(2,1)S(1)}, u32[]{:S(2)}, u32[]{:S(2)}) collective-permute-start(bf16[512,256]{1,0:T(8,128)(2,1)S(1)} %get-tuple-element.67), channel_id=1, source_target_pairs={{0,4},{4,0},{8,12},{12,8},{16,20},{20,16},{24,28},{28,24},{1,5},{5... | collective-permute-start | bytes 786440 | tf_op jit(solution)/shard_map/ppermute | solution.py:288
  69.4 7.5 %collective-permute-done.7.dense_ref = bf16[512,256]{1,0:T(8,128)(2,1)S(1)} collective-permute-done((bf16[512,256]{1,0:T(8,128)(2,1)S(1)}, bf16[512,256]{1,0:T(8,128)(2,1)S(1)}, u32[]{:S(2)}, u32[]{:S(2)}) %collective-permute-start.7) | collective-permute-done | bytes 262176 | tf_op jit(solution)/shard_map/ppermute | solution.py:288
  76.9 0.0 collective-permute-done.4.refs_5_
  77.0 0.0 collective-permute-done.5.refs_6_
  77.0 0.0 collective-permute-done.6.refs_7_
  77.0 0.0 copy-start.7
  77.0 0.7 copy-done.15
  77.7 2.3 %shard_map.97 = (bf16[512,128]{1,0:T(8,128)(2,1)}, bf16[512,128]{1,0:T(8,128)(2,1)}, bf16[512,128]{1,0:T(8,128)(2,1)}, bf16[512,128]{1,0:T(8,128)(2,1)}) custom-call(s32[2]{0:T(128)} %pad_add_fusion.where_ref, s32[8,256]{1,0:T(8,128)} %refs_18_.1, bf16[512,256]{1,0:T(8,128)(2,1)} %copy-done.15), custom_call_target="tpu_custom_call" | custom-call | flops 1024 | bytes 1024 | tf_op jit(solution)/shard_map/pallas_call | solution.py:295
  80.0 0.0 collective-permute-start.8
  80.0 6.0 %collective-permute-start.10 = (bf16[512,128]{1,0:T(8,128)(2,1)}, bf16[512,128]{1,0:T(8,128)(2,1)S(1)}, u32[]{:S(2)}, u32[]{:S(2)}) collective-permute-start(bf16[512,128]{1,0:T(8,128)(2,1)} %get-tuple-element.69), channel_id=1, source_target_pairs={{0,16},{4,20},{8,24},{12,28},{16,0},{20,4},{24,8},{28,12},{1,17},{... | collective-permute-start | bytes 393224 | tf_op jit(solution)/shard_map/ppermute | solution.py:283
  85.9 0.0 collective-permute-start.11
  85.9 3.0 %collective-permute-done.8.refs_9_ = bf16[512,128]{1,0:T(8,128)(2,1)S(1)} collective-permute-done((bf16[512,128]{1,0:T(8,128)(2,1)}, bf16[512,128]{1,0:T(8,128)(2,1)S(1)}, u32[]{:S(2)}, u32[]{:S(2)}) %collective-permute-start.8) | collective-permute-done | bytes 131104 | tf_op jit(solution)/shard_map/ppermute | solution.py:283
  89.0 0.0 collective-permute-done.9.dense_ref
  89.0 0.7 copy-done.14
  89.7 2.3 %shard_map.98 = (bf16[512,128]{1,0:T(8,128)(2,1)}, bf16[512,128]{1,0:T(8,128)(2,1)}, bf16[512,128]{1,0:T(8,128)(2,1)}, bf16[512,128]{1,0:T(8,128)(2,1)}) custom-call(s32[2]{0:T(128)} %pad_add_fusion.where_ref, s32[8,256]{1,0:T(8,128)} %refs_18_.1, bf16[512,256]{1,0:T(8,128)(2,1)} %copy-done.14), custom_call_target="tpu_custom_call" | custom-call | flops 1024 | bytes 1024 | tf_op jit(solution)/shard_map/pallas_call | solution.py:295
  92.0 0.0 collective-permute-start.12
  92.0 2.9 %collective-permute-start.13 = (bf16[512,128]{1,0:T(8,128)(2,1)}, bf16[512,128]{1,0:T(8,128)(2,1)S(1)}, u32[]{:S(2)}, u32[]{:S(2)}) collective-permute-start(bf16[512,128]{1,0:T(8,128)(2,1)} %get-tuple-element.74), channel_id=1, source_target_pairs={{0,16},{4,20},{8,24},{12,28},{16,0},{20,4},{24,8},{28,12},{1,17},{... | collective-permute-start | bytes 393224 | tf_op jit(solution)/shard_map/ppermute | solution.py:283
  94.9 0.3 collective-permute-start.14
  95.2 0.0 collective-permute-done.10.refs_10_
  95.2 0.0 collective-permute-done.11.refs_11_
  95.3 4.5 %collective-permute-done.12.refs_13_ = bf16[512,128]{1,0:T(8,128)(2,1)S(1)} collective-permute-done((bf16[512,128]{1,0:T(8,128)(2,1)}, bf16[512,128]{1,0:T(8,128)(2,1)S(1)}, u32[]{:S(2)}, u32[]{:S(2)}) %collective-permute-start.12) | collective-permute-done | bytes 131104 | tf_op jit(solution)/shard_map/ppermute | solution.py:283
  99.8 0.0 collective-permute-done.13.refs_14_
  99.8 0.9 collective-permute-done.14.refs_15_
  100.7 0.0 copy-done.2
  100.7 0.0 copy-done.4
  100.7 0.0 copy-done.5
  100.7 0.0 copy-done.6
  100.7 0.0 copy-done.7
  100.7 0.0 copy-done.8
  100.8 0.0 copy-done.9
  100.8 0.0 copy-done.10
  100.8 0.5 copy-done.13
  101.3 13.9 %shard_map.99 = (bf16[384,256]{1,0:T(8,128)(2,1)}, bf16[384,512]{1,0:T(8,128)(2,1)}, bf16[8,4,2,4,96,128]{5,4,3,2,1,0:T(8,128)(2,1)}) custom-call(s32[2]{0:T(128)} %pad_add_fusion.where_ref, bf16[8,4,2,4,96,128]{5,4,3,2,1,0:T(8,128)(2,1)} %bitcast.23, bf16[3,4,2,512,128]{4,3,2,1,0:T(8,128)(2,1)} %bitcast.25, bf16[3,512,128]{2,1,0:T(8,128)(2,1)} %bitcast.33, ...), custom_call_target="tpu_custom_call" | custom-call | flops 1024 | bytes 1024 | tf_op jit(solution)/shard_map/pallas_call | solution.py:325
  115.2 0.0 reduce-scatter.2.cloned.1.call-update
  115.3 42.2 %reduce-scatter.2.cloned.1.call-done = bf16[3072,128]{1,0:T(8,128)(2,1)} async-done(((bf16[24576,128]{1,0:T(8,128)(2,1)}), bf16[3072,128]{1,0:T(8,128)(2,1)}) %reduce-scatter.2.cloned.1.call-update) | async-done | bytes 786448 | tf_op jit(solution)/shard_map/reduce_scatter | solution.py:335
  157.5 10.1 %all-to-all-start.1 = ((bf16[32,96,128]{2,1,0:T(8,128)(2,1)}), bf16[32,96,128]{2,1,0:T(8,128)(2,1)S(1)}, u32[]{:S(2)}, u32[]{:S(2)}) async-start(bf16[32,96,128]{2,1,0:T(8,128)(2,1)} %bitcast.41), calls=%async_computation.2 | async-start | bytes 1572864 | tf_op jit(solution)/shard_map/all_to_all | solution.py:291
  167.5 12.2 %shard_map.101 = bf16[3,4,2,512,256]{4,3,2,1,0:T(8,128)(2,1)} custom-call(s32[2]{0:T(128)} %pad_add_fusion.where_ref, bf16[8,4,2,4,96,128]{5,4,3,2,1,0:T(8,128)(2,1)} %bitcast.24, bf16[3,4,2,512,128]{4,3,2,1,0:T(8,128)(2,1)} %bitcast.26, bf16[3,512,128]{2,1,0:T(8,128)(2,1)} %bitcast.34, bf16[3,512,128]{2,1,0:T(8,128)(2,1)} %bitcast.36, ...), custom_call_target="tpu_custom_call" | custom-call | flops 1024 | bytes 1024 | tf_op jit(solution)/shard_map/pallas_call | solution.py:338
  179.8 10.4 %all-to-all-done.1 = bf16[32,96,128]{2,1,0:T(8,128)(2,1)S(1)} async-done(((bf16[32,96,128]{2,1,0:T(8,128)(2,1)}), bf16[32,96,128]{2,1,0:T(8,128)(2,1)S(1)}, u32[]{:S(2)}, u32[]{:S(2)}) %all-to-all-start.1) | async-done | bytes 786464 | tf_op jit(solution)/shard_map/all_to_all | solution.py:291
  190.1 0.9 copy-done.1
  191.0 2.5 %shard_map.100 = (bf16[128,128]{1,0:T(8,128)(2,1)}, bf16[128,128]{1,0:T(8,128)(2,1)}) custom-call(s32[2,128]{1,0:T(2,128)} %bitcast.43, f32[2,128]{1,0:T(2,128)} %bitcast.45, bf16[8,4,96,128]{3,2,1,0:T(8,128)(2,1)} %bitcast.32), custom_call_target="tpu_custom_call" | custom-call | flops 1024 | bytes 1024 | tf_op jit(solution)/shard_map/pallas_call | solution.py:353
  (20 shorter events, 0.0 us)
Async XLA Ops:
  10.4 44.0 %all-to-all-start = ((bf16[32,96,128]{2,1,0:T(8,128)(2,1)}), bf16[32,96,128]{2,1,0:T(8,128)(2,1)S(1)}, u32[]{:S(2)}, u32[]{:S(2)}) async-start(bf16[32,96,128]{2,1,0:T(8,128)(2,1)} %bitcast.31), calls=%async_computation | async-start | bytes 1572864 | tf_op jit(solution)/shard_map/all_to_all | solution.py:291
  21.6 79.1 %all-gather.2.cloned.1.call-start = ((), (), s32[]{:S(2)}) async-start(), calls=%async_computation.3 | async-start | bytes 7077888 | tf_op jit(solution)/shard_map/all_gather | solution.py:314
  25.5 28.9 %collective-permute-start = (bf16[1536,128]{1,0:T(8,128)(2,1)}, bf16[1536,128]{1,0:T(8,128)(2,1)S(1)}, u32[]{:S(2)}, u32[]{:S(2)}) collective-permute-start(bf16[1536,128]{1,0:T(8,128)(2,1)} %get-tuple-element.44), channel_id=1, source_target_pairs={{0,8},{4,12},{8,16},{12,20},{16,24},{20,28},{24,0},{28,4},{1,9},{5... | collective-permute-start | bytes 1179656 | tf_op jit(solution)/shard_map/ppermute | solution.py:283
  27.0 27.4 %collective-permute-start.1 = (bf16[1536,128]{1,0:T(8,128)(2,1)}, bf16[1536,128]{1,0:T(8,128)(2,1)S(1)}, u32[]{:S(2)}, u32[]{:S(2)}) collective-permute-start(bf16[1536,128]{1,0:T(8,128)(2,1)} %get-tuple-element.45), channel_id=1, source_target_pairs={{0,16},{4,20},{8,24},{12,28},{16,0},{20,4},{24,8},{28,12},{1,17},{... | collective-permute-start | bytes 1179656 | tf_op jit(solution)/shard_map/ppermute | solution.py:283
  29.7 24.7 %collective-permute-start.2 = (bf16[1536,128]{1,0:T(8,128)(2,1)}, bf16[1536,128]{1,0:T(8,128)(2,1)S(1)}, u32[]{:S(2)}, u32[]{:S(2)}) collective-permute-start(bf16[1536,128]{1,0:T(8,128)(2,1)} %get-tuple-element.46), channel_id=1, source_target_pairs={{0,24},{4,28},{8,0},{12,4},{16,8},{20,12},{24,16},{28,20},{1,25},{... | collective-permute-start | bytes 1179656 | tf_op jit(solution)/shard_map/ppermute | solution.py:283
  31.1 23.3 %collective-permute-start.3 = (bf16[512,256]{1,0:T(8,128)(2,1)S(1)}, bf16[512,256]{1,0:T(8,128)(2,1)S(1)}, u32[]{:S(2)}, u32[]{:S(2)}) collective-permute-start(bf16[512,256]{1,0:T(8,128)(2,1)S(1)} %get-tuple-element.47), channel_id=1, source_target_pairs={{0,4},{4,0},{8,12},{12,8},{16,20},{20,16},{24,28},{28,24},{1,5},{5... | collective-permute-start | bytes 786440 | tf_op jit(solution)/shard_map/ppermute | solution.py:288
  54.4 2.8 %copy-start.16 = (bf16[512,256]{1,0:T(8,128)(2,1)}, bf16[512,256]{1,0:T(8,128)(2,1)S(1)}, u32[]{:S(2)}) copy-start(bf16[512,256]{1,0:T(8,128)(2,1)S(1)} %collective-permute-done.3.dense_ref) | copy-start | bytes 786436
  54.4 46.3 %copy-start.2 = (bf16[1536,128]{1,0:T(8,128)(2,1)}, bf16[1536,128]{1,0:T(8,128)(2,1)S(1)}, u32[]{:S(2)}) copy-start(bf16[1536,128]{1,0:T(8,128)(2,1)S(1)} %collective-permute-done) | copy-start | bytes 1179652
  54.4 46.3 %copy-start.3 = (bf16[1536,128]{1,0:T(8,128)(2,1)}, bf16[1536,128]{1,0:T(8,128)(2,1)S(1)}, u32[]{:S(2)}) copy-start(bf16[1536,128]{1,0:T(8,128)(2,1)S(1)} %collective-permute-done.1) | copy-start | bytes 1179652
  54.4 46.3 %copy-start.4 = (bf16[1536,128]{1,0:T(8,128)(2,1)}, bf16[1536,128]{1,0:T(8,128)(2,1)S(1)}, u32[]{:S(2)}) copy-start(bf16[1536,128]{1,0:T(8,128)(2,1)S(1)} %collective-permute-done.2) | copy-start | bytes 1179652
  54.4 0.9 copy-start
  55.4 102.1 %reduce-scatter.2.cloned.1.call-start = ((), (), s32[]{:S(2)}) async-start(), calls=%async_computation.4 | async-start | bytes 7077888 | tf_op jit(solution)/shard_map/reduce_scatter | solution.py:335
  55.5 21.5 %collective-permute-start.7 = (bf16[512,256]{1,0:T(8,128)(2,1)S(1)}, bf16[512,256]{1,0:T(8,128)(2,1)S(1)}, u32[]{:S(2)}, u32[]{:S(2)}) collective-permute-start(bf16[512,256]{1,0:T(8,128)(2,1)S(1)} %get-tuple-element.59), channel_id=1, source_target_pairs={{0,4},{4,0},{8,12},{12,8},{16,20},{20,16},{24,28},{28,24},{1,5},{5... | collective-permute-start | bytes 786440 | tf_op jit(solution)/shard_map/ppermute | solution.py:288
  59.5 17.4 %collective-permute-start.4 = (bf16[512,128]{1,0:T(8,128)(2,1)}, bf16[512,128]{1,0:T(8,128)(2,1)S(1)}, u32[]{:S(2)}, u32[]{:S(2)}) collective-permute-start(bf16[512,128]{1,0:T(8,128)(2,1)} %get-tuple-element.56), channel_id=1, source_target_pairs={{0,8},{4,12},{8,16},{12,20},{16,24},{20,28},{24,0},{28,4},{1,9},{5... | collective-permute-start | bytes 393224 | tf_op jit(solution)/shard_map/ppermute | solution.py:283
  60.8 16.1 %collective-permute-start.5 = (bf16[512,128]{1,0:T(8,128)(2,1)}, bf16[512,128]{1,0:T(8,128)(2,1)S(1)}, u32[]{:S(2)}, u32[]{:S(2)}) collective-permute-start(bf16[512,128]{1,0:T(8,128)(2,1)} %get-tuple-element.57), channel_id=1, source_target_pairs={{0,16},{4,20},{8,24},{12,28},{16,0},{20,4},{24,8},{28,12},{1,17},{... | collective-permute-start | bytes 393224 | tf_op jit(solution)/shard_map/ppermute | solution.py:283
  63.5 13.4 %collective-permute-start.6 = (bf16[512,128]{1,0:T(8,128)(2,1)}, bf16[512,128]{1,0:T(8,128)(2,1)S(1)}, u32[]{:S(2)}, u32[]{:S(2)}) collective-permute-start(bf16[512,128]{1,0:T(8,128)(2,1)} %get-tuple-element.58), channel_id=1, source_target_pairs={{0,24},{4,28},{8,0},{12,4},{16,8},{20,12},{24,16},{28,20},{1,25},{... | collective-permute-start | bytes 393224 | tf_op jit(solution)/shard_map/ppermute | solution.py:283
  65.0 24.0 %collective-permute-start.9 = (bf16[512,256]{1,0:T(8,128)(2,1)S(1)}, bf16[512,256]{1,0:T(8,128)(2,1)S(1)}, u32[]{:S(2)}, u32[]{:S(2)}) collective-permute-start(bf16[512,256]{1,0:T(8,128)(2,1)S(1)} %get-tuple-element.67), channel_id=1, source_target_pairs={{0,4},{4,0},{8,12},{12,8},{16,20},{20,16},{24,28},{28,24},{1,5},{5... | collective-permute-start | bytes 786440 | tf_op jit(solution)/shard_map/ppermute | solution.py:288
  76.9 0.7 copy-start.15
  77.0 23.8 %copy-start.5 = (bf16[512,128]{1,0:T(8,128)(2,1)}, bf16[512,128]{1,0:T(8,128)(2,1)S(1)}, u32[]{:S(2)}) copy-start(bf16[512,128]{1,0:T(8,128)(2,1)S(1)} %collective-permute-done.4.refs_5_) | copy-start | bytes 393220
  77.0 23.8 %copy-start.6 = (bf16[512,128]{1,0:T(8,128)(2,1)}, bf16[512,128]{1,0:T(8,128)(2,1)S(1)}, u32[]{:S(2)}) copy-start(bf16[512,128]{1,0:T(8,128)(2,1)S(1)} %collective-permute-done.5.refs_6_) | copy-start | bytes 393220
  77.0 23.8 %copy-start.7 = (bf16[512,128]{1,0:T(8,128)(2,1)}, bf16[512,128]{1,0:T(8,128)(2,1)S(1)}, u32[]{:S(2)}) copy-start(bf16[512,128]{1,0:T(8,128)(2,1)S(1)} %collective-permute-done.6.refs_7_) | copy-start | bytes 393220
  80.0 9.0 %collective-permute-start.8 = (bf16[512,128]{1,0:T(8,128)(2,1)}, bf16[512,128]{1,0:T(8,128)(2,1)S(1)}, u32[]{:S(2)}, u32[]{:S(2)}) collective-permute-start(bf16[512,128]{1,0:T(8,128)(2,1)} %get-tuple-element.66), channel_id=1, source_target_pairs={{0,8},{4,12},{8,16},{12,20},{16,24},{20,28},{24,0},{28,4},{1,9},{5... | collective-permute-start | bytes 393224 | tf_op jit(solution)/shard_map/ppermute | solution.py:283
  80.0 15.3 %collective-permute-start.10 = (bf16[512,128]{1,0:T(8,128)(2,1)}, bf16[512,128]{1,0:T(8,128)(2,1)S(1)}, u32[]{:S(2)}, u32[]{:S(2)}) collective-permute-start(bf16[512,128]{1,0:T(8,128)(2,1)} %get-tuple-element.69), channel_id=1, source_target_pairs={{0,16},{4,20},{8,24},{12,28},{16,0},{20,4},{24,8},{28,12},{1,17},{... | collective-permute-start | bytes 393224 | tf_op jit(solution)/shard_map/ppermute | solution.py:283
  85.9 9.3 %collective-permute-start.11 = (bf16[512,128]{1,0:T(8,128)(2,1)}, bf16[512,128]{1,0:T(8,128)(2,1)S(1)}, u32[]{:S(2)}, u32[]{:S(2)}) collective-permute-start(bf16[512,128]{1,0:T(8,128)(2,1)} %get-tuple-element.70), channel_id=1, source_target_pairs={{0,24},{4,28},{8,0},{12,4},{16,8},{20,12},{24,16},{28,20},{1,25},{... | collective-permute-start | bytes 393224 | tf_op jit(solution)/shard_map/ppermute | solution.py:283
  88.9 11.8 %copy-start.8 = (bf16[512,128]{1,0:T(8,128)(2,1)}, bf16[512,128]{1,0:T(8,128)(2,1)S(1)}, u32[]{:S(2)}) copy-start(bf16[512,128]{1,0:T(8,128)(2,1)S(1)} %collective-permute-done.8.refs_9_) | copy-start | bytes 393220
  89.0 0.7 copy-start.14
  92.0 7.8 %collective-permute-start.12 = (bf16[512,128]{1,0:T(8,128)(2,1)}, bf16[512,128]{1,0:T(8,128)(2,1)S(1)}, u32[]{:S(2)}, u32[]{:S(2)}) collective-permute-start(bf16[512,128]{1,0:T(8,128)(2,1)} %get-tuple-element.73), channel_id=1, source_target_pairs={{0,8},{4,12},{8,16},{12,20},{16,24},{20,28},{24,0},{28,4},{1,9},{5... | collective-permute-start | bytes 393224 | tf_op jit(solution)/shard_map/ppermute | solution.py:283
  92.0 7.8 %collective-permute-start.13 = (bf16[512,128]{1,0:T(8,128)(2,1)}, bf16[512,128]{1,0:T(8,128)(2,1)S(1)}, u32[]{:S(2)}, u32[]{:S(2)}) collective-permute-start(bf16[512,128]{1,0:T(8,128)(2,1)} %get-tuple-element.74), channel_id=1, source_target_pairs={{0,16},{4,20},{8,24},{12,28},{16,0},{20,4},{24,8},{28,12},{1,17},{... | collective-permute-start | bytes 393224 | tf_op jit(solution)/shard_map/ppermute | solution.py:283
  94.9 5.8 %collective-permute-start.14 = (bf16[512,128]{1,0:T(8,128)(2,1)}, bf16[512,128]{1,0:T(8,128)(2,1)S(1)}, u32[]{:S(2)}, u32[]{:S(2)}) collective-permute-start(bf16[512,128]{1,0:T(8,128)(2,1)} %get-tuple-element.75), channel_id=1, source_target_pairs={{0,24},{4,28},{8,0},{12,4},{16,8},{20,12},{24,16},{28,20},{1,25},{... | collective-permute-start | bytes 393224 | tf_op jit(solution)/shard_map/ppermute | solution.py:283
  95.2 5.5 %copy-start.9 = (bf16[512,128]{1,0:T(8,128)(2,1)}, bf16[512,128]{1,0:T(8,128)(2,1)S(1)}, u32[]{:S(2)}) copy-start(bf16[512,128]{1,0:T(8,128)(2,1)S(1)} %collective-permute-done.10.refs_10_) | copy-start | bytes 393220
  95.2 5.5 %copy-start.10 = (bf16[512,128]{1,0:T(8,128)(2,1)}, bf16[512,128]{1,0:T(8,128)(2,1)S(1)}, u32[]{:S(2)}) copy-start(bf16[512,128]{1,0:T(8,128)(2,1)S(1)} %collective-permute-done.11.refs_11_) | copy-start | bytes 393220
  99.8 1.0 copy-start.11
  99.8 1.0 copy-start.12
  100.7 0.6 copy-start.13
  157.5 32.7 %all-to-all-start.1 = ((bf16[32,96,128]{2,1,0:T(8,128)(2,1)}), bf16[32,96,128]{2,1,0:T(8,128)(2,1)S(1)}, u32[]{:S(2)}, u32[]{:S(2)}) async-start(bf16[32,96,128]{2,1,0:T(8,128)(2,1)} %bitcast.41), calls=%async_computation.2 | async-start | bytes 1572864 | tf_op jit(solution)/shard_map/all_to_all | solution.py:291
  190.1 0.9 copy-start.1
Sparse Core Ops, SparseCore 0:
  55.5 41.6 all-gather.1
  115.4 42.0 reduce-scatter.1
